TPU v7x, 128 devices: a whole 4x4x4 slice. The times are simulated.
128 devices in a mesh: row: 8 (over x, z_lo), col: 16 (over y, z_hi, core).
Axes of the slice: x: 4, y: 4, z: 4 (z_hi: 2, z_lo: 2; z = z_hi * 2 + z_lo), core: 2. Of those that a mesh axis runs over, the one named last changes fastest.
Arguments:
- features: bfloat16 [64, 256, 8, 64], P('row', 'col'), may hold values from -6 to 6
- block_active: int32 [8, 32, 1], P('row', 'col'), may hold values 0 or 1
- encode_fine: bfloat16 [3, 3, 3, 64, 64], replicated, may hold values from -0.15625 to 0.15625
- encode_coarse: bfloat16 [3, 3, 3, 64, 128], replicated, may hold values from -0.15625 to 0.15625
- decode_coarse: bfloat16 [3, 3, 3, 128, 128], replicated, may hold values from -0.109375 to 0.109375
- decode_fine: bfloat16 [3, 3, 3, 192, 64], replicated, may hold values from -0.078125 to 0.078125
- out_cotangent: bfloat16 [64, 256, 8, 64], P('row', 'col'), may hold values from -6 to 6
Outputs:
- decoded: bfloat16 [64, 256, 8, 64], P('row', 'col')
- grad_encode_fine: float32 [3, 3, 3, 64, 64], replicated
- grad_encode_coarse: float32 [3, 3, 3, 64, 128], replicated
- grad_decode_coarse: float32 [3, 3, 3, 128, 128], replicated
- grad_decode_fine: float32 [3, 3, 3, 192, 64], replicated
All inputs are finite; a program needn't handle non-finite values. No bound on the sum of `block_active` on one device may be relied on, other than what follows from the above.
Results may differ from a plain program's by a relative error of at most 0.013.
Values may be sent and summed in bfloat16 or wider, within the bound.
No kernel may reach another device: no remote copies, remote signals or barrier semaphores. Data moves between devices by JAX's collectives and lax.ppermute only.
A program may use at most 128 MiB of HBM per device.

v0:
```python
import functools
import math

import jax
import jax.numpy as jnp
from jax import lax
from jax.experimental import pallas as pl
from jax.experimental.pallas import tpu as pltpu
from jax.sharding import Mesh, PartitionSpec as P

F32 = jnp.float32
BF16 = jnp.bfloat16
VMEM_LIMIT = 50 * 1024 * 1024
VM = pl.BlockSpec(memory_space=pltpu.VMEM)
SM = pl.BlockSpec(memory_space=pltpu.SMEM)
FACTOR = 1.0 / math.sqrt(64 * 256 * 8)
CHUNK = 72


def call(kernel, outs, scratch=(), flops=0, n_scalar=1, n_in=0):
    return pl.pallas_call(
        kernel,
        out_shape=[jax.ShapeDtypeStruct(s, d) for s, d in outs],
        in_specs=[SM] * n_scalar + [VM] * (n_in - n_scalar),
        out_specs=[VM] * len(outs),
        scratch_shapes=list(scratch),
        compiler_params=pltpu.CompilerParams(vmem_limit_bytes=VMEM_LIMIT),
        cost_estimate=pl.CostEstimate(flops=flops, bytes_accessed=4_000_000, transcendentals=0),
    )


def dot(lhs, rhs):
    return jnp.dot(lhs, rhs, preferred_element_type=F32)


def dot_t(lhs, rhs):
    return lax.dot_general(lhs, rhs, (((0,), (0,)), ((), ())), preferred_element_type=F32)


def bround(v):
    return v.astype(BF16).astype(F32)


def z_of(shape):
    return lax.broadcasted_iota(jnp.int32, shape, len(shape) - 2)


def z_later(v):
    return jnp.where(z_of(v.shape) > 0, pltpu.roll(v, 1, 1), 0.0)


def z_earlier(v):
    return jnp.where(z_of(v.shape) < 7, pltpu.roll(v, 7, 1), 0.0)


def fold64(acc):
    rows = acc.shape[0]
    cube = acc.reshape(rows // 8, 8, 192)
    ends, middle = cube[..., :128], cube[..., 128:]
    lane = lax.broadcasted_iota(jnp.int32, ends.shape, 2)
    z = z_of(ends.shape)
    low = lane < 64
    moved = jnp.where(low, pltpu.roll(ends, 1, 1), pltpu.roll(ends, 7, 1))
    moved = jnp.where(z == jnp.where(low, 0, 7), 0.0, moved)
    return moved[..., :64] + moved[..., 64:] + middle


def fold128(acc):
    rows = acc.shape[0]
    cube = acc.reshape(rows // 8, 8, 384)
    return z_later(cube[..., :128]) + cube[..., 128:256] + z_earlier(cube[..., 256:])


def taps_y(v, count):
    depth = v.shape[2]
    wide = jnp.concatenate([v[b : b + count] for b in range(3)], axis=2)
    return wide.reshape(count * 8, 3 * depth).astype(BF16)


def taps_z(g):
    wide = jnp.concatenate([z_earlier(g), g, z_later(g)], axis=2)
    return wide.reshape(g.shape[0] * 8, 3 * g.shape[2]).astype(BF16)


def halve_z(s):
    pair = s + pltpu.roll(s, 7, 1)
    z = z_of(s.shape)
    out = jnp.where(z == 0, pair, 0.0)
    for zc in (1, 2, 3):
        out = jnp.where(z == zc, pltpu.roll(pair, 8 - zc, 1), out)
    return out


def double_z(u):
    z = z_of(u.shape)
    out = u
    for shift in (1, 2, 3, 4):
        out = jnp.where((z + 1) // 2 == shift, pltpu.roll(u, shift, 1), out)
    return out


def silu_parts(v):
    sigma = jax.nn.sigmoid(v)
    act = v * sigma
    return act, sigma + act * (1.0 - sigma)


def mask_rows(sc):
    row = lax.broadcasted_iota(jnp.int32, (128, 64), 0)
    return jnp.where(row < 64, sc[6], sc[7]).astype(F32)


def pack_x(sc, feat, cot, p1, p2):
    mask = mask_rows(sc)
    for p, odd in ((p1, sc[0]), (p2, 1 - sc[0])):
        first = 1 - odd
        for k in range(7):
            p[k] = (feat[first + k].astype(F32) * mask).astype(BF16)
        p[7] = cot[7 * first]
        p[8] = mask.astype(BF16)


def pack_y(sc, feat, cot, rz, rxz, xall, p3, p4):
    mask = mask_rows(sc)
    odd = sc[0] == 1
    v_lo, v_hi = sc[1].astype(F32), sc[2].astype(F32)

    def lo(k):
        return jnp.where(odd, rz[k].astype(F32), rxz[k].astype(F32)) * v_lo

    def hi(k):
        return jnp.where(odd, rxz[k].astype(F32), rz[k].astype(F32)) * v_hi

    for k in range(7):
        xall[k] = lo(k).astype(BF16)
        xall[15 + k] = hi(k).astype(BF16)
    for k in range(8):
        xall[7 + k] = (feat[k].astype(F32) * mask).astype(BF16)
        xall[23 + k] = cot[k]
    xall[22] = lo(7).astype(BF16)
    xall[31] = hi(7).astype(BF16)
    xall[32] = lo(8).astype(BF16)
    xall[33] = mask.astype(BF16)
    xall[34] = hi(8).astype(BF16)
    odd_c = sc[3] == 1
    for p, low in ((p3, odd_c), (p4, jnp.logical_not(odd_c))):
        for k in range(22):
            p[k] = jnp.where(low, xall[k, 0:64].astype(F32), xall[k, 64:128].astype(F32)).astype(BF16)
        cols = []
        for k in range(22, 35):
            slab = xall[k].astype(F32)
            cols.append(jnp.where(low, slab[0:8], slab[120:128]))
        cols += [jnp.zeros((24, 64), F32)]
        extra = jnp.concatenate(cols, axis=0).astype(BF16)
        p[22] = extra[0:64]
        p[23] = extra[64:128]


def forward(
    sc, xall, r3, r4, w1, w2, w3, w4l, w4e, w5,
    decoded, slope_ef, g_skip, slope_ec, g_dc, s_in, s_pool, s_ec, s_lift, s_skip, gz,
    ff, mm, cc, s1, ee, po, s2, ec, s3, slope_dc, gd, s4,
):
    odd = sc[3] == 1
    v_lo, v_hi = sc[4].astype(F32), sc[5].astype(F32)

    def lo(k):
        return jnp.where(odd, r3[k].astype(F32), r4[k].astype(F32)) * v_lo

    def hi(k):
        return jnp.where(odd, r4[k].astype(F32), r3[k].astype(F32)) * v_hi

    def gather(x, _):
        ff[x, 0:8] = lo(x).reshape(8, 8, 64)
        ff[x, 8:24] = xall[x].astype(F32).reshape(16, 8, 64)
        ff[x, 24:32] = hi(x).reshape(8, 8, 64)
        return 0

    lax.fori_loop(0, 22, gather, 0)
    extra_lo = jnp.concatenate([lo(22), lo(23)], axis=0).reshape(16, 8, 64)
    extra_hi = jnp.concatenate([hi(22), hi(23)], axis=0).reshape(16, 8, 64)
    for k in range(10):
        cc[k, 0] = extra_lo[k]
        cc[k, 1:17] = xall[22 + k].astype(F32).reshape(16, 8, 64)
        cc[k, 17] = extra_hi[k]
    for k in range(3):
        mm[k, 0:8] = jnp.broadcast_to(extra_lo[10 + k][None], (8, 8, 64))
        mm[k, 8:24] = xall[32 + k].astype(F32).reshape(16, 8, 64)
        mm[k, 24:32] = jnp.broadcast_to(extra_hi[10 + k][None], (8, 8, 64))

    def spread(x, _):
        v = ff[x]
        zero = jnp.zeros((1, 8, 64), F32)
        s1[x] = taps_y(jnp.concatenate([zero, v, zero], axis=0), 32)
        return 0

    lax.fori_loop(0, 22, spread, 0)

    def encode(x, _):
        acc = dot(s1[x], w1[0]) + dot(s1[x + 1], w1[1]) + dot(s1[x + 2], w1[2])
        pre = fold64(acc)
        mask = mm[jnp.where(x < 6, 0, jnp.where(x < 14, 1, 2))]
        act, slope = silu_parts(pre)
        ee[x] = bround(act * mask)

        @pl.when(jnp.logical_and(x >= 6, x < 14))
        def _():
            slope_ef[x - 6] = (slope * mask)[8:24].reshape(128, 64)

        return 0

    lax.fori_loop(0, 20, encode, 0)
    for x in range(10):
        s_in[x] = taps_y(ff[6 + x, 7:25], 16)

    def pool(x, _):
        s = (ee[2 * x] + ee[2 * x + 1]).reshape(16, 2, 8, 64)
        v = bround(halve_z(s[:, 0] + s[:, 1]) * 0.125)
        po[x] = v
        zero = jnp.zeros((1, 8, 64), F32)
        s2[x] = taps_y(jnp.concatenate([zero, v, zero], axis=0), 16)
        return 0

    lax.fori_loop(0, 10, pool, 0)
    for x in range(6):
        s_pool[x] = taps_y(po[2 + x, 3:13], 8)

    def mask_coarse(block):
        m = mm[block].reshape(16, 2, 8, 64)[:, 0]
        m = jnp.concatenate([m, m], axis=2)
        return jnp.where(z_of(m.shape) < 4, m, 0.0)

    def encode2(x, _):
        acc = dot(s2[x], w2[0]) + dot(s2[x + 1], w2[1]) + dot(s2[x + 2], w2[2])
        mask = mask_coarse(jnp.where(x < 2, 0, jnp.where(x < 6, 1, 2)))
        act, slope = silu_parts(fold128(acc))
        v = bround(act * mask)
        ec[x] = v
        zero = jnp.zeros((1, 8, 128), F32)
        s3[x] = taps_y(jnp.concatenate([zero, v, zero], axis=0), 16)

        @pl.when(jnp.logical_and(x >= 1, x < 7))
        def _():
            slope_ec[x - 1] = (slope * mask)[3:13].reshape(80, 128)

        return 0

    lax.fori_loop(0, 8, encode2, 0)
    for x in range(6):
        s_ec[x] = taps_y(ec[1 + x, 3:13], 8)

    def decode2(x, _):
        acc = dot(s3[x], w3[0]) + dot(s3[x + 1], w3[1]) + dot(s3[x + 2], w3[2])
        mask = mask_coarse(jnp.where(x < 1, 0, jnp.where(x < 5, 1, 2)))
        act, slope = silu_parts(fold128(acc))
        v = double_z(bround(act * mask)[3:13])
        up = jnp.concatenate([v[:, None], v[:, None]], axis=1).reshape(20, 8, 128)
        wide = taps_y(up, 18)
        s_lift[2 * x] = wide
        s_lift[2 * x + 1] = wide

        @pl.when(jnp.logical_and(x >= 1, x < 5))
        def _():
            slope_dc[x - 1] = (slope * mask)[4:12]

        return 0

    lax.fori_loop(0, 6, decode2, 0)

    def skip(x, _):
        s_skip[x] = taps_y(ee[x + 4, 6:26], 18)
        return 0

    lax.fori_loop(0, 12, skip, 0)

    def decode(i, _):
        acc = jnp.zeros((288, 192), F32)
        for a in range(3):
            acc += dot(s_lift[pl.ds(2 * i + a, 2)].reshape(288, 384), w4l[a])
            acc += dot(s_skip[pl.ds(2 * i + a, 2)].reshape(288, 192), w4e[a])
        pre = fold64(acc).reshape(2, 18, 8, 64)
        for k in range(2):
            x = 2 * i + k
            mask = mm[jnp.where(x < 1, 0, jnp.where(x < 9, 1, 2)), 7:25]
            act, slope = silu_parts(pre[k])
            g = bround(cc[x] * mask * slope)
            gd[x] = g
            s4[x] = taps_y(g, 16)

            @pl.when(jnp.logical_and(x >= 1, x < 9))
            def _():
                decoded[x - 1] = (act * mask)[1:17].reshape(128, 64).astype(BF16)
                zero = jnp.zeros((1, 8, 64), F32)
                gz[x - 1] = taps_z(jnp.concatenate([zero, g[1:17], zero], axis=0))

        return 0

    lax.fori_loop(0, 5, decode, 0)

    def back(i, _):
        acc = jnp.zeros((256, 576), F32)
        for a in range(3):
            acc += dot(s4[pl.ds(2 * i + a, 2)].reshape(256, 192), w5[a])
        g_skip[pl.ds(2 * i, 2)] = fold64(acc[:, 384:]).reshape(2, 128, 64)
        up = acc[:, :384].reshape(2, 8, 2, 8, 384)
        up = up[0] + up[1]
        up = fold128((up[:, 0] + up[:, 1]).reshape(64, 384))
        g = halve_z(up) * slope_dc[i]
        g_dc[i] = g.reshape(64, 128).astype(BF16)
        return 0

    lax.fori_loop(0, 4, back, 0)


def wire64(res, rows):
    out = res.reshape(3, rows, 192)
    tail = out[..., 128:]
    return out[..., :128].astype(BF16), jnp.concatenate([tail[:, : rows // 2], tail[:, rows // 2 :]], axis=2).astype(BF16)


def weights_decode(sc, s_lift, s_skip, gz, s_ec, g_dc, wd1, wd2, wc):
    grad = gz[...].reshape(1152, 192)
    gc = taps_z(g_dc[...].astype(F32).reshape(32, 8, 128))
    for a in range(3):
        up = (dot_t(s_lift[a + 1 : a + 9].reshape(1152, 384), grad) * FACTOR).reshape(3, 128, 192)
        same = (dot_t(s_skip[a + 1 : a + 9].reshape(1152, 192), grad) * FACTOR).reshape(3, 64, 192)
        both = jnp.concatenate([up, same], axis=1).reshape(576, 192)
        wd1[3 * a : 3 * a + 3], wd2[3 * a : 3 * a + 3] = wire64(both, 192)
        res = dot_t(s_ec[a : a + 4].reshape(256, 384), gc) * FACTOR
        for b in range(3):
            for c in range(3):
                wc[9 * a + 3 * b + c] = res[128 * b : 128 * b + 128, 128 * c : 128 * c + 128].astype(BF16)


def back_encode(sc, gx, slope_ec, s_pool, s_in, g_skip, slope_ef, w6, w7, we1, we2, wec, s5, ge, gz):
    def spread(x, _):
        s5[x] = taps_y(gx[x].astype(F32).reshape(12, 8, 128), 10)
        return 0

    lax.fori_loop(0, 8, spread, 0)
    acc = jnp.zeros((480, 384), F32)
    for a in range(3):
        acc += dot(s5[a : a + 6].reshape(480, 384), w6[a])
    g_ec = bround(fold128(acc) * slope_ec[...].reshape(60, 8, 128)).reshape(6, 10, 8, 128)
    for x in range(6):
        ge[x] = taps_y(g_ec[x], 8)
    gc = taps_z(g_ec[1:5, 1:9].reshape(32, 8, 128))
    acc = jnp.zeros((256, 192), F32)
    for a in range(3):
        acc += dot(ge[a : a + 4].reshape(256, 384), w7[a])
    up = double_z(fold64(acc) * 0.125)
    up = jnp.concatenate([up[:, None], up[:, None]], axis=1).reshape(4, 16, 8, 64)
    for x in range(8):
        g = (g_skip[x].reshape(16, 8, 64) + up[x // 2]) * slope_ef[x].reshape(16, 8, 64)
        gz[x] = taps_z(bround(g))
    gf = gz[...].reshape(1024, 192)
    for a in range(3):
        res = dot_t(s_in[a : a + 8].reshape(1024, 192), gf) * FACTOR
        we1[3 * a : 3 * a + 3], we2[3 * a : 3 * a + 3] = wire64(res, 64)
        res = dot_t(s_pool[a : a + 4].reshape(256, 192), gc) * FACTOR
        for b in range(3):
            for c in range(3):
                wec[9 * a + 3 * b + c] = res[64 * b : 64 * b + 64, 128 * c : 128 * c + 128].astype(BF16)


def unpack(sc, wd1, wd2, wc, we1, we2, wec, d_df, d_dc, d_ef, d_ec):
    for first, second, out, rows in ((wd1, wd2, d_df, 192), (we1, we2, d_ef, 64)):
        for k in range(9):
            both = first[k].astype(F32)
            tail = second[k].astype(F32)
            out[3 * k] = both[:, :64]
            out[3 * k + 1] = both[:, 64:]
            out[3 * k + 2] = jnp.concatenate([tail[:, :64], tail[:, 64:]], axis=0)
    d_dc[...] = wc[...].astype(F32)
    d_ec[...] = wec[...].astype(F32)


def side(v, order):
    return jnp.concatenate([v[..., c, :] for c in order], axis=-1)


def forward_weight(kernel, order):
    t = jnp.transpose(kernel, (0, 1, 3, 2, 4))
    return side(t, order)


def backward_weight(kernel, order):
    t = jnp.transpose(kernel[::-1, ::-1, ::-1], (0, 1, 4, 2, 3))
    return side(t, order)


def swap(v, pairs):
    return lax.ppermute(v, ("row", "colh", "core"), pairs)


def body(
    features, block_active, encode_fine, encode_coarse, decode_coarse, decode_fine, out_cotangent
):
    row = lax.axis_index("row")
    core = lax.axis_index("core")
    col = 2 * lax.axis_index("colh") + core
    at = [(r, c) for r in range(8) for c in range(16)]

    def up(i, n):
        return (i + 1) % n if i % 2 else (i - 1) % n

    swap_z = [(16 * r + c, 16 * (r ^ 1) + c) for r, c in at]
    swap_xz = [(16 * r + c, 16 * up(r, 8) + c) for r, c in at]
    swap_core = [(16 * r + c, 16 * r + (c ^ 1)) for r, c in at]
    swap_yz = [(16 * r + c, 16 * r + up(c, 16)) for r, c in at]

    odd_r, odd_c = row % 2, core
    sc = jnp.stack(
        [odd_r, row > 0, row < 7, odd_c, col > 0, col < 15, block_active[0, 0, 0], block_active[0, 1, 0]]
    ).astype(jnp.int32)

    order = (0, 2, 1)
    natural = (0, 1, 2)
    w1 = forward_weight(encode_fine, order).reshape(3, 192, 192)
    w2 = forward_weight(encode_coarse, natural).reshape(3, 192, 384)
    w3 = forward_weight(decode_coarse, natural).reshape(3, 384, 384)
    w4l = forward_weight(decode_fine[..., :128, :], order).reshape(3, 384, 192)
    w4e = forward_weight(decode_fine[..., 128:, :], order).reshape(3, 192, 192)
    w5 = jnp.concatenate(
        [backward_weight(decode_fine[..., :128, :], natural), backward_weight(decode_fine[..., 128:, :], order)],
        axis=-1,
    ).reshape(3, 192, 576)
    w6 = backward_weight(decode_coarse, natural).reshape(3, 384, 384)
    w7 = backward_weight(encode_coarse, order).reshape(3, 384, 192)

    feat = features.reshape(8, 128, 64)
    cot = out_cotangent.reshape(8, 128, 64)
    p1, p2 = call(pack_x, [((9, 128, 64), BF16)] * 2, n_in=3)(sc, feat, cot)
    rz, rxz = swap(p1, swap_z), swap(p2, swap_xz)
    xall, p3, p4 = call(
        pack_y, [((35, 128, 64), BF16), ((24, 64, 64), BF16), ((24, 64, 64), BF16)], n_in=5
    )(sc, feat, cot, rz, rxz)
    r3, r4 = swap(p3, swap_core), swap(p4, swap_yz)

    decoded, slope_ef, g_skip, slope_ec, g_dc, s_in, s_pool, s_ec, s_lift, s_skip, gz = call(
        forward,
        [
            ((8, 128, 64), BF16),
            ((8, 128, 64), F32),
            ((8, 128, 64), F32),
            ((6, 80, 128), F32),
            ((4, 64, 128), BF16),
            ((10, 128, 192), BF16),
            ((6, 64, 192), BF16),
            ((6, 64, 384), BF16),
            ((12, 144, 384), BF16),
            ((12, 144, 192), BF16),
            ((8, 144, 192), BF16),
        ],
        scratch=[
            pltpu.VMEM((22, 32, 8, 64), F32),
            pltpu.VMEM((3, 32, 8, 64), F32),
            pltpu.VMEM((10, 18, 8, 64), F32),
            pltpu.VMEM((22, 256, 192), BF16),
            pltpu.VMEM((20, 32, 8, 64), F32),
            pltpu.VMEM((10, 16, 8, 64), F32),
            pltpu.VMEM((10, 128, 192), BF16),
            pltpu.VMEM((8, 16, 8, 128), F32),
            pltpu.VMEM((8, 128, 384), BF16),
            pltpu.VMEM((4, 8, 8, 128), F32),
            pltpu.VMEM((10, 18, 8, 64), F32),
            pltpu.VMEM((10, 128, 192), BF16),
        ],
        n_in=10,
        flops=4_000_000_000,
    )(sc, xall, r3, r4, w1, w2, w3, w4l, w4e, w5)

    is_odd = odd_r == 1
    q1 = swap(jnp.where(is_odd, g_dc[:2], g_dc[2:]), swap_z)
    q2 = swap(jnp.where(is_odd, g_dc[2:], g_dc[:2]), swap_xz)
    zero = jnp.zeros_like(q1)
    before = jnp.where(row > 0, jnp.where(is_odd, q1, q2), zero)
    after = jnp.where(row < 7, jnp.where(is_odd, q2, q1), zero)
    gx = jnp.concatenate([before, g_dc, after], axis=0)
    is_odd = odd_c == 1
    q3 = swap(jnp.where(is_odd, gx[:, :16], gx[:, 48:]), swap_core)
    q4 = swap(jnp.where(is_odd, gx[:, 48:], gx[:, :16]), swap_yz)
    zero = jnp.zeros_like(q3)
    before = jnp.where(col > 0, jnp.where(is_odd, q3, q4), zero)
    after = jnp.where(col < 15, jnp.where(is_odd, q4, q3), zero)
    gx = jnp.concatenate([before, gx, after], axis=1)

    wd1, wd2, wc = call(
        weights_decode,
        [((9, 192, 128), BF16), ((9, 96, 128), BF16), ((27, 128, 128), BF16)],
        n_in=6,
        flops=1_000_000_000,
    )(sc, s_lift, s_skip, gz, s_ec, g_dc)

    we1, we2, wec = call(
        back_encode,
        [((9, 64, 128), BF16), ((9, 32, 128), BF16), ((27, 64, 128), BF16)],
        scratch=[
            pltpu.VMEM((8, 80, 384), BF16),
            pltpu.VMEM((6, 64, 384), BF16),
            pltpu.VMEM((8, 128, 192), BF16),
        ],
        n_in=9,
        flops=500_000_000,
    )(sc, gx, slope_ec, s_pool, s_in, g_skip, slope_ef, w6, w7)

    parts = [wd1, wd2, wc, we1, we2, wec]
    flat = jnp.concatenate([p.reshape(-1, 128) for p in parts], axis=0)
    flat = jnp.pad(flat, ((0, 128 * CHUNK - flat.shape[0]), (0, 0))).reshape(2, 64, CHUNK, 128)
    mine = lax.dynamic_index_in_dim(flat, core, 0, keepdims=False)
    other = lax.dynamic_index_in_dim(flat, 1 - core, 0, keepdims=False)
    mine = (mine.astype(F32) + swap(other, swap_core).astype(F32)).astype(BF16)
    terms = lax.all_to_all(mine, ("row", "colh"), 0, 0, tiled=True)
    total = jnp.sum(terms.astype(F32), axis=0).astype(BF16)
    mine = lax.all_to_all(jnp.broadcast_to(total[None], terms.shape), ("row", "colh"), 0, 0, tiled=True)
    other = swap(mine, swap_core)
    first = jnp.where(core == 0, mine, other)
    second = jnp.where(core == 0, other, mine)
    flat = jnp.concatenate([first.reshape(-1, 128), second.reshape(-1, 128)], axis=0)
    pieces, start = [], 0
    for p in parts:
        rows = p.size // 128
        pieces.append(flat[start : start + rows].reshape(p.shape))
        start += rows
    d_df, d_dc, d_ef, d_ec = call(
        unpack,
        [((27, 192, 64), F32), ((27, 128, 128), F32), ((27, 64, 64), F32), ((27, 64, 128), F32)],
        n_in=7,
    )(sc, *pieces)
    return (
        decoded.reshape(8, 16, 8, 64),
        d_ef.reshape(3, 3, 3, 64, 64),
        d_ec.reshape(3, 3, 3, 64, 128),
        d_dc.reshape(3, 3, 3, 128, 128),
        d_df.reshape(3, 3, 3, 192, 64),
    )


def solution(mesh):
    split = Mesh(mesh.devices.reshape(8, 8, 2), ("row", "colh", "core"))
    field = P("row", ("colh", "core"), None, None)
    return jax.shard_map(
        body,
        mesh=split,
        in_specs=(field, P("row", ("colh", "core"), None), P(), P(), P(), P(), field),
        out_specs=(field, P(), P(), P(), P()),
        check_vma=False,
    )
```

profile of v0, /device:TPU:1, one launch (start us, length us, event | category | flops | bytes accessed | tf_op | source)
XLA Modules:
  0.0 165.5 jit_solution(578576705490244440)
XLA Ops:
  0.7 1.3 fusion.12
  2.0 1.4 stack.43.sc
  5.9 2.5 %collective-permute-start = (bf16[9,128,64]{2,1,0:T(8,128)(2,1)S(1)}, bf16[9,128,64]{2,1,0:T(8,128)(2,1)S(1)}, u32[]{:S(2)}, u32[]{:S(2)}) collective-permute-start(bf16[9,128,64]{2,1,0:T(8,128)(2,1)S(1)} %get-tuple-element.31), channel_id=1, source_target_pairs={{0,16},{1,17},{2,18},{3,19},{4,20},{5,21},{6,22},{7,23},{8,24},{9,... | collective-permute-start | bytes 442376 | tf_op jit(solution)/shard_map/ppermute | solution.py:393
  8.5 2.3 %collective-permute-start.1 = (bf16[9,128,64]{2,1,0:T(8,128)(2,1)S(1)}, bf16[9,128,64]{2,1,0:T(8,128)(2,1)S(1)}, u32[]{:S(2)}, u32[]{:S(2)}) collective-permute-start(bf16[9,128,64]{2,1,0:T(8,128)(2,1)S(1)} %get-tuple-element.32), channel_id=1, source_target_pairs={{0,112},{1,113},{2,114},{3,115},{4,116},{5,117},{6,118},{7,119},{8... | collective-permute-start | bytes 442376 | tf_op jit(solution)/shard_map/ppermute | solution.py:393
  10.8 1.2 fusion.3
  16.3 1.8 %fusion.11 = (bf16[3,3,64,1,64]{4,2,3,1,0:T(8,128)(2,1)}, bf16[3,3,64,1,64]{4,2,3,1,0:T(8,128)(2,1)}, bf16[3,3,64,1,64]{4,2,3,1,0:T(8,128)(2,1)}) fusion(bf16[3,3,64,3,64]{4,2,3,1,0:T(8,128)(2,1)} %bitcast.127), kind=kLoop, calls=%fused_computation.47 | loop fusion | bytes 442368 | tf_op jit(solution)/shard_map/slice | solution.py:379
  23.1 1.1 copy.22
  24.3 1.8 %copy.23 = bf16[3,3,128,1,64]{4,2,1,0,3:T(8,128)(2,1)} copy(bf16[3,3,128,1,64]{2,4,3,1,0:T(8,128)(2,1)} %get-tuple-element.78) | data formatting | bytes 294912 | tf_op jit(solution)/shard_map/slice | solution.py:379
  26.1 2.1 %pad_maximum_fusion.3.w4l = bf16[3,384,192]{2,1,0:T(8,128)(2,1)} fusion(bf16[3,384,64]{2,1,0:T(8,128)(2,1)} %bitcast.108, bf16[3,384,64]{2,1,0:T(8,128)(2,1)S(1)} %bitcast.107, bf16[3,384,64]{2,1,0:T(8,128)(2,1)S(1)} %bitcast.106), kind=kLoop, calls=%fused_computation.9 | loop fusion | flops 1327104 | bytes 884736 | tf_op jit(solution)/shard_map/concatenate | solution.py:379
  28.2 1.2 pad_maximum_fusion.4.w7
  29.8 1.9 %copy.18 = bf16[3,3,128,1,128]{4,2,1,0,3:T(8,128)(2,1)} copy(bf16[3,3,128,1,128]{2,4,3,1,0:T(8,128)(2,1)} %get-tuple-element.67) | data formatting | bytes 589824 | tf_op jit(solution)/shard_map/slice | solution.py:379
  33.5 2.2 %concatenate.124.w5 = bf16[3,192,576]{2,1,0:T(8,128)(2,1)} concatenate(bf16[3,192,128]{2,1,0:T(8,128)(2,1)} %bitcast.114, bf16[3,192,128]{2,1,0:T(8,128)(2,1)} %bitcast.113, bf16[3,192,128]{2,1,0:T(8,128)(2,1)} %bitcast.112, bf16[3,192,64]{2,1,0:T(8,128)(2,1)} %bitcast.117, bf16[3,192,64]{2,1,0:T(8,128)(2,1)} %bitcast.116, bf16[3,192,64]{2,1,0:T(8,128)(2,1)} %bitcast.115), dimensions={2} | concatenate | bytes 1327104 | tf_op jit(solution)/shard_map/concatenate | solution.py:424
  35.7 2.2 %pad_maximum_fusion.1.w3 = bf16[3,384,384]{2,1,0:T(8,128)(2,1)} fusion(bf16[3,384,128]{2,1,0:T(8,128)(2,1)S(1)} %bitcast.101, bf16[3,384,128]{2,1,0:T(8,128)(2,1)} %bitcast.102, bf16[3,384,128]{2,1,0:T(8,128)(2,1)S(1)} %bitcast.100), kind=kLoop, calls=%fused_computation.6 | loop fusion | flops 2654208 | bytes 1769472 | tf_op jit(solution)/shard_map/concatenate | solution.py:379
  40.9 3.5 %collective-permute-start.3 = (bf16[24,64,64]{2,1,0:T(8,128)(2,1)S(1)}, bf16[24,64,64]{2,1,0:T(8,128)(2,1)S(1)}, u32[]{:S(2)}, u32[]{:S(2)}) collective-permute-start(bf16[24,64,64]{2,1,0:T(8,128)(2,1)S(1)} %get-tuple-element.35), channel_id=1, source_target_pairs={{0,15},{1,2},{2,1},{3,4},{4,3},{5,6},{6,5},{7,8},{8,7},{9,10},{10,... | collective-permute-start | bytes 589832 | tf_op jit(solution)/shard_map/ppermute | solution.py:393
  44.4 1.1 pad_maximum_fusion.2.w6
  45.5 8.5 %collective-permute-done.3.r4 = bf16[24,64,64]{2,1,0:T(8,128)(2,1)S(1)} collective-permute-done((bf16[24,64,64]{2,1,0:T(8,128)(2,1)S(1)}, bf16[24,64,64]{2,1,0:T(8,128)(2,1)S(1)}, u32[]{:S(2)}, u32[]{:S(2)}) %collective-permute-start.3) | collective-permute-done | bytes 196640 | tf_op jit(solution)/shard_map/ppermute | solution.py:393
  54.0 25.7 %shard_map.112 = (bf16[8,128,64]{2,1,0:T(8,128)(2,1)}, f32[8,128,64]{2,1,0:T(8,128)S(1)}, f32[8,128,64]{2,1,0:T(8,128)S(1)}, f32[6,80,128]{2,1,0:T(8,128)S(1)}, ...) custom-call(s32[8]{0:T(128)S(1)} %stack.43.sc, ...), custom_call_target="tpu_custom_call" | custom-call | flops 4000000000 | bytes 4000000 | tf_op jit(solution)/shard_map/pallas_call | solution.py:440
  80.0 1.6 collective-permute-start.5
  81.6 1.2 copy-done.6
  82.7 1.1 copy-done.7
  83.8 3.1 %shard_map.113 = (bf16[9,192,128]{2,1,0:T(8,128)(2,1)S(1)}, bf16[9,96,128]{2,1,0:T(8,128)(2,1)S(1)}, bf16[27,128,128]{2,1,0:T(8,128)(2,1)S(1)}) custom-call(s32[8]{0:T(128)S(1)} %stack.43.sc, bf16[12,144,384]{2,1,0:T(8,128)(2,1)} %get-tuple-element.37.s_lift, bf16[12,144,192]{2,1,0:T(8,128)(2,1)S(1)} %copy-done.6, bf16[8,144,192]{2,1,0:T(8,128)(2,1)S(1)} %copy-done.7, ...), custom_call_target="tpu_custom_call" | custom-call | flops 1000000000 | bytes 4000000 | tf_op jit(solution)/shard_map/pallas_call | solution.py:488
  87.1 3.9 %collective-permute-start.7 = (bf16[8,16,128]{2,1,0:T(8,128)(2,1)S(1)}, bf16[8,16,128]{2,1,0:T(8,128)(2,1)S(1)}, u32[]{:S(2)}, u32[]{:S(2)}) collective-permute-start(bf16[8,16,128]{2,1,0:T(8,128)(2,1)S(1)} %broadcast_select_fusion.4), channel_id=1, source_target_pairs={{0,15},{1,2},{2,1},{3,4},{4,3},{5,6},{6,5},{7,8},{8,7},{9,10},{10,... | collective-permute-start | bytes 98312 | tf_op jit(solution)/shard_map/ppermute | solution.py:393
  91.5 1.4 collective-permute-done.7
  92.9 3.7 %shard_map.114 = (bf16[9,64,128]{2,1,0:T(8,128)(2,1)S(1)}, bf16[9,32,128]{2,1,0:T(8,128)(2,1)S(1)}, bf16[27,64,128]{2,1,0:T(8,128)(2,1)S(1)}) custom-call(s32[8]{0:T(128)S(1)} %stack.43.sc, bf16[8,96,128]{2,1,0:T(8,128)(2,1)S(1)} %pad_maximum_fusion.8.gx, f32[6,80,128]{2,1,0:T(8,128)S(1)} %get-tuple-element.45.slope_ec, ...), custom_call_target="tpu_custom_call" | custom-call | flops 500000000 | bytes 4000000 | tf_op jit(solution)/shard_map/pallas_call | solution.py:495
  98.3 2.6 %collective-permute-done.8 = bf16[64,72,128]{2,1,0:T(8,128)(2,1)} collective-permute-done((bf16[64,72,128]{2,1,0:T(8,128)(2,1)S(1)}, bf16[64,72,128]{2,1,0:T(8,128)(2,1)}, u32[]{:S(2)}, u32[]{:S(2)}) %collective-permute-start.8) | collective-permute-done | bytes 1179680 | tf_op jit(solution)/shard_map/ppermute | solution.py:393
  100.9 1.6 fusion
  102.5 27.1 %all_to_all.10 = bf16[64,72,128]{2,1,0:T(8,128)(2,1)S(1)} all-to-all(bf16[64,72,128]{2,1,0:T(8,128)(2,1)S(1)} %fusion), channel_id=1, replica_groups=mesh['row'=8,'colh'=8,'core'=2] {'row','colh'}, dimensions={0} | all-to-all | bytes 2359296 | tf_op jit(solution)/shard_map/all_to_all | solution.py:513
  129.9 22.5 %all_to_all.11 = bf16[64,72,128]{2,1,0:T(8,128)(2,1)S(1)} all-to-all(bf16[64,72,128]{2,1,0:T(8,128)(2,1)S(1)} %broadcast_in_dim.14), channel_id=1, replica_groups=mesh['row'=8,'colh'=8,'core'=2] {'row','colh'}, dimensions={0} | all-to-all | bytes 2359296 | tf_op jit(solution)/shard_map/all_to_all | solution.py:515
  152.4 3.4 %collective-permute-start.9 = (bf16[64,72,128]{2,1,0:T(8,128)(2,1)S(1)}, bf16[64,72,128]{2,1,0:T(8,128)(2,1)S(1)}, u32[]{:S(2)}, u32[]{:S(2)}) collective-permute-start(bf16[64,72,128]{2,1,0:T(8,128)(2,1)S(1)} %all_to_all.11), channel_id=1, source_target_pairs={{0,1},{1,0},{2,3},{3,2},{4,5},{5,4},{6,7},{7,6},{8,9},{9,8},{10,11... | collective-permute-start | bytes 3538952 | tf_op jit(solution)/shard_map/ppermute | solution.py:393
  155.8 2.5 %collective-permute-done.9 = bf16[64,72,128]{2,1,0:T(8,128)(2,1)S(1)} collective-permute-done((bf16[64,72,128]{2,1,0:T(8,128)(2,1)S(1)}, bf16[64,72,128]{2,1,0:T(8,128)(2,1)S(1)}, u32[]{:S(2)}, u32[]{:S(2)}) %collective-permute-start.9) | collective-permute-done | bytes 1179680 | tf_op jit(solution)/shard_map/ppermute | solution.py:393
  158.6 3.4 %shard_map.115 = (f32[27,192,64]{2,1,0:T(8,128)}, f32[27,128,128]{2,1,0:T(8,128)}, f32[27,64,64]{2,1,0:T(8,128)}, f32[27,64,128]{2,1,0:T(8,128)}) custom-call(s32[8]{0:T(128)S(1)} %stack.43.sc, bf16[9,192,128]{2,1,0:T(8,128)(2,1)S(1)} %bitcast.78, bf16[9,96,128]{2,1,0:T(8,128)(2,1)S(1)} %bitcast.84, bf16[27,128,128]{2,1,0:T(8,128)(2,1)S(1)} %bitcast.77, ...), custom_call_target="tpu_custom_call" | custom-call | bytes 4000000 | tf_op jit(solution)/shard_map/pallas_call | solution.py:525
  162.0 3.4 %copy.24 = f32[3,3,3,192,64]{3,4,2,1,0:T(8,128)} copy(f32[3,3,3,192,64]{4,3,2,1,0:T(8,128)} %bitcast.98) | data formatting | bytes 2654208
  (103 shorter events, 20.2 us)
Async XLA Ops:
  3.4 1.0 copy-start
  5.3 6.7 %copy-start.13 = (bf16[3,3,3,192,64]{3,4,2,1,0:T(8,128)(2,1)S(1)}, bf16[3,3,3,192,64]{3,4,2,1,0:T(8,128)(2,1)}, u32[]{:S(2)}) copy-start(bf16[3,3,3,192,64]{3,4,2,1,0:T(8,128)(2,1)} %param.12) | copy-start | bytes 1990660
  5.9 31.9 %collective-permute-start = (bf16[9,128,64]{2,1,0:T(8,128)(2,1)S(1)}, bf16[9,128,64]{2,1,0:T(8,128)(2,1)S(1)}, u32[]{:S(2)}, u32[]{:S(2)}) collective-permute-start(bf16[9,128,64]{2,1,0:T(8,128)(2,1)S(1)} %get-tuple-element.31), channel_id=1, source_target_pairs={{0,16},{1,17},{2,18},{3,19},{4,20},{5,21},{6,22},{7,23},{8,24},{9,... | collective-permute-start | bytes 442376 | tf_op jit(solution)/shard_map/ppermute | solution.py:393
  8.5 29.4 %collective-permute-start.1 = (bf16[9,128,64]{2,1,0:T(8,128)(2,1)S(1)}, bf16[9,128,64]{2,1,0:T(8,128)(2,1)S(1)}, u32[]{:S(2)}, u32[]{:S(2)}) collective-permute-start(bf16[9,128,64]{2,1,0:T(8,128)(2,1)S(1)} %get-tuple-element.32), channel_id=1, source_target_pairs={{0,112},{1,113},{2,114},{3,115},{4,116},{5,117},{6,118},{7,119},{8... | collective-permute-start | bytes 442376 | tf_op jit(solution)/shard_map/ppermute | solution.py:393
  15.5 4.0 %copy-start.8 = (bf16[3,3,3,128,128]{4,3,2,1,0:T(8,128)(2,1)S(1)}, bf16[3,3,3,128,128]{4,3,2,1,0:T(8,128)(2,1)}, u32[]{:S(2)}) copy-start(bf16[3,3,3,128,128]{4,3,2,1,0:T(8,128)(2,1)} %param.11) | copy-start | bytes 2654212
  19.5 1.0 copy-start.9
  26.1 3.4 %copy-start.14 = (bf16[3,3,64,1,64]{4,2,3,1,0:T(8,128)(2,1)S(1)}, bf16[3,3,64,1,64]{4,2,3,1,0:T(8,128)(2,1)}, u32[]{:S(2)}) copy-start(bf16[3,3,64,1,64]{4,2,3,1,0:T(8,128)(2,1)} %get-tuple-element.95) | copy-start | bytes 221188
  26.1 3.4 %copy-start.15 = (bf16[3,3,64,1,64]{4,2,3,1,0:T(8,128)(2,1)S(1)}, bf16[3,3,64,1,64]{4,2,3,1,0:T(8,128)(2,1)}, u32[]{:S(2)}) copy-start(bf16[3,3,64,1,64]{4,2,3,1,0:T(8,128)(2,1)} %get-tuple-element.96) | copy-start | bytes 221188
  26.1 3.4 %copy-start.16 = (bf16[3,3,64,1,64]{4,2,3,1,0:T(8,128)(2,1)S(1)}, bf16[3,3,64,1,64]{4,2,3,1,0:T(8,128)(2,1)}, u32[]{:S(2)}) copy-start(bf16[3,3,64,1,64]{4,2,3,1,0:T(8,128)(2,1)} %get-tuple-element.97) | copy-start | bytes 221188
  26.1 3.4 %copy-start.17 = (bf16[3,3,64,1,64]{4,2,1,0,3:T(8,128)(2,1)S(1)}, bf16[3,3,64,1,64]{4,2,1,0,3:T(8,128)(2,1)}, u32[]{:S(2)}) copy-start(bf16[3,3,64,1,64]{4,2,1,0,3:T(8,128)(2,1)} %copy.15) | copy-start | bytes 221188
  26.1 3.4 %copy-start.18 = (bf16[3,3,64,1,64]{4,2,1,0,3:T(8,128)(2,1)S(1)}, bf16[3,3,64,1,64]{4,2,1,0,3:T(8,128)(2,1)}, u32[]{:S(2)}) copy-start(bf16[3,3,64,1,64]{4,2,1,0,3:T(8,128)(2,1)} %copy.16) | copy-start | bytes 221188
  26.1 3.4 %copy-start.19 = (bf16[3,3,64,1,64]{4,2,1,0,3:T(8,128)(2,1)S(1)}, bf16[3,3,64,1,64]{4,2,1,0,3:T(8,128)(2,1)}, u32[]{:S(2)}) copy-start(bf16[3,3,64,1,64]{4,2,1,0,3:T(8,128)(2,1)} %copy.17) | copy-start | bytes 221188
  33.5 4.4 %copy-start.1 = (bf16[8,16,8,64]{3,2,1,0:T(8,128)(2,1)S(1)}, bf16[8,16,8,64]{3,2,1,0:T(8,128)(2,1)}, u32[]{:S(2)}) copy-start(bf16[8,16,8,64]{3,2,1,0:T(8,128)(2,1)} %param.7) | copy-start | bytes 393220
  33.5 4.4 %copy-start.3 = (bf16[8,16,8,64]{3,2,1,0:T(8,128)(2,1)S(1)}, bf16[8,16,8,64]{3,2,1,0:T(8,128)(2,1)}, u32[]{:S(2)}) copy-start(bf16[8,16,8,64]{3,2,1,0:T(8,128)(2,1)} %param.13) | copy-start | bytes 393220
  35.7 8.7 %copy-start.20 = (bf16[3,3,64,1,128]{4,2,3,1,0:T(8,128)(2,1)S(1)}, bf16[3,3,64,1,128]{4,2,3,1,0:T(8,128)(2,1)}, u32[]{:S(2)}) copy-start(bf16[3,3,64,1,128]{4,2,3,1,0:T(8,128)(2,1)} %get-tuple-element.92) | copy-start | bytes 442372
  35.7 8.7 %copy-start.21 = (bf16[3,3,64,1,128]{4,2,3,1,0:T(8,128)(2,1)S(1)}, bf16[3,3,64,1,128]{4,2,3,1,0:T(8,128)(2,1)}, u32[]{:S(2)}) copy-start(bf16[3,3,64,1,128]{4,2,3,1,0:T(8,128)(2,1)} %get-tuple-element.93) | copy-start | bytes 442372
  35.7 8.7 %copy-start.22 = (bf16[3,3,64,1,128]{4,2,3,1,0:T(8,128)(2,1)S(1)}, bf16[3,3,64,1,128]{4,2,3,1,0:T(8,128)(2,1)}, u32[]{:S(2)}) copy-start(bf16[3,3,64,1,128]{4,2,3,1,0:T(8,128)(2,1)} %get-tuple-element.94) | copy-start | bytes 442372
  35.7 8.7 %copy-start.10 = (bf16[3,3,128,1,128]{4,2,1,0,3:T(8,128)(2,1)S(1)}, bf16[3,3,128,1,128]{4,2,1,0,3:T(8,128)(2,1)}, u32[]{:S(2)}) copy-start(bf16[3,3,128,1,128]{4,2,1,0,3:T(8,128)(2,1)} %copy.18) | copy-start | bytes 884740
  35.7 8.7 %copy-start.11 = (bf16[3,3,128,1,128]{4,2,1,0,3:T(8,128)(2,1)S(1)}, bf16[3,3,128,1,128]{4,2,1,0,3:T(8,128)(2,1)}, u32[]{:S(2)}) copy-start(bf16[3,3,128,1,128]{4,2,1,0,3:T(8,128)(2,1)} %copy.19) | copy-start | bytes 884740
  35.7 8.7 %copy-start.12 = (bf16[3,3,128,1,128]{4,2,1,0,3:T(8,128)(2,1)S(1)}, bf16[3,3,128,1,128]{4,2,1,0,3:T(8,128)(2,1)}, u32[]{:S(2)}) copy-start(bf16[3,3,128,1,128]{4,2,1,0,3:T(8,128)(2,1)} %copy.20) | copy-start | bytes 884740
  38.9 1.0 copy-start.5
  39.9 5.6 %collective-permute-start.2 = (bf16[24,64,64]{2,1,0:T(8,128)(2,1)S(1)}, bf16[24,64,64]{2,1,0:T(8,128)(2,1)S(1)}, u32[]{:S(2)}, u32[]{:S(2)}) collective-permute-start(bf16[24,64,64]{2,1,0:T(8,128)(2,1)S(1)} %get-tuple-element.34), channel_id=1, source_target_pairs={{0,1},{1,0},{2,3},{3,2},{4,5},{5,4},{6,7},{7,6},{8,9},{9,8},{10,11... | collective-permute-start | bytes 589832 | tf_op jit(solution)/shard_map/ppermute | solution.py:393
  40.9 13.2 %collective-permute-start.3 = (bf16[24,64,64]{2,1,0:T(8,128)(2,1)S(1)}, bf16[24,64,64]{2,1,0:T(8,128)(2,1)S(1)}, u32[]{:S(2)}, u32[]{:S(2)}) collective-permute-start(bf16[24,64,64]{2,1,0:T(8,128)(2,1)S(1)} %get-tuple-element.35), channel_id=1, source_target_pairs={{0,15},{1,2},{2,1},{3,4},{4,3},{5,6},{6,5},{7,8},{8,7},{9,10},{10,... | collective-permute-start | bytes 589832 | tf_op jit(solution)/shard_map/ppermute | solution.py:393
  79.8 7.2 %collective-permute-start.4 = (bf16[2,64,128]{2,1,0:T(8,128)(2,1)S(1)}, bf16[2,64,128]{2,1,0:T(8,128)(2,1)S(1)}, u32[]{:S(2)}, u32[]{:S(2)}) collective-permute-start(bf16[2,64,128]{2,1,0:T(8,128)(2,1)S(1)} %get-tuple-element.102), channel_id=1, source_target_pairs={{0,16},{1,17},{2,18},{3,19},{4,20},{5,21},{6,22},{7,23},{8,24},{9,... | collective-permute-start | bytes 98312 | tf_op jit(solution)/shard_map/ppermute | solution.py:393
  80.0 7.0 %collective-permute-start.5 = (bf16[2,64,128]{2,1,0:T(8,128)(2,1)S(1)}, bf16[2,64,128]{2,1,0:T(8,128)(2,1)S(1)}, u32[]{:S(2)}, u32[]{:S(2)}) collective-permute-start(bf16[2,64,128]{2,1,0:T(8,128)(2,1)S(1)} %get-tuple-element.103), channel_id=1, source_target_pairs={{0,112},{1,113},{2,114},{3,115},{4,116},{5,117},{6,118},{7,119},{8... | collective-permute-start | bytes 98312 | tf_op jit(solution)/shard_map/ppermute | solution.py:393
  81.6 1.2 copy-start.6
  82.7 1.1 copy-start.7
  86.9 6.0 %copy-start.4 = (bf16[10,128,192]{2,1,0:T(8,128)(2,1)S(1)}, bf16[10,128,192]{2,1,0:T(8,128)(2,1)}, u32[]{:S(2)}) copy-start(bf16[10,128,192]{2,1,0:T(8,128)(2,1)} %get-tuple-element.47.s_in) | copy-start | bytes 1474564
  87.1 5.8 %collective-permute-start.7 = (bf16[8,16,128]{2,1,0:T(8,128)(2,1)S(1)}, bf16[8,16,128]{2,1,0:T(8,128)(2,1)S(1)}, u32[]{:S(2)}, u32[]{:S(2)}) collective-permute-start(bf16[8,16,128]{2,1,0:T(8,128)(2,1)S(1)} %broadcast_select_fusion.4), channel_id=1, source_target_pairs={{0,15},{1,2},{2,1},{3,4},{4,3},{5,6},{6,5},{7,8},{8,7},{9,10},{10,... | collective-permute-start | bytes 98312 | tf_op jit(solution)/shard_map/ppermute | solution.py:393
  90.9 1.9 %collective-permute-start.6 = (bf16[8,16,128]{2,1,0:T(8,128)(2,1)S(1)}, bf16[8,16,128]{2,1,0:T(8,128)(2,1)S(1)}, u32[]{:S(2)}, u32[]{:S(2)}) collective-permute-start(bf16[8,16,128]{2,1,0:T(8,128)(2,1)S(1)} %get-tuple-element.62), channel_id=1, source_target_pairs={{0,1},{1,0},{2,3},{3,2},{4,5},{5,4},{6,7},{7,6},{8,9},{9,8},{10,11... | collective-permute-start | bytes 98312 | tf_op jit(solution)/shard_map/ppermute | solution.py:393
  97.5 3.4 %collective-permute-start.8 = (bf16[64,72,128]{2,1,0:T(8,128)(2,1)S(1)}, bf16[64,72,128]{2,1,0:T(8,128)(2,1)}, u32[]{:S(2)}, u32[]{:S(2)}) collective-permute-start(bf16[64,72,128]{2,1,0:T(8,128)(2,1)S(1)} %dynamic-slice_bitcast_fusion), channel_id=1, source_target_pairs={{0,1},{1,0},{2,3},{3,2},{4,5},{5,4},{6,7},{7,6},{8,9},{9,8},{10,11... | collective-permute-start | bytes 3538952 | tf_op jit(solution)/shard_map/ppermute | solution.py:393
  152.4 5.8 %collective-permute-start.9 = (bf16[64,72,128]{2,1,0:T(8,128)(2,1)S(1)}, bf16[64,72,128]{2,1,0:T(8,128)(2,1)S(1)}, u32[]{:S(2)}, u32[]{:S(2)}) collective-permute-start(bf16[64,72,128]{2,1,0:T(8,128)(2,1)S(1)} %all_to_all.11), channel_id=1, source_target_pairs={{0,1},{1,0},{2,3},{3,2},{4,5},{5,4},{6,7},{7,6},{8,9},{9,8},{10,11... | collective-permute-start | bytes 3538952 | tf_op jit(solution)/shard_map/ppermute | solution.py:393
  (1 other events, 0.9 us)
where the time goes:
time: 166 us; the launch traced here: 165 us
  blocking collectives  49.5 us (30%)
  Pallas kernels  37.6 us (23%)
  local copies, waits for them, and re-layouts  33.7 us (20%)
  starting transfers between devices  19.5 us (12%)
  waiting for transfers between devices  15 us (9%)
  other arithmetic  9.02 us (5%)
    all_to_all x1, blocking collectives, body(): terms = lax.all_to_all(mine, ('row', 'colh'), 0, 0, tiled=True)  27.1 us
    pallas_call x1, Pallas kernels, body(): call(forward, [((8, 128, 64), BF16), ((8, 128, 64), F32), ((8, 128, 64),...  25.7 us
    all_to_all x1, blocking collectives, body(): lax.all_to_all(jnp.broadcast_to(total[None], terms.shape), ('row', 'colh'...  22.5 us
    ppermute x10, starting transfers between devices, swap(): return lax.ppermute(v, ('row', 'colh', 'core'), pairs)  19.5 us
    slice x21, local copies, waits for them, and re-layouts, side(): return jnp.concatenate([v[..., c, :] for c in order], axis=-1)  17.2 us
    ppermute x10, waiting for transfers between devices, swap(): return lax.ppermute(v, ('row', 'colh', 'core'), pairs)  15 us
    unnamed x52, local copies, waits for them, and re-layouts  8.97 us
    concatenate x6, other arithmetic, side(): return jnp.concatenate([v[..., c, :] for c in order], axis=-1)  6.96 us
  transfers between devices with their start and end apart: 10, of which 4 were waited for; matrix products, arithmetic and copies ran while one was open for 17% of the time, Pallas kernels for 2%

commit v1 on v0

v1 whole, which is shorter than its diff:
```python
import functools
import math

import jax
import jax.numpy as jnp
from jax import lax
from jax.experimental import pallas as pl
from jax.experimental.pallas import tpu as pltpu
from jax.sharding import Mesh, PartitionSpec as P

F32 = jnp.float32
BF16 = jnp.bfloat16
VMEM_LIMIT = 50 * 1024 * 1024
VM = pl.BlockSpec(memory_space=pltpu.VMEM)
SM = pl.BlockSpec(memory_space=pltpu.SMEM)
FACTOR = 1.0 / math.sqrt(64 * 256 * 8)
CHUNK = 72
ROWS_A, ROWS_B = 6144, 3072


def call(kernel, outs, scratch=(), flops=0, n_scalar=0, n_in=0):
    return pl.pallas_call(
        kernel,
        out_shape=[jax.ShapeDtypeStruct(s, d) for s, d in outs],
        in_specs=[SM] * n_scalar + [VM] * (n_in - n_scalar),
        out_specs=[VM] * len(outs),
        scratch_shapes=list(scratch),
        compiler_params=pltpu.CompilerParams(vmem_limit_bytes=VMEM_LIMIT),
        cost_estimate=pl.CostEstimate(flops=flops, bytes_accessed=4_000_000, transcendentals=0),
    )


def dot(lhs, rhs):
    return jnp.dot(lhs, rhs, preferred_element_type=F32)


def dot_n(lhs, rhs):
    return lax.dot_general(lhs, rhs, (((1,), (1,)), ((), ())), preferred_element_type=F32)


def dot_t(lhs, rhs):
    return lax.dot_general(lhs, rhs, (((0,), (0,)), ((), ())), preferred_element_type=F32)


def bround(v):
    return v.astype(BF16).astype(F32)


def z_of(shape):
    return lax.broadcasted_iota(jnp.int32, shape, len(shape) - 2)


def z_later(v):
    return jnp.where(z_of(v.shape) > 0, pltpu.roll(v, 1, 1), 0.0)


def z_earlier(v):
    return jnp.where(z_of(v.shape) < 7, pltpu.roll(v, 7, 1), 0.0)


def fold128(acc):
    rows = acc.shape[0]
    cube = acc.reshape(rows // 8, 8, 384)
    return z_later(cube[..., :128]) + cube[..., 128:256] + z_earlier(cube[..., 256:])


def taps_y(v, count):
    depth = v.shape[2]
    wide = jnp.concatenate([v[b : b + count] for b in range(3)], axis=2)
    return wide.reshape(count * 8, 3 * depth).astype(BF16)


def taps_z(g):
    wide = jnp.concatenate([z_earlier(g), g, z_later(g)], axis=2)
    return wide.reshape(g.shape[0] * 8, 3 * g.shape[2]).astype(BF16)


def halve_z(s):
    pair = s + pltpu.roll(s, 7, 1)
    z = z_of(s.shape)
    out = jnp.where(z == 0, pair, 0.0)
    for zc in (1, 2, 3):
        out = jnp.where(z == zc, pltpu.roll(pair, 8 - zc, 1), out)
    return out


def double_z(u):
    z = z_of(u.shape)
    out = u
    for shift in (1, 2, 3, 4):
        out = jnp.where((z + 1) // 2 == shift, pltpu.roll(u, shift, 1), out)
    return out


def silu_parts(v):
    sigma = jax.nn.sigmoid(v)
    act = v * sigma
    return act, sigma + act * (1.0 - sigma)


def place(axis):
    at = lax.axis_index("row") if axis == 0 else 2 * lax.axis_index("colh") + lax.axis_index("core")
    last = 7 if axis == 0 else 15
    return at % 2 == 1, (at > 0).astype(F32), (at < last).astype(F32)


def beside(first, second):
    return jnp.concatenate([first.astype(F32), second.astype(F32)], axis=1)


def pack_x(active, feat, cot, p1, p2):
    row = lax.broadcasted_iota(jnp.int32, (128, 64), 0)
    mask = jnp.where(row < 64, active[0], active[1]).astype(F32)
    row = lax.broadcasted_iota(jnp.int32, (16, 128), 0)
    ends = jnp.where(row < 8, active[0], active[1]).astype(F32).astype(BF16)
    odd, _, _ = place(0)
    for k in range(3):
        pair = beside(feat[2 * k + 1].astype(F32) * mask, feat[2 * k + 2].astype(F32) * mask).astype(BF16)
        p1[128 * k : 128 * k + 128] = pair
        p2[128 * k : 128 * k + 128] = pair
    for p, edge in ((p1, jnp.where(odd, 0, 7)), (p2, jnp.where(odd, 7, 0))):
        p[384:512] = beside(feat[edge].astype(F32) * mask, cot[edge]).astype(BF16)
        p[512:528] = ends


def pack_y(active, feat, cot, rz, rxz, xall, xmask, p3, p4):
    row = lax.broadcasted_iota(jnp.int32, (128, 64), 0)
    mask = jnp.where(row < 64, active[0], active[1]).astype(F32)
    row = lax.broadcasted_iota(jnp.int32, (16, 128), 0)
    odd, v_lo, v_hi = place(0)

    def lo(rows):
        return jnp.where(odd, rz[rows].astype(F32), rxz[rows].astype(F32)) * v_lo

    def hi(rows):
        return jnp.where(odd, rxz[rows].astype(F32), rz[rows].astype(F32)) * v_hi

    def own(k):
        return feat[k].astype(F32) * mask

    for k in range(3):
        slab = slice(128 * k, 128 * k + 128)
        xall[k] = lo(slab).astype(BF16)
        xall[4 + k] = beside(own(2 * k + 1), own(2 * k + 2)).astype(BF16)
        xall[8 + k] = hi(slab).astype(BF16)
        xall[12 + k] = beside(cot[2 * k + 1], cot[2 * k + 2]).astype(BF16)
    edge_lo, edge_hi = lo(slice(384, 512)), hi(slice(384, 512))
    xall[3] = beside(edge_lo[:, :64], own(0)).astype(BF16)
    xall[7] = beside(own(7), edge_hi[:, :64]).astype(BF16)
    xall[11] = beside(edge_lo[:, 64:], cot[0]).astype(BF16)
    xall[15] = beside(cot[7], edge_hi[:, 64:]).astype(BF16)
    xmask[0] = lo(slice(512, 528))
    xmask[1] = jnp.where(row < 8, active[0], active[1]).astype(F32)
    xmask[2] = hi(slice(512, 528))
    odd_c, _, _ = place(1)
    for p, low in ((p3, odd_c), (p4, jnp.logical_not(odd_c))):
        for k in range(11):
            near = jnp.where(low, xall[k, 0:64].astype(F32), xall[k, 64:128].astype(F32))
            p[64 * k : 64 * k + 64] = near.astype(BF16)
        cols = []
        for k in range(11, 16):
            slab = xall[k].astype(F32)
            cols.append(jnp.where(low, slab[0:8], slab[120:128]))
        for k in range(3):
            cols.append(jnp.where(low, xmask[k, 0:8], xmask[k, 8:16]))
        p[704:768] = jnp.concatenate(cols, axis=0).astype(BF16)


def forward(
    xall, xmask, r3, r4, w1, w2, w3, w4l, w4e, w5l, w5s,
    decoded, slope_ef, g_skip, slope_ec, g_dc, s_in, s_pool, s_ec, s_lift, s_skip, gz,
    mm, cc, s1, ee, s2, s3, slope_dc, s4, acc,
):
    odd, v_lo, v_hi = place(1)

    def lo(at, rows):
        at = pl.ds(at, rows)
        return (jnp.where(odd, r3[at].astype(F32), r4[at].astype(F32)) * v_lo).reshape(rows // 8, 8, 128)

    def hi(at, rows):
        at = pl.ds(at, rows)
        return (jnp.where(odd, r4[at].astype(F32), r3[at].astype(F32)) * v_hi).reshape(rows // 8, 8, 128)

    extra_lo, extra_hi = lo(704, 64), hi(704, 64)
    for k in range(5):
        cc[k, 0] = extra_lo[k]
        cc[k, 1:17] = xall[11 + k].astype(F32).reshape(16, 8, 128)
        cc[k, 17] = extra_hi[k]
    for k in range(3):
        mm[k, 0:6] = jnp.broadcast_to(extra_lo[5 + k][None], (6, 8, 128))
        mm[k, 6:14] = jnp.broadcast_to(xmask[k, 0:8][None], (8, 8, 128))
        mm[k, 14:22] = jnp.broadcast_to(xmask[k, 8:16][None], (8, 8, 128))
        mm[k, 22:28] = jnp.broadcast_to(extra_hi[5 + k][None], (6, 8, 128))

    def spread(i, _):
        at = pl.multiple_of(64 * i, 64)
        v = jnp.concatenate([lo(at, 64), xall[i].astype(F32).reshape(16, 8, 128), hi(at, 64)], axis=0)
        s1[i] = taps_y(v[1:31], 28)

        @pl.when(jnp.logical_and(i >= 3, i < 8))
        def _():
            s_in[i - 3] = taps_y(v[7:25], 16)

        return 0

    lax.fori_loop(0, 11, spread, 0)

    def encode(i, _):
        pre = fold128(dot(jnp.concatenate([s1[i], s1[i + 1]], axis=1), w1[...]))
        mask = mm[jnp.where(i < 3, 0, jnp.where(i < 7, 1, 2))]
        act, slope = silu_parts(pre)
        v = bround(act * mask)
        ee[i] = v

        @pl.when(jnp.logical_and(i >= 3, i < 7))
        def _():
            slope_ef[i - 3] = (slope * mask)[6:22].reshape(128, 128)

        s = v.reshape(14, 2, 8, 128)
        s = s[:, 0] + s[:, 1]
        s = s[..., :64] + s[..., 64:]
        v = bround(halve_z(s) * 0.125)
        s2[i] = taps_y(v, 12)

        @pl.when(jnp.logical_and(i >= 2, i < 8))
        def _():
            s_pool[i - 2] = taps_y(v[2:12], 8)

        return 0

    lax.fori_loop(0, 10, encode, 0)

    def mask_coarse(block, first, count):
        m = mm[block].reshape(14, 2, 8, 128)[first : first + count, 0]
        return jnp.where(z_of(m.shape) < 4, m, 0.0)

    def encode2(i, _):
        pre = jnp.zeros((384, 384), F32)
        for a in range(3):
            pre += dot(s2[pl.ds(4 * i + a, 4)].reshape(384, 192), w2[a])
        pre = fold128(pre).reshape(4, 12, 8, 128)
        for k in range(4):
            x = 4 * i + k
            mask = mask_coarse(jnp.where(x < 2, 0, jnp.where(x < 6, 1, 2)), 1, 12)
            act, slope = silu_parts(pre[k])
            v = bround(act * mask)
            s3[x] = taps_y(v, 10)

            @pl.when(jnp.logical_and(x >= 1, x < 7))
            def _():
                slope_ec[x - 1] = (slope * mask)[1:11].reshape(80, 128)
                s_ec[x - 1] = taps_y(v[1:11], 8)

        return 0

    lax.fori_loop(0, 2, encode2, 0)

    def decode2(i, _):
        pre = jnp.zeros((240, 384), F32)
        for a in range(3):
            pre += dot(s3[pl.ds(3 * i + a, 3)].reshape(240, 384), w3[a])
        pre = fold128(pre).reshape(3, 10, 8, 128)
        for k in range(3):
            x = 3 * i + k
            mask = mask_coarse(jnp.where(x < 1, 0, jnp.where(x < 5, 1, 2)), 2, 10)
            act, slope = silu_parts(pre[k])
            v = double_z(bround(act * mask))
            up = jnp.concatenate([v[:, None], v[:, None]], axis=1).reshape(20, 8, 128)
            s_lift[x] = taps_y(up, 18)

            @pl.when(jnp.logical_and(x >= 1, x < 5))
            def _():
                slope_dc[x - 1] = (slope * mask)[1:9]

        return 0

    lax.fori_loop(0, 2, decode2, 0)

    def skip(i, _):
        s_skip[i] = taps_y(ee[i + 2, 4:24], 18)
        return 0

    lax.fori_loop(0, 6, skip, 0)

    first, second = s_lift[0:5].reshape(720, 384), s_lift[1:6].reshape(720, 384)
    acc[...] = dot_n(first, w4l[0]) + dot_n(first, w4l[1]) + dot_n(second, w4l[2]) + dot_n(second, w4l[3])
    acc[...] += dot_n(s_skip[0:5].reshape(720, 384), w4e[0]) + dot_n(s_skip[1:6].reshape(720, 384), w4e[1])

    def decode(i, _):
        pre = fold128(acc[pl.ds(pl.multiple_of(144 * i, 144), 144)])
        lane = lax.broadcasted_iota(jnp.int32, (18, 8, 128), 2)
        before, after = jnp.where(i < 1, 0, 1), jnp.where(i < 4, 1, 2)
        mask = jnp.where(lane < 64, mm[before, 5:23], mm[after, 5:23])
        act, slope = silu_parts(pre)
        g = bround(cc[i] * mask * slope)
        s4[i] = taps_y(g, 16)
        out = (act * mask)[1:17].reshape(128, 128).astype(BF16)

        @pl.when(i > 0)
        def _():
            decoded[2 * i - 1] = out[:, :64]

        @pl.when(i < 4)
        def _():
            decoded[2 * i] = out[:, 64:]

        own = jnp.logical_and(jnp.logical_or(lane >= 64, i > 0), jnp.logical_or(lane < 64, i < 4))
        g = jnp.where(own, g, 0.0)
        zero = jnp.zeros((1, 8, 128), F32)
        gz[i] = taps_z(jnp.concatenate([zero, g[1:17], zero], axis=0))
        return 0

    lax.fori_loop(0, 5, decode, 0)

    def back(i, _):
        wide = jnp.concatenate([s4[pl.ds(2 * i, 2)], s4[pl.ds(2 * i + 1, 2)]], axis=2).reshape(256, 768)
        g_skip[pl.ds(2 * i, 2)] = fold128(dot(wide, w5s[...])).reshape(2, 128, 128)
        up = (dot(wide, w5l[0]) + dot(wide, w5l[1])).reshape(16, 2, 8, 384)
        g = halve_z(fold128((up[:, 0] + up[:, 1]).reshape(128, 384)))
        g = g.reshape(2, 8, 8, 128) * slope_dc[pl.ds(2 * i, 2)]
        g_dc[pl.ds(2 * i, 2)] = g.reshape(2, 64, 128).astype(BF16)
        return 0

    lax.fori_loop(0, 2, back, 0)


def unhalve(both):
    return jnp.concatenate([both[:, :64], both[:, 64:]], axis=0)


def split_wire(wire, keep, send):
    rows = wire.shape[0] // 2
    core = lax.axis_index("core")
    keep[...] = wire[pl.ds(pl.multiple_of(core * rows, rows), rows)]
    send[...] = wire[pl.ds(pl.multiple_of((1 - core) * rows, rows), rows)]


A_SKIP, A_SKIP2, A_COARSE, A_END = 1728, 2304, 2592, 6048
B_FINE2, B_COARSE, B_END = 576, 864, 2592


def weights_decode(s_lift, s_skip, gz, s_ec, g_dc, keep, send, wire):
    grad = gz[...].reshape(720, 384)
    gc = taps_z(g_dc[...].astype(F32).reshape(32, 8, 128))
    wire[A_END:] = jnp.zeros((wire.shape[0] - A_END, 128), BF16)
    up = [(dot_t(grad, s_lift[p : p + 5].reshape(720, 384)) * FACTOR).reshape(3, 2, 64, 384) for p in range(2)]
    same = [(dot_t(grad, s_skip[p : p + 5].reshape(720, 384)) * FACTOR).reshape(3, 2, 64, 384) for p in range(2)]
    for a, (p, q) in enumerate(((0, 0), (0, 1), (1, 0))):
        p2, q2 = (0, 1) if a == 0 else (1, a - 1)
        lifted = (up[p][:, 0] + up[p2][:, 1]).reshape(192, 384).astype(BF16)
        for b in range(3):
            at = 64 * (9 * a + 3 * b)
            wire[at : at + 192] = lifted[:, 128 * b : 128 * b + 128]
        taps = []
        for b in range(3):
            lanes = slice(128 * b, 128 * b + 128)
            taps.append(add_halves(same[p][:, 0, :, lanes].reshape(192, 128), q, same[p2][:, 1, :, lanes].reshape(192, 128), q2))
        put_three(wire, A_SKIP + 192 * a, A_SKIP2 + 96 * a, taps)
        res = (dot_t(s_ec[a : a + 4].reshape(256, 384), gc) * FACTOR).astype(BF16)
        for b in range(3):
            for c in range(3):
                at = A_COARSE + 128 * (9 * a + 3 * b + c)
                wire[at : at + 128] = res[128 * b : 128 * b + 128, 128 * c : 128 * c + 128]
    split_wire(wire, keep, send)


def add_halves(first, q, second, q2):
    low = (first if q == 0 else pltpu.roll(first, 64, 1)) + (second if q2 == 0 else pltpu.roll(second, 64, 1))
    high = (first if q == 1 else pltpu.roll(first, 64, 1)) + (second if q2 == 1 else pltpu.roll(second, 64, 1))
    return low, high


def put_three(wire, at, at2, taps):
    lane = lax.broadcasted_iota(jnp.int32, (192, 128), 1)
    wire[at : at + 192] = jnp.where(lane < 64, taps[0][0], taps[1][1]).astype(BF16)
    wire[at2 : at2 + 96] = jnp.where(lane[:96] < 64, taps[2][0][:96], taps[2][1][96:]).astype(BF16)


def back_encode(gx, slope_ec, s_pool, s_in, g_skip, slope_ef, w6, w7, keep, send, s5, ge, gz, wire):
    def spread(x, _):
        s5[x] = taps_y(gx[x].astype(F32).reshape(12, 8, 128), 10)
        return 0

    lax.fori_loop(0, 8, spread, 0)
    acc = jnp.zeros((480, 384), F32)
    for a in range(3):
        acc += dot_n(s5[a : a + 6].reshape(480, 384), w6[a])
    g_ec = bround(fold128(acc) * slope_ec[...].reshape(60, 8, 128)).reshape(6, 10, 8, 128)
    for x in range(6):
        ge[x] = taps_y(g_ec[x], 8)
    gc = taps_z(g_ec[1:5, 1:9].reshape(32, 8, 128))
    acc = jnp.zeros((256, 384), F32)
    for a in range(3):
        acc += dot_n(ge[a : a + 4].reshape(256, 384), w7[a])
    up = double_z(fold128(acc) * 0.125)
    up = jnp.concatenate([up[:, None], up[:, None]], axis=1).reshape(4, 16, 8, 128)
    for x in range(4):
        g = (g_skip[x].reshape(16, 8, 128) + up[x]) * slope_ef[x].reshape(16, 8, 128)
        gz[x] = taps_z(bround(g))
    gf = gz[...].reshape(512, 384)
    wire[B_END:] = jnp.zeros((wire.shape[0] - B_END, 128), BF16)
    parts = [(dot_t(s_in[p : p + 4].reshape(512, 384), gf) * FACTOR).reshape(3, 2, 64, 384) for p in range(2)]
    for a, (p, q) in enumerate(((0, 0), (0, 1), (1, 0))):
        p2, q2 = (0, 1) if a == 0 else (1, a - 1)
        taps = []
        for c in range(3):
            lanes = slice(128 * c, 128 * c + 128)
            taps.append(add_halves(parts[p][:, q, :, lanes].reshape(192, 128), 0, parts[p2][:, q2, :, lanes].reshape(192, 128), 1))
        put_three(wire, 192 * a, B_FINE2 + 96 * a, taps)
        res = (dot_t(s_pool[a : a + 4].reshape(256, 192), gc) * FACTOR).astype(BF16)
        for b in range(3):
            for c in range(3):
                at = B_COARSE + 64 * (9 * a + 3 * b + c)
                wire[at : at + 64] = res[64 * b : 64 * b + 64, 128 * c : 128 * c + 128]
    split_wire(wire, keep, send)


def unpack(mine, other, d_df, d_dc, d_ef, d_ec, wire_a, wire_b):
    core = lax.axis_index("core")
    for wire, first in ((wire_a, 0), (wire_b, ROWS_A // 128)):
        rows = wire.shape[0] // 2
        each = rows // 64
        here = pl.ds(pl.multiple_of(core * rows, rows), rows)
        there = pl.ds(pl.multiple_of((1 - core) * rows, rows), rows)
        wire[here] = mine[:, first : first + each].reshape(rows, 128)
        wire[there] = other[:, first : first + each].reshape(rows, 128)
    d_dc[...] = wire_a[A_COARSE:A_END].astype(F32).reshape(27, 128, 128)
    d_ec[...] = wire_b[B_COARSE:B_END].astype(F32).reshape(27, 64, 128)
    for a in range(3):
        two = wire_a[A_SKIP + 192 * a : A_SKIP + 192 * a + 192].astype(F32)
        three = unhalve(wire_a[A_SKIP2 + 96 * a : A_SKIP2 + 96 * a + 96].astype(F32))
        skip = (two[:, :64], two[:, 64:], three)
        two = wire_b[192 * a : 192 * a + 192].astype(F32)
        three = unhalve(wire_b[B_FINE2 + 96 * a : B_FINE2 + 96 * a + 96].astype(F32))
        fine = (two[:, :64], two[:, 64:], three)
        for b in range(3):
            for c in range(3):
                k = 9 * a + 3 * b + c
                d_df[k, :, :128] = wire_a[64 * k : 64 * k + 64].astype(F32)
                d_df[k, :, 128:] = skip[b][64 * c : 64 * c + 64]
                d_ef[k] = fine[c][64 * b : 64 * b + 64]


def arrange(e1, e2, d3, d4, w1, w2, w3, w4l, w4e, w5l, w5s, w6, w7):
    for a in range(3):
        for b in range(3):
            fine, coarse = slice(64 * b, 64 * b + 64), slice(128 * b, 128 * b + 128)
            for c in range(3):
                k = 9 * a + 3 * b + c
                lanes = slice(128 * c, 128 * c + 128)
                w2[a, fine, lanes] = e2[k]
                w3[a, coarse, lanes] = d3[k]
                w6[a, lanes, coarse] = d3[26 - k]
                w7[a, 128 * c : 128 * c + 64, coarse] = e2[26 - k]
                w7[a, 128 * c + 64 : 128 * c + 128, coarse] = e2[26 - k]
    none = jnp.zeros((64, 64), F32)

    def tap(ref, a, rest, lanes, turned=False):
        if a < 0 or a > 2:
            return none
        k = 9 * a + rest
        return ref[26 - k if turned else k, :, lanes].astype(F32)

    all_, low, high = slice(0, 64), slice(0, 128), slice(128, 192)
    for p in range(2):
        for b in range(3):
            for c in range(3):
                rest = 3 * b + c
                lanes = slice(128 * c, 128 * c + 128)
                for q in range(2):
                    rows = slice(384 * p + 128 * b + 64 * q, 384 * p + 128 * b + 64 * q + 64)
                    a = 2 * p + q
                    w1[rows, lanes] = beside(tap(e1, a, rest, all_), tap(e1, a - 1, rest, all_)).astype(BF16)
                    w5s[rows, lanes] = beside(
                        tap(d4, a, rest, high, True), tap(d4, a - 1, rest, high, True)
                    ).astype(BF16)
                    for o in range(2):
                        cols = slice(128 * c + 64 * o, 128 * c + 64 * o + 64)
                        coarse = slice(128 * b, 128 * b + 128)
                        if 0 <= a - o <= 2:
                            w5l[o, rows, lanes] = d4[26 - 9 * (a - o) - rest, :, low]
                            w4l[2 * p + q, cols, coarse] = d4[9 * (a - o) + rest, :, low]
                        else:
                            w5l[o, rows, lanes] = jnp.zeros((64, 128), BF16)
                            w4l[2 * p + q, cols, coarse] = jnp.zeros((64, 128), BF16)
                for o in range(2):
                    cols = slice(128 * c + 64 * o, 128 * c + 64 * o + 64)
                    w4e[p, cols, 128 * b : 128 * b + 128] = beside(
                        tap(d4, 2 * p - o, rest, high), tap(d4, 2 * p + 1 - o, rest, high)
                    ).astype(BF16)


def swap(v, pairs):
    return lax.ppermute(v, ("row", "colh", "core"), pairs)


def body(
    features, block_active, encode_fine, encode_coarse, decode_coarse, decode_fine, out_cotangent
):
    row = lax.axis_index("row")
    core = lax.axis_index("core")
    col = 2 * lax.axis_index("colh") + core
    at = [(r, c) for r in range(8) for c in range(16)]

    def up(i, n):
        return (i + 1) % n if i % 2 else (i - 1) % n

    swap_z = [(16 * r + c, 16 * (r ^ 1) + c) for r, c in at]
    swap_xz = [(16 * r + c, 16 * up(r, 8) + c) for r, c in at]
    swap_core = [(16 * r + c, 16 * r + (c ^ 1)) for r, c in at]
    swap_yz = [(16 * r + c, 16 * r + up(c, 16)) for r, c in at]

    odd_r, odd_c = row % 2, core
    active = block_active.reshape(2)
    w1, w2, w3, w4l, w4e, w5l, w5s, w6, w7 = call(
        arrange,
        [
            ((768, 384), BF16),
            ((3, 192, 384), BF16),
            ((3, 384, 384), BF16),
            ((4, 384, 384), BF16),
            ((2, 384, 384), BF16),
            ((2, 768, 384), BF16),
            ((768, 384), BF16),
            ((3, 384, 384), BF16),
            ((3, 384, 384), BF16),
        ],
        n_in=4,
    )(
        encode_fine.reshape(27, 64, 64),
        encode_coarse.reshape(27, 64, 128),
        decode_coarse.reshape(27, 128, 128),
        jnp.transpose(decode_fine, (0, 1, 2, 4, 3)).reshape(27, 64, 192),
    )

    feat = features.reshape(8, 128, 64)
    cot = out_cotangent.reshape(8, 128, 64)
    p1, p2 = call(pack_x, [((528, 128), BF16)] * 2, n_in=3, n_scalar=1)(active, feat, cot)
    rz, rxz = swap(p1, swap_z), swap(p2, swap_xz)
    xall, xmask, p3, p4 = call(
        pack_y,
        [((16, 128, 128), BF16), ((3, 16, 128), F32), ((768, 128), BF16), ((768, 128), BF16)],
        n_in=5,
        n_scalar=1,
    )(active, feat, cot, rz, rxz)
    r3, r4 = swap(p3, swap_core), swap(p4, swap_yz)

    decoded, slope_ef, g_skip, slope_ec, g_dc, s_in, s_pool, s_ec, s_lift, s_skip, gz = call(
        forward,
        [
            ((8, 128, 64), BF16),
            ((4, 128, 128), F32),
            ((4, 128, 128), F32),
            ((6, 80, 128), F32),
            ((4, 64, 128), BF16),
            ((5, 128, 384), BF16),
            ((6, 64, 192), BF16),
            ((6, 64, 384), BF16),
            ((6, 144, 384), BF16),
            ((6, 144, 384), BF16),
            ((5, 144, 384), BF16),
        ],
        scratch=[
            pltpu.VMEM((3, 28, 8, 128), F32),
            pltpu.VMEM((5, 18, 8, 128), F32),
            pltpu.VMEM((11, 224, 384), BF16),
            pltpu.VMEM((10, 28, 8, 128), F32),
            pltpu.VMEM((10, 96, 192), BF16),
            pltpu.VMEM((8, 80, 384), BF16),
            pltpu.VMEM((4, 8, 8, 128), F32),
            pltpu.VMEM((5, 128, 384), BF16),
            pltpu.VMEM((720, 384), F32),
        ],
        n_in=11,
        flops=4_000_000_000,
    )(xall, xmask, r3, r4, w1, w2, w3, w4l, w4e, w5l, w5s)

    is_odd = odd_r == 1
    q1 = swap(jnp.where(is_odd, g_dc[:2], g_dc[2:]), swap_z)
    q2 = swap(jnp.where(is_odd, g_dc[2:], g_dc[:2]), swap_xz)
    zero = jnp.zeros_like(q1)
    before = jnp.where(row > 0, jnp.where(is_odd, q1, q2), zero)
    after = jnp.where(row < 7, jnp.where(is_odd, q2, q1), zero)
    gx = jnp.concatenate([before, g_dc, after], axis=0)
    is_odd = odd_c == 1
    q3 = swap(jnp.where(is_odd, gx[:, :16], gx[:, 48:]), swap_core)
    q4 = swap(jnp.where(is_odd, gx[:, 48:], gx[:, :16]), swap_yz)
    zero = jnp.zeros_like(q3)
    before = jnp.where(col > 0, jnp.where(is_odd, q3, q4), zero)
    after = jnp.where(col < 15, jnp.where(is_odd, q4, q3), zero)
    gx = jnp.concatenate([before, gx, after], axis=1)

    keep_a, send_a = call(
        weights_decode,
        [((ROWS_A // 2, 128), BF16)] * 2,
        scratch=[pltpu.VMEM((ROWS_A, 128), BF16)],
        n_in=5,
        flops=1_000_000_000,
    )(s_lift, s_skip, gz, s_ec, g_dc)
    got_a = swap(send_a, swap_core)

    keep_b, send_b = call(
        back_encode,
        [((ROWS_B // 2, 128), BF16)] * 2,
        scratch=[
            pltpu.VMEM((8, 80, 384), BF16),
            pltpu.VMEM((6, 64, 384), BF16),
            pltpu.VMEM((4, 128, 384), BF16),
            pltpu.VMEM((ROWS_B, 128), BF16),
        ],
        n_in=8,
        flops=500_000_000,
    )(gx, slope_ec, s_pool, s_in, g_skip, slope_ef, w6, w7)
    got_b = swap(send_b, swap_core)

    chips = ("row", "colh")
    half = jnp.concatenate(
        [
            (keep.astype(F32) + got.astype(F32)).astype(BF16).reshape(64, -1, 128)
            for keep, got in ((keep_a, got_a), (keep_b, got_b))
        ],
        axis=1,
    )
    terms = lax.all_to_all(half, chips, 0, 0, tiled=True)
    total = jnp.sum(terms.astype(F32), axis=0).astype(BF16)
    mine = lax.all_to_all(jnp.broadcast_to(total[None], (64, CHUNK, 128)), chips, 0, 0, tiled=True)
    other = swap(mine, swap_core)
    d_df, d_dc, d_ef, d_ec = call(
        unpack,
        [((27, 64, 192), F32), ((27, 128, 128), F32), ((27, 64, 64), F32), ((27, 64, 128), F32)],
        scratch=[pltpu.VMEM((ROWS_A, 128), BF16), pltpu.VMEM((ROWS_B, 128), BF16)],
        n_in=2,
    )(mine, other)
    return (
        decoded.reshape(8, 16, 8, 64),
        d_ef.reshape(3, 3, 3, 64, 64),
        d_ec.reshape(3, 3, 3, 64, 128),
        d_dc.reshape(3, 3, 3, 128, 128),
        jnp.transpose(d_df.reshape(3, 3, 3, 64, 192), (0, 1, 2, 4, 3)),
    )


def solution(mesh):
    split = Mesh(mesh.devices.reshape(8, 8, 2), ("row", "colh", "core"))
    field = P("row", ("colh", "core"), None, None)
    return jax.shard_map(
        body,
        mesh=split,
        in_specs=(field, P("row", ("colh", "core"), None), P(), P(), P(), P(), field),
        out_specs=(field, P(), P(), P(), P()),
        check_vma=False,
    )
```

time: 166 us -> 125 us (0.75)
  local copies, waits for them, and re-layouts: 33.7 us -> 7.63 us
  other arithmetic: 9.02 us -> 0.67 us
  starting transfers between devices: 19.5 us -> 27.4 us
  Pallas kernels: 37.6 us -> 30.2 us
  waiting for transfers between devices: 15 us -> 11.1 us
  blocking collectives: 49.5 us -> 47.2 us
    slice x29 -> x0, local copies, waits for them, and re-layouts: 20 us -> none  [the longest x21 17.2 us: side(): return jnp.concatenate([v[..., c, :] for c in order], axis=-1)]
    ppermute x10 -> x11, starting transfers between devices: 19.5 us -> 27.4 us  [swap(): return lax.ppermute(v, ('row', 'colh', 'core'), pairs)]
    pallas_call x6 -> x7, Pallas kernels: 37.6 us -> 30.2 us  [the longest x1 15.5 us: body(): call(forward, [((8, 128, 64), BF16), ((4, 128, 128), F32), ((4, 128, 128)...]
    concatenate x7 -> x1, other arithmetic: 7.01 us -> 0.09 us  [body(): jnp.concatenate([(keep.astype(F32) + got.astype(F32)).astype(BF16).reshap...]
    ppermute x10 -> x11, waiting for transfers between devices: 15 us -> 11.1 us  [swap(): return lax.ppermute(v, ('row', 'colh', 'core'), pairs)]
    all_to_all x2, blocking collectives: 49.5 us -> 47.2 us  [the longest x1 24.3 us: body(): terms = lax.all_to_all(half, chips, 0, 0, tiled=True)]
    concatenate x2 -> x0, local copies, waits for them, and re-layouts: 2.21 us -> none  [the longest x1 2.15 us: body(): jnp.concatenate([backward_weight(decode_fine[..., :128, :], natural), bac...]
    unnamed x52 -> x32, local copies, waits for them, and re-layouts: 8.97 us -> 7.48 us
  transfers between devices with their start and end apart: 10 -> 11, of which waited for: 4 -> 7; matrix products, arithmetic and copies ran while one was open for 17% -> 0% of each run, Pallas kernels for 2% -> 5%
where the time goes in v1:
time: 125 us
  blocking collectives  47.2 us (38%)
  Pallas kernels  30.2 us (24%)
  starting transfers between devices  27.4 us (22%)
  waiting for transfers between devices  11.1 us (9%)
  local copies, waits for them, and re-layouts  7.63 us (6%)
    ppermute x11, starting transfers between devices, swap(): return lax.ppermute(v, ('row', 'colh', 'core'), pairs)  27.4 us
    all_to_all x1, blocking collectives, body(): terms = lax.all_to_all(half, chips, 0, 0, tiled=True)  24.3 us
    all_to_all x1, blocking collectives, body(): lax.all_to_all(jnp.broadcast_to(total[None], (64, CHUNK, 128)), chips, 0,...  22.9 us
    pallas_call x1, Pallas kernels, body(): call(forward, [((8, 128, 64), BF16), ((4, 128, 128), F32), ((4, 128, 128)...  15.5 us
    ppermute x11, waiting for transfers between devices, swap(): return lax.ppermute(v, ('row', 'colh', 'core'), pairs)  11.1 us
    unnamed x32, local copies, waits for them, and re-layouts  7.48 us
    pallas_call x1, Pallas kernels, body(): call(arrange, [((768, 384), BF16), ((3, 192, 384), BF16), ((3, 384, 384),...  4.3 us
    pallas_call x1, Pallas kernels, body(): call(back_encode, [((ROWS_B // 2, 128), BF16)] * 2, scratch=[pltpu.VMEM((...  3.88 us
  transfers between devices with their start and end apart: 11, of which 7 were waited for; matrix products, arithmetic and copies ran while one was open for 0% of the time, Pallas kernels for 5%

profile of v1, /device:TPU:1, one launch (start us, length us, event | category | flops | bytes accessed | tf_op | source)
XLA Modules:
  0.0 124.9 jit_solution(14822849962820965776)
XLA Ops:
  0.6 0.9 copy-done
  1.6 0.9 copy-done.1
  2.5 0.7 copy-done.5
  3.2 0.7 shard_map.110
  3.9 2.5 %collective-permute-start = (bf16[528,128]{1,0:T(8,128)(2,1)S(1)}, bf16[528,128]{1,0:T(8,128)(2,1)S(1)}, u32[]{:S(2)}, u32[]{:S(2)}) collective-permute-start(bf16[528,128]{1,0:T(8,128)(2,1)S(1)} %get-tuple-element.39), channel_id=1, source_target_pairs={{0,16},{1,17},{2,18},{3,19},{4,20},{5,21},{6,22},{7,23},{8,24},{9,... | collective-permute-start | bytes 405512 | tf_op jit(solution)/shard_map/ppermute | solution.py:494
  6.4 2.3 %collective-permute-start.1 = (bf16[528,128]{1,0:T(8,128)(2,1)S(1)}, bf16[528,128]{1,0:T(8,128)(2,1)S(1)}, u32[]{:S(2)}, u32[]{:S(2)}) collective-permute-start(bf16[528,128]{1,0:T(8,128)(2,1)S(1)} %get-tuple-element.40), channel_id=1, source_target_pairs={{0,112},{1,113},{2,114},{3,115},{4,116},{5,117},{6,118},{7,119},{8... | collective-permute-start | bytes 405512 | tf_op jit(solution)/shard_map/ppermute | solution.py:494
  8.7 2.8 %collective-permute-done.rz = bf16[528,128]{1,0:T(8,128)(2,1)S(1)} collective-permute-done((bf16[528,128]{1,0:T(8,128)(2,1)S(1)}, bf16[528,128]{1,0:T(8,128)(2,1)S(1)}, u32[]{:S(2)}, u32[]{:S(2)}) %collective-permute-start) | collective-permute-done | bytes 135200 | tf_op jit(solution)/shard_map/ppermute | solution.py:494
  11.5 0.9 collective-permute-done.1.rxz
  12.4 0.8 shard_map.111
  13.2 2.2 %collective-permute-start.2 = (bf16[768,128]{1,0:T(8,128)(2,1)S(1)}, bf16[768,128]{1,0:T(8,128)(2,1)S(1)}, u32[]{:S(2)}, u32[]{:S(2)}) collective-permute-start(bf16[768,128]{1,0:T(8,128)(2,1)S(1)} %get-tuple-element.43), channel_id=1, source_target_pairs={{0,1},{1,0},{2,3},{3,2},{4,5},{5,4},{6,7},{7,6},{8,9},{9,8},{10,11... | collective-permute-start | bytes 589832 | tf_op jit(solution)/shard_map/ppermute | solution.py:494
  15.4 3.3 %collective-permute-start.3 = (bf16[768,128]{1,0:T(8,128)(2,1)S(1)}, bf16[768,128]{1,0:T(8,128)(2,1)S(1)}, u32[]{:S(2)}, u32[]{:S(2)}) collective-permute-start(bf16[768,128]{1,0:T(8,128)(2,1)S(1)} %get-tuple-element.44), channel_id=1, source_target_pairs={{0,15},{1,2},{2,1},{3,4},{4,3},{5,6},{6,5},{7,8},{8,7},{9,10},{10,... | collective-permute-start | bytes 589832 | tf_op jit(solution)/shard_map/ppermute | solution.py:494
  18.7 4.3 %shard_map.112 = (bf16[768,384]{1,0:T(8,128)(2,1)S(1)}, bf16[3,192,384]{2,1,0:T(8,128)(2,1)S(1)}, bf16[3,384,384]{2,1,0:T(8,128)(2,1)S(1)}, bf16[4,384,384]{2,1,...) custom-call(bf16[27,64,64]{2,1,0:T(8,128)(2,1)S(1)} %bitcast.22, ...), custom_call_target="tpu_custom_call" | custom-call | bytes 4000000 | tf_op jit(solution)/shard_map/pallas_call | solution.py:515
  23.0 0.9 copy-done.6
  23.9 0.8 copy-done.7
  24.7 0.8 copy-done.8
  25.6 0.8 copy-done.9
  26.4 15.5 %shard_map.113 = (bf16[8,128,64]{2,1,0:T(8,128)(2,1)}, f32[4,128,128]{2,1,0:T(8,128)S(1)}, f32[4,128,128]{2,1,0:T(8,128)S(1)}, f32[6,80,128]{2,1,0:T(8,128)S(1)}...) custom-call(bf16[16,128,128]{2,1,0:T(8,128)(2,1)S(1)} %get-tuple-ele, ...), custom_call_target="tpu_custom_call" | custom-call | flops 4000000000 | bytes 4000000 | tf_op jit(solution)/shard_map/pallas_call | solution.py:548
  41.9 0.8 copy-done.12
  42.7 0.7 copy-done.14
  43.7 2.9 %collective-permute-start.6 = (bf16[2,64,128]{2,1,0:T(8,128)(2,1)S(1)}, bf16[2,64,128]{2,1,0:T(8,128)(2,1)S(1)}, u32[]{:S(2)}, u32[]{:S(2)}) collective-permute-start(bf16[2,64,128]{2,1,0:T(8,128)(2,1)S(1)} %get-tuple-element.81), channel_id=1, source_target_pairs={{0,112},{1,113},{2,114},{3,115},{4,116},{5,117},{6,118},{7,119},{8... | collective-permute-start | bytes 98312 | tf_op jit(solution)/shard_map/ppermute | solution.py:494
  46.6 1.9 %collective-permute-done.6 = bf16[2,64,128]{2,1,0:T(8,128)(2,1)S(1)} collective-permute-done((bf16[2,64,128]{2,1,0:T(8,128)(2,1)S(1)}, bf16[2,64,128]{2,1,0:T(8,128)(2,1)S(1)}, u32[]{:S(2)}, u32[]{:S(2)}) %collective-permute-start.6) | collective-permute-done | bytes 32800 | tf_op jit(solution)/shard_map/ppermute | solution.py:494
  48.6 3.1 %collective-permute-start.8 = (bf16[8,16,128]{2,1,0:T(8,128)(2,1)S(1)}, bf16[8,16,128]{2,1,0:T(8,128)(2,1)S(1)}, u32[]{:S(2)}, u32[]{:S(2)}) collective-permute-start(bf16[8,16,128]{2,1,0:T(8,128)(2,1)S(1)} %broadcast_select_fusion.2), channel_id=1, source_target_pairs={{0,15},{1,2},{2,1},{3,4},{4,3},{5,6},{6,5},{7,8},{8,7},{9,10},{10,... | collective-permute-start | bytes 98312 | tf_op jit(solution)/shard_map/ppermute | solution.py:494
  51.8 1.4 %collective-permute-start.7 = (bf16[8,16,128]{2,1,0:T(8,128)(2,1)S(1)}, bf16[8,16,128]{2,1,0:T(8,128)(2,1)S(1)}, u32[]{:S(2)}, u32[]{:S(2)}) collective-permute-start(bf16[8,16,128]{2,1,0:T(8,128)(2,1)S(1)} %get-tuple-element.73), channel_id=1, source_target_pairs={{0,1},{1,0},{2,3},{3,2},{4,5},{5,4},{6,7},{7,6},{8,9},{9,8},{10,11... | collective-permute-start | bytes 98312 | tf_op jit(solution)/shard_map/ppermute | solution.py:494
  54.2 3.9 %shard_map.115 = (bf16[1536,128]{1,0:T(8,128)(2,1)S(1)}, bf16[1536,128]{1,0:T(8,128)(2,1)S(1)}) custom-call(bf16[8,96,128]{2,1,0:T(8,128)(2,1)S(1)} %pad_maximum_fusion.1.gx, f32[6,80,128]{2,1,0:T(8,128)S(1)} %get-tuple-element.60.slope_ec, bf16[6,64,192]{2,1,0:T(8,128)(2,1)S(1)} %get-tuple-element.61.s_pool, ...), custom_call_target="tpu_custom_call" | custom-call | flops 500000000 | bytes 4000000 | tf_op jit(solution)/shard_map/pallas_call | solution.py:602
  58.0 6.1 %collective-permute-start.9 = (bf16[1536,128]{1,0:T(8,128)(2,1)S(1)}, bf16[1536,128]{1,0:T(8,128)(2,1)S(1)}, u32[]{:S(2)}, u32[]{:S(2)}) collective-permute-start(bf16[1536,128]{1,0:T(8,128)(2,1)S(1)} %get-tuple-element.68), channel_id=1, source_target_pairs={{0,1},{1,0},{2,3},{3,2},{4,5},{5,4},{6,7},{7,6},{8,9},{9,8},{10,11... | collective-permute-start | bytes 1179656 | tf_op jit(solution)/shard_map/ppermute | solution.py:494
  64.1 2.2 %shard_map.114 = (bf16[3072,128]{1,0:T(8,128)(2,1)S(1)}, bf16[3072,128]{1,0:T(8,128)(2,1)S(1)}) custom-call(bf16[6,144,384]{2,1,0:T(8,128)(2,1)S(1)} %copy-done.10, bf16[6,144,384]{2,1,0:T(8,128)(2,1)S(1)} %copy-done.11, bf16[5,144,384]{2,1,0:T(8,128)(2,1)S(1)} %copy-done.13, bf16[6,64,384]{2,1,0:T(8,128)(2,1)S(1)} %copy-done.15, ...), custom_call_target="tpu_custom_call" | custom-call | flops 1000000000 | bytes 4000000 | tf_op jit(solution)/shard_map/pallas_call | solution.py:593
  66.7 2.1 %collective-permute-done.4 = bf16[3072,128]{1,0:T(8,128)(2,1)S(1)} collective-permute-done((bf16[3072,128]{1,0:T(8,128)(2,1)S(1)}, bf16[3072,128]{1,0:T(8,128)(2,1)S(1)}, u32[]{:S(2)}, u32[]{:S(2)}) %collective-permute-start.4) | collective-permute-done | bytes 786464 | tf_op jit(solution)/shard_map/ppermute | solution.py:494
  69.1 24.3 %all_to_all.10 = bf16[64,72,128]{2,1,0:T(8,128)(2,1)S(1)} all-to-all(bf16[64,72,128]{2,1,0:T(8,128)(2,1)S(1)} %pad_maximum_fusion), channel_id=1, replica_groups=mesh['row'=8,'colh'=8,'core'=2] {'row','colh'}, dimensions={0} | all-to-all | bytes 2359296 | tf_op jit(solution)/shard_map/all_to_all | solution.py:624
  93.8 22.9 %all_to_all.11.mine = bf16[64,72,128]{2,1,0:T(8,128)(2,1)S(1)} all-to-all(bf16[64,72,128]{2,1,0:T(8,128)(2,1)S(1)} %broadcast_in_dim.14), channel_id=1, replica_groups=mesh['row'=8,'colh'=8,'core'=2] {'row','colh'}, dimensions={0} | all-to-all | bytes 2359296 | tf_op jit(solution)/shard_map/all_to_all | solution.py:626
  116.7 2.9 %collective-permute-start.10 = (bf16[64,72,128]{2,1,0:T(8,128)(2,1)S(1)}, bf16[64,72,128]{2,1,0:T(8,128)(2,1)S(1)}, u32[]{:S(2)}, u32[]{:S(2)}) collective-permute-start(bf16[64,72,128]{2,1,0:T(8,128)(2,1)S(1)} %all_to_all.11.mine), channel_id=1, source_target_pairs={{0,1},{1,0},{2,3},{3,2},{4,5},{5,4},{6,7},{7,6},{8,9},{9,8},{10,11... | collective-permute-start | bytes 3538952 | tf_op jit(solution)/shard_map/ppermute | solution.py:494
  119.6 2.5 %collective-permute-done.10.other = bf16[64,72,128]{2,1,0:T(8,128)(2,1)S(1)} collective-permute-done((bf16[64,72,128]{2,1,0:T(8,128)(2,1)S(1)}, bf16[64,72,128]{2,1,0:T(8,128)(2,1)S(1)}, u32[]{:S(2)}, u32[]{:S(2)}) %collective-permute-start.10) | collective-permute-done | bytes 1179680 | tf_op jit(solution)/shard_map/ppermute | solution.py:494
  122.1 2.8 %shard_map.116 = (f32[27,64,192]{2,1,0:T(8,128)}, f32[27,128,128]{2,1,0:T(8,128)}, f32[27,64,64]{2,1,0:T(8,128)}, f32[27,64,128]{2,1,0:T(8,128)}) custom-call(bf16[64,72,128]{2,1,0:T(8,128)(2,1)S(1)} %all_to_all.11.mine, bf16[64,72,128]{2,1,0:T(8,128)(2,1)S(1)} %collective-permute-done.10.other), custom_call_target="tpu_custom_call" | custom-call | bytes 4000000 | tf_op jit(solution)/shard_map/pallas_call | solution.py:628
  (42 shorter events, 2.3 us)
Async XLA Ops:
  0.6 1.0 copy-start
  1.6 0.9 copy-start.1
  2.5 0.7 copy-start.5
  3.2 15.5 %copy-start.3 = (bf16[3,3,3,64,64]{4,3,2,1,0:T(8,128)(2,1)S(1)}, bf16[3,3,3,64,64]{4,3,2,1,0:T(8,128)(2,1)}, u32[]{:S(2)}) copy-start(bf16[3,3,3,64,64]{4,3,2,1,0:T(8,128)(2,1)} %param.9) | copy-start | bytes 663556
  3.2 15.5 %copy-start.4 = (bf16[3,3,3,64,128]{4,3,2,1,0:T(8,128)(2,1)S(1)}, bf16[3,3,3,64,128]{4,3,2,1,0:T(8,128)(2,1)}, u32[]{:S(2)}) copy-start(bf16[3,3,3,64,128]{4,3,2,1,0:T(8,128)(2,1)} %param.10) | copy-start | bytes 1327108
  3.9 7.6 %collective-permute-start = (bf16[528,128]{1,0:T(8,128)(2,1)S(1)}, bf16[528,128]{1,0:T(8,128)(2,1)S(1)}, u32[]{:S(2)}, u32[]{:S(2)}) collective-permute-start(bf16[528,128]{1,0:T(8,128)(2,1)S(1)} %get-tuple-element.39), channel_id=1, source_target_pairs={{0,16},{1,17},{2,18},{3,19},{4,20},{5,21},{6,22},{7,23},{8,24},{9,... | collective-permute-start | bytes 405512 | tf_op jit(solution)/shard_map/ppermute | solution.py:494
  6.4 6.0 %collective-permute-start.1 = (bf16[528,128]{1,0:T(8,128)(2,1)S(1)}, bf16[528,128]{1,0:T(8,128)(2,1)S(1)}, u32[]{:S(2)}, u32[]{:S(2)}) collective-permute-start(bf16[528,128]{1,0:T(8,128)(2,1)S(1)} %get-tuple-element.40), channel_id=1, source_target_pairs={{0,112},{1,113},{2,114},{3,115},{4,116},{5,117},{6,118},{7,119},{8... | collective-permute-start | bytes 405512 | tf_op jit(solution)/shard_map/ppermute | solution.py:494
  13.2 13.2 %collective-permute-start.2 = (bf16[768,128]{1,0:T(8,128)(2,1)S(1)}, bf16[768,128]{1,0:T(8,128)(2,1)S(1)}, u32[]{:S(2)}, u32[]{:S(2)}) collective-permute-start(bf16[768,128]{1,0:T(8,128)(2,1)S(1)} %get-tuple-element.43), channel_id=1, source_target_pairs={{0,1},{1,0},{2,3},{3,2},{4,5},{5,4},{6,7},{7,6},{8,9},{9,8},{10,11... | collective-permute-start | bytes 589832 | tf_op jit(solution)/shard_map/ppermute | solution.py:494
  15.4 11.0 %collective-permute-start.3 = (bf16[768,128]{1,0:T(8,128)(2,1)S(1)}, bf16[768,128]{1,0:T(8,128)(2,1)S(1)}, u32[]{:S(2)}, u32[]{:S(2)}) collective-permute-start(bf16[768,128]{1,0:T(8,128)(2,1)S(1)} %get-tuple-element.44), channel_id=1, source_target_pairs={{0,15},{1,2},{2,1},{3,4},{4,3},{5,6},{6,5},{7,8},{8,7},{9,10},{10,... | collective-permute-start | bytes 589832 | tf_op jit(solution)/shard_map/ppermute | solution.py:494
  23.0 0.9 copy-start.6
  23.9 0.8 copy-start.7
  24.7 0.8 copy-start.8
  25.6 0.8 copy-start.9
  41.9 0.8 copy-start.12
  42.7 0.7 copy-start.14
  43.4 10.7 %copy-start.2 = (bf16[3,384,384]{2,1,0:T(8,128)(2,1)S(1)}, bf16[3,384,384]{2,1,0:T(8,128)(2,1)}, u32[]{:S(2)}) copy-start(bf16[3,384,384]{2,1,0:T(8,128)(2,1)} %get-tuple-element.65.w6) | copy-start | bytes 2654212
  43.4 3.2 %collective-permute-start.5 = (bf16[2,64,128]{2,1,0:T(8,128)(2,1)S(1)}, bf16[2,64,128]{2,1,0:T(8,128)(2,1)S(1)}, u32[]{:S(2)}, u32[]{:S(2)}) collective-permute-start(bf16[2,64,128]{2,1,0:T(8,128)(2,1)S(1)} %get-tuple-element.80), channel_id=1, source_target_pairs={{0,16},{1,17},{2,18},{3,19},{4,20},{5,21},{6,22},{7,23},{8,24},{9,... | collective-permute-start | bytes 98312 | tf_op jit(solution)/shard_map/ppermute | solution.py:494
  43.7 4.9 %collective-permute-start.6 = (bf16[2,64,128]{2,1,0:T(8,128)(2,1)S(1)}, bf16[2,64,128]{2,1,0:T(8,128)(2,1)S(1)}, u32[]{:S(2)}, u32[]{:S(2)}) collective-permute-start(bf16[2,64,128]{2,1,0:T(8,128)(2,1)S(1)} %get-tuple-element.81), channel_id=1, source_target_pairs={{0,112},{1,113},{2,114},{3,115},{4,116},{5,117},{6,118},{7,119},{8... | collective-permute-start | bytes 98312 | tf_op jit(solution)/shard_map/ppermute | solution.py:494
  48.6 4.9 %collective-permute-start.8 = (bf16[8,16,128]{2,1,0:T(8,128)(2,1)S(1)}, bf16[8,16,128]{2,1,0:T(8,128)(2,1)S(1)}, u32[]{:S(2)}, u32[]{:S(2)}) collective-permute-start(bf16[8,16,128]{2,1,0:T(8,128)(2,1)S(1)} %broadcast_select_fusion.2), channel_id=1, source_target_pairs={{0,15},{1,2},{2,1},{3,4},{4,3},{5,6},{6,5},{7,8},{8,7},{9,10},{10,... | collective-permute-start | bytes 98312 | tf_op jit(solution)/shard_map/ppermute | solution.py:494
  51.8 2.3 %collective-permute-start.7 = (bf16[8,16,128]{2,1,0:T(8,128)(2,1)S(1)}, bf16[8,16,128]{2,1,0:T(8,128)(2,1)S(1)}, u32[]{:S(2)}, u32[]{:S(2)}) collective-permute-start(bf16[8,16,128]{2,1,0:T(8,128)(2,1)S(1)} %get-tuple-element.73), channel_id=1, source_target_pairs={{0,1},{1,0},{2,3},{3,2},{4,5},{5,4},{6,7},{7,6},{8,9},{9,8},{10,11... | collective-permute-start | bytes 98312 | tf_op jit(solution)/shard_map/ppermute | solution.py:494
  54.1 10.0 %copy-start.10 = (bf16[6,144,384]{2,1,0:T(8,128)(2,1)S(1)}, bf16[6,144,384]{2,1,0:T(8,128)(2,1)}, u32[]{:S(2)}) copy-start(bf16[6,144,384]{2,1,0:T(8,128)(2,1)} %get-tuple-element.53.s_lift) | copy-start | bytes 1990660
  54.1 10.0 %copy-start.11 = (bf16[6,144,384]{2,1,0:T(8,128)(2,1)S(1)}, bf16[6,144,384]{2,1,0:T(8,128)(2,1)}, u32[]{:S(2)}) copy-start(bf16[6,144,384]{2,1,0:T(8,128)(2,1)} %get-tuple-element.54.s_skip) | copy-start | bytes 1990660
  54.1 10.0 %copy-start.13 = (bf16[5,144,384]{2,1,0:T(8,128)(2,1)S(1)}, bf16[5,144,384]{2,1,0:T(8,128)(2,1)}, u32[]{:S(2)}) copy-start(bf16[5,144,384]{2,1,0:T(8,128)(2,1)} %copy-done.12) | copy-start | bytes 1658884
  54.1 10.0 %copy-start.15 = (bf16[6,64,384]{2,1,0:T(8,128)(2,1)S(1)}, bf16[6,64,384]{2,1,0:T(8,128)(2,1)}, u32[]{:S(2)}) copy-start(bf16[6,64,384]{2,1,0:T(8,128)(2,1)} %copy-done.14) | copy-start | bytes 884740
  58.0 8.5 %collective-permute-start.9 = (bf16[1536,128]{1,0:T(8,128)(2,1)S(1)}, bf16[1536,128]{1,0:T(8,128)(2,1)S(1)}, u32[]{:S(2)}, u32[]{:S(2)}) collective-permute-start(bf16[1536,128]{1,0:T(8,128)(2,1)S(1)} %get-tuple-element.68), channel_id=1, source_target_pairs={{0,1},{1,0},{2,3},{3,2},{4,5},{5,4},{6,7},{7,6},{8,9},{9,8},{10,11... | collective-permute-start | bytes 1179656 | tf_op jit(solution)/shard_map/ppermute | solution.py:494
  66.3 2.5 %collective-permute-start.4 = (bf16[3072,128]{1,0:T(8,128)(2,1)S(1)}, bf16[3072,128]{1,0:T(8,128)(2,1)S(1)}, u32[]{:S(2)}, u32[]{:S(2)}) collective-permute-start(bf16[3072,128]{1,0:T(8,128)(2,1)S(1)} %get-tuple-element.59), channel_id=1, source_target_pairs={{0,1},{1,0},{2,3},{3,2},{4,5},{5,4},{6,7},{7,6},{8,9},{9,8},{10,11... | collective-permute-start | bytes 2359304 | tf_op jit(solution)/shard_map/ppermute | solution.py:494
  116.7 5.4 %collective-permute-start.10 = (bf16[64,72,128]{2,1,0:T(8,128)(2,1)S(1)}, bf16[64,72,128]{2,1,0:T(8,128)(2,1)S(1)}, u32[]{:S(2)}, u32[]{:S(2)}) collective-permute-start(bf16[64,72,128]{2,1,0:T(8,128)(2,1)S(1)} %all_to_all.11.mine), channel_id=1, source_target_pairs={{0,1},{1,0},{2,3},{3,2},{4,5},{5,4},{6,7},{7,6},{8,9},{9,8},{10,11... | collective-permute-start | bytes 3538952 | tf_op jit(solution)/shard_map/ppermute | solution.py:494

commit v2 on v1

--- a/solution.py
+++ b/solution.py
@@ -10,22 +10,22 @@
 
 F32 = jnp.float32
 BF16 = jnp.bfloat16
-VMEM_LIMIT = 50 * 1024 * 1024
+MIB = 1024 * 1024
 VM = pl.BlockSpec(memory_space=pltpu.VMEM)
-SM = pl.BlockSpec(memory_space=pltpu.SMEM)
+HB = pl.BlockSpec(memory_space=pltpu.HBM)
 FACTOR = 1.0 / math.sqrt(64 * 256 * 8)
 CHUNK = 72
 ROWS_A, ROWS_B = 6144, 3072
 
 
-def call(kernel, outs, scratch=(), flops=0, n_scalar=0, n_in=0):
+def call(kernel, outs, ins, scratch=(), flops=0, limit=58):
     return pl.pallas_call(
         kernel,
-        out_shape=[jax.ShapeDtypeStruct(s, d) for s, d in outs],
-        in_specs=[SM] * n_scalar + [VM] * (n_in - n_scalar),
-        out_specs=[VM] * len(outs),
+        out_shape=[jax.ShapeDtypeStruct(o[0], o[1]) for o in outs],
+        in_specs=list(ins),
+        out_specs=[o[2] if len(o) > 2 else VM for o in outs],
         scratch_shapes=list(scratch),
-        compiler_params=pltpu.CompilerParams(vmem_limit_bytes=VMEM_LIMIT),
+        compiler_params=pltpu.CompilerParams(vmem_limit_bytes=int(limit * MIB)),
         cost_estimate=pl.CostEstimate(flops=flops, bytes_accessed=4_000_000, transcendentals=0),
     )
 
@@ -93,9 +93,15 @@
 
 
 def silu_parts(v):
-    sigma = jax.nn.sigmoid(v)
+    sigma = 0.5 * jnp.tanh(0.5 * v) + 0.5
     act = v * sigma
-    return act, sigma + act * (1.0 - sigma)
+    return act, lambda: sigma + act * (1.0 - sigma)
+
+
+W1, W2, W3, W4L, W4E, W5L, W5S, WF = 0, 768, 1344, 2496, 4032, 4800, 6336, 7104
+W6, W7, WB = 0, 1152, 2304
+LIFT, SKIP, GRAD, COARSE, KEPT = 0, 864, 1728, 2448, 2832
+ROOM = 51200
 
 
 def place(axis):
@@ -108,25 +114,29 @@
     return jnp.concatenate([first.astype(F32), second.astype(F32)], axis=1)
 
 
-def pack_x(active, feat, cot, p1, p2):
+def pack_x(active_hbm, feat_hbm, cot_hbm, p1, p2, active, feat, cot, sem):
+    odd, _, _ = place(0)
+    copies = [pltpu.make_async_copy(active_hbm, active, sem.at[0])]
+    copies += [pltpu.make_async_copy(feat_hbm.at[k], feat.at[k], sem.at[1 + k]) for k in range(8)]
+    copies += [pltpu.make_async_copy(cot_hbm.at[7 * k], cot.at[k], sem.at[9 + k]) for k in range(2)]
+    for copy in copies:
+        copy.start()
+    for copy in copies:
+        copy.wait()
     row = lax.broadcasted_iota(jnp.int32, (128, 64), 0)
     mask = jnp.where(row < 64, active[0], active[1]).astype(F32)
     row = lax.broadcasted_iota(jnp.int32, (16, 128), 0)
     ends = jnp.where(row < 8, active[0], active[1]).astype(F32).astype(BF16)
-    odd, _, _ = place(0)
     for k in range(3):
         pair = beside(feat[2 * k + 1].astype(F32) * mask, feat[2 * k + 2].astype(F32) * mask).astype(BF16)
         p1[128 * k : 128 * k + 128] = pair
         p2[128 * k : 128 * k + 128] = pair
-    for p, edge in ((p1, jnp.where(odd, 0, 7)), (p2, jnp.where(odd, 7, 0))):
-        p[384:512] = beside(feat[edge].astype(F32) * mask, cot[edge]).astype(BF16)
+    for p, edge in ((p1, jnp.where(odd, 0, 1)), (p2, jnp.where(odd, 1, 0))):
+        p[384:512] = beside(feat[7 * edge].astype(F32) * mask, cot[edge]).astype(BF16)
         p[512:528] = ends
 
 
-def pack_y(active, feat, cot, rz, rxz, xall, xmask, p3, p4):
-    row = lax.broadcasted_iota(jnp.int32, (128, 64), 0)
-    mask = jnp.where(row < 64, active[0], active[1]).astype(F32)
-    row = lax.broadcasted_iota(jnp.int32, (16, 128), 0)
+def pack_y(cot, p1, p2, rz, rxz, xall, xmask, p3, p4):
     odd, v_lo, v_hi = place(0)
 
     def lo(rows):
@@ -134,23 +144,23 @@
 
     def hi(rows):
         return jnp.where(odd, rxz[rows].astype(F32), rz[rows].astype(F32)) * v_hi
-
-    def own(k):
-        return feat[k].astype(F32) * mask
 
     for k in range(3):
         slab = slice(128 * k, 128 * k + 128)
         xall[k] = lo(slab).astype(BF16)
-        xall[4 + k] = beside(own(2 * k + 1), own(2 * k + 2)).astype(BF16)
+        xall[4 + k] = p1[slab]
         xall[8 + k] = hi(slab).astype(BF16)
         xall[12 + k] = beside(cot[2 * k + 1], cot[2 * k + 2]).astype(BF16)
-    edge_lo, edge_hi = lo(slice(384, 512)), hi(slice(384, 512))
-    xall[3] = beside(edge_lo[:, :64], own(0)).astype(BF16)
-    xall[7] = beside(own(7), edge_hi[:, :64]).astype(BF16)
-    xall[11] = beside(edge_lo[:, 64:], cot[0]).astype(BF16)
-    xall[15] = beside(cot[7], edge_hi[:, 64:]).astype(BF16)
+    slab = slice(384, 512)
+    edge_lo, edge_hi = lo(slab), hi(slab)
+    first = jnp.where(odd, p1[slab].astype(F32), p2[slab].astype(F32))
+    last = jnp.where(odd, p2[slab].astype(F32), p1[slab].astype(F32))
+    xall[3] = beside(edge_lo[:, :64], first[:, :64]).astype(BF16)
+    xall[7] = beside(last[:, :64], edge_hi[:, :64]).astype(BF16)
+    xall[11] = beside(edge_lo[:, 64:], first[:, 64:]).astype(BF16)
+    xall[15] = beside(last[:, 64:], edge_hi[:, 64:]).astype(BF16)
     xmask[0] = lo(slice(512, 528))
-    xmask[1] = jnp.where(row < 8, active[0], active[1]).astype(F32)
+    xmask[1] = p1[512:528].astype(F32)
     xmask[2] = hi(slice(512, 528))
     odd_c, _, _ = place(1)
     for p, low in ((p3, odd_c), (p4, jnp.logical_not(odd_c))):
@@ -167,10 +177,23 @@
 
 
 def forward(
-    xall, xmask, r3, r4, w1, w2, w3, w4l, w4e, w5l, w5s,
-    decoded, slope_ef, g_skip, slope_ec, g_dc, s_in, s_pool, s_ec, s_lift, s_skip, gz,
-    mm, cc, s1, ee, s2, s3, slope_dc, s4, acc,
+    xall, xmask, r3, r4, weights_hbm,
+    decoded_hbm, slope_ef, g_skip, slope_ec, g_dc, s_in, s_pool, kept_hbm,
+    mm, cc, s1, ee, s2, s3, slope_dc, s4, acc, acc1, weights, kept, decoded, w_sem, out_sem,
 ):
+    cuts = (W1, W2, W3, W4L, W4E, W5L, W5S, WF)
+    loads = []
+    for k in range(7):
+        rows = pl.ds(cuts[k], cuts[k + 1] - cuts[k])
+        loads.append(pltpu.make_async_copy(weights_hbm.at[rows], weights.at[rows], w_sem.at[k]))
+        loads[-1].start()
+    stores = []
+
+    def store(first, end):
+        rows = pl.ds(first, end - first)
+        stores.append(pltpu.make_async_copy(kept.at[rows], kept_hbm.at[rows], out_sem.at[len(stores)]))
+        stores[-1].start()
+
     odd, v_lo, v_hi = place(1)
 
     def lo(at, rows):
@@ -205,8 +228,17 @@
 
     lax.fori_loop(0, 11, spread, 0)
 
+    loads[0].wait()
+
+    def encode_dots(i, _):
+        wide = jnp.concatenate([s1[pl.ds(5 * i, 5)], s1[pl.ds(5 * i + 1, 5)]], axis=2)
+        acc1[pl.ds(pl.multiple_of(1120 * i, 1120), 1120)] = dot(wide.reshape(1120, 768), weights[W1:W2])
+        return 0
+
+    lax.fori_loop(0, 2, encode_dots, 0)
+
     def encode(i, _):
-        pre = fold128(dot(jnp.concatenate([s1[i], s1[i + 1]], axis=1), w1[...]))
+        pre = fold128(acc1[pl.ds(pl.multiple_of(224 * i, 224), 224)])
         mask = mm[jnp.where(i < 3, 0, jnp.where(i < 7, 1, 2))]
         act, slope = silu_parts(pre)
         v = bround(act * mask)
@@ -214,7 +246,7 @@
 
         @pl.when(jnp.logical_and(i >= 3, i < 7))
         def _():
-            slope_ef[i - 3] = (slope * mask)[6:22].reshape(128, 128)
+            slope_ef[i - 3] = (slope() * mask)[6:22].reshape(128, 128)
 
         s = v.reshape(14, 2, 8, 128)
         s = s[:, 0] + s[:, 1]
@@ -234,10 +266,12 @@
         m = mm[block].reshape(14, 2, 8, 128)[first : first + count, 0]
         return jnp.where(z_of(m.shape) < 4, m, 0.0)
 
+    loads[1].wait()
+
     def encode2(i, _):
         pre = jnp.zeros((384, 384), F32)
         for a in range(3):
-            pre += dot(s2[pl.ds(4 * i + a, 4)].reshape(384, 192), w2[a])
+            pre += dot(s2[pl.ds(4 * i + a, 4)].reshape(384, 192), weights[W2 + 192 * a : W2 + 192 * a + 192])
         pre = fold128(pre).reshape(4, 12, 8, 128)
         for k in range(4):
             x = 4 * i + k
@@ -248,17 +282,19 @@
 
             @pl.when(jnp.logical_and(x >= 1, x < 7))
             def _():
-                slope_ec[x - 1] = (slope * mask)[1:11].reshape(80, 128)
-                s_ec[x - 1] = taps_y(v[1:11], 8)
+                slope_ec[x - 1] = (slope() * mask)[1:11].reshape(80, 128)
+                kept[pl.ds(pl.multiple_of(COARSE + 64 * (x - 1), 64), 64)] = taps_y(v[1:11], 8)
 
         return 0
 
     lax.fori_loop(0, 2, encode2, 0)
+    store(COARSE, KEPT)
+    loads[2].wait()
 
     def decode2(i, _):
         pre = jnp.zeros((240, 384), F32)
         for a in range(3):
-            pre += dot(s3[pl.ds(3 * i + a, 3)].reshape(240, 384), w3[a])
+            pre += dot(s3[pl.ds(3 * i + a, 3)].reshape(240, 384), weights[W3 + 384 * a : W3 + 384 * a + 384])
         pre = fold128(pre).reshape(3, 10, 8, 128)
         for k in range(3):
             x = 3 * i + k
@@ -266,25 +302,33 @@
             act, slope = silu_parts(pre[k])
             v = double_z(bround(act * mask))
             up = jnp.concatenate([v[:, None], v[:, None]], axis=1).reshape(20, 8, 128)
-            s_lift[x] = taps_y(up, 18)
+            kept[pl.ds(pl.multiple_of(LIFT + 144 * x, 144), 144)] = taps_y(up, 18)
 
             @pl.when(jnp.logical_and(x >= 1, x < 5))
             def _():
-                slope_dc[x - 1] = (slope * mask)[1:9]
+                slope_dc[x - 1] = (slope() * mask)[1:9]
 
         return 0
 
     lax.fori_loop(0, 2, decode2, 0)
 
     def skip(i, _):
-        s_skip[i] = taps_y(ee[i + 2, 4:24], 18)
+        kept[pl.ds(pl.multiple_of(SKIP + 144 * i, 144), 144)] = taps_y(ee[i + 2, 4:24], 18)
         return 0
 
     lax.fori_loop(0, 6, skip, 0)
 
-    first, second = s_lift[0:5].reshape(720, 384), s_lift[1:6].reshape(720, 384)
-    acc[...] = dot_n(first, w4l[0]) + dot_n(first, w4l[1]) + dot_n(second, w4l[2]) + dot_n(second, w4l[3])
-    acc[...] += dot_n(s_skip[0:5].reshape(720, 384), w4e[0]) + dot_n(s_skip[1:6].reshape(720, 384), w4e[1])
+    store(LIFT, GRAD)
+    loads[3].wait()
+    loads[4].wait()
+    total = jnp.zeros((720, 384), F32)
+    for p in range(2):
+        for q in range(2):
+            at = W4L + 384 * (2 * p + q)
+            total += dot_n(kept[LIFT + 144 * p : LIFT + 144 * p + 720], weights[at : at + 384])
+        at = W4E + 384 * p
+        total += dot_n(kept[SKIP + 144 * p : SKIP + 144 * p + 720], weights[at : at + 384])
+    acc[...] = total
 
     def decode(i, _):
         pre = fold128(acc[pl.ds(pl.multiple_of(144 * i, 144), 144)])
@@ -292,7 +336,7 @@
         before, after = jnp.where(i < 1, 0, 1), jnp.where(i < 4, 1, 2)
         mask = jnp.where(lane < 64, mm[before, 5:23], mm[after, 5:23])
         act, slope = silu_parts(pre)
-        g = bround(cc[i] * mask * slope)
+        g = bround(cc[i] * mask * slope())
         s4[i] = taps_y(g, 16)
         out = (act * mask)[1:17].reshape(128, 128).astype(BF16)
 
@@ -307,21 +351,31 @@
         own = jnp.logical_and(jnp.logical_or(lane >= 64, i > 0), jnp.logical_or(lane < 64, i < 4))
         g = jnp.where(own, g, 0.0)
         zero = jnp.zeros((1, 8, 128), F32)
-        gz[i] = taps_z(jnp.concatenate([zero, g[1:17], zero], axis=0))
+        kept[pl.ds(pl.multiple_of(GRAD + 144 * i, 144), 144)] = taps_z(
+            jnp.concatenate([zero, g[1:17], zero], axis=0)
+        )
         return 0
 
     lax.fori_loop(0, 5, decode, 0)
+    store(GRAD, COARSE)
+    stores.append(pltpu.make_async_copy(decoded, decoded_hbm, out_sem.at[3]))
+    stores[-1].start()
+    loads[5].wait()
+    loads[6].wait()
 
     def back(i, _):
         wide = jnp.concatenate([s4[pl.ds(2 * i, 2)], s4[pl.ds(2 * i + 1, 2)]], axis=2).reshape(256, 768)
-        g_skip[pl.ds(2 * i, 2)] = fold128(dot(wide, w5s[...])).reshape(2, 128, 128)
-        up = (dot(wide, w5l[0]) + dot(wide, w5l[1])).reshape(16, 2, 8, 384)
+        g_skip[pl.ds(2 * i, 2)] = fold128(dot(wide, weights[W5S:WF])).reshape(2, 128, 128)
+        up = dot(wide, weights[W5L : W5L + 768]) + dot(wide, weights[W5L + 768 : W5S])
+        up = up.reshape(16, 2, 8, 384)
         g = halve_z(fold128((up[:, 0] + up[:, 1]).reshape(128, 384)))
         g = g.reshape(2, 8, 8, 128) * slope_dc[pl.ds(2 * i, 2)]
         g_dc[pl.ds(2 * i, 2)] = g.reshape(2, 64, 128).astype(BF16)
         return 0
 
     lax.fori_loop(0, 2, back, 0)
+    for copy in stores:
+        copy.wait()
 
 
 def unhalve(both):
@@ -339,12 +393,20 @@
 B_FINE2, B_COARSE, B_END = 576, 864, 2592
 
 
-def weights_decode(s_lift, s_skip, gz, s_ec, g_dc, keep, send, wire):
-    grad = gz[...].reshape(720, 384)
+def weights_decode(kept_hbm, g_dc, keep, send, wire, kept, sem):
+    copies = []
+    cuts = (LIFT, SKIP, GRAD, COARSE, KEPT)
+    for k in range(4):
+        rows = pl.ds(cuts[k], cuts[k + 1] - cuts[k])
+        copies.append(pltpu.make_async_copy(kept_hbm.at[rows], kept.at[rows], sem.at[k]))
+        copies[-1].start()
+    for copy in copies:
+        copy.wait()
+    grad = kept[GRAD:COARSE]
     gc = taps_z(g_dc[...].astype(F32).reshape(32, 8, 128))
     wire[A_END:] = jnp.zeros((wire.shape[0] - A_END, 128), BF16)
-    up = [(dot_t(grad, s_lift[p : p + 5].reshape(720, 384)) * FACTOR).reshape(3, 2, 64, 384) for p in range(2)]
-    same = [(dot_t(grad, s_skip[p : p + 5].reshape(720, 384)) * FACTOR).reshape(3, 2, 64, 384) for p in range(2)]
+    up = [(dot_t(grad, kept[LIFT + 144 * p : LIFT + 144 * p + 720]) * FACTOR).reshape(3, 2, 64, 384) for p in range(2)]
+    same = [(dot_t(grad, kept[SKIP + 144 * p : SKIP + 144 * p + 720]) * FACTOR).reshape(3, 2, 64, 384) for p in range(2)]
     for a, (p, q) in enumerate(((0, 0), (0, 1), (1, 0))):
         p2, q2 = (0, 1) if a == 0 else (1, a - 1)
         lifted = (up[p][:, 0] + up[p2][:, 1]).reshape(192, 384).astype(BF16)
@@ -356,7 +418,7 @@
             lanes = slice(128 * b, 128 * b + 128)
             taps.append(add_halves(same[p][:, 0, :, lanes].reshape(192, 128), q, same[p2][:, 1, :, lanes].reshape(192, 128), q2))
         put_three(wire, A_SKIP + 192 * a, A_SKIP2 + 96 * a, taps)
-        res = (dot_t(s_ec[a : a + 4].reshape(256, 384), gc) * FACTOR).astype(BF16)
+        res = (dot_t(kept[COARSE + 64 * a : COARSE + 64 * a + 256], gc) * FACTOR).astype(BF16)
         for b in range(3):
             for c in range(3):
                 at = A_COARSE + 128 * (9 * a + 3 * b + c)
@@ -376,7 +438,7 @@
     wire[at2 : at2 + 96] = jnp.where(lane[:96] < 64, taps[2][0][:96], taps[2][1][96:]).astype(BF16)
 
 
-def back_encode(gx, slope_ec, s_pool, s_in, g_skip, slope_ef, w6, w7, keep, send, s5, ge, gz, wire):
+def back_encode(gx, slope_ec, s_pool, s_in, g_skip, slope_ef, weights, keep, send, s5, ge, gz, wire):
     def spread(x, _):
         s5[x] = taps_y(gx[x].astype(F32).reshape(12, 8, 128), 10)
         return 0
@@ -384,14 +446,14 @@
     lax.fori_loop(0, 8, spread, 0)
     acc = jnp.zeros((480, 384), F32)
     for a in range(3):
-        acc += dot_n(s5[a : a + 6].reshape(480, 384), w6[a])
+        acc += dot_n(s5[a : a + 6].reshape(480, 384), weights[W6 + 384 * a : W6 + 384 * a + 384])
     g_ec = bround(fold128(acc) * slope_ec[...].reshape(60, 8, 128)).reshape(6, 10, 8, 128)
     for x in range(6):
         ge[x] = taps_y(g_ec[x], 8)
     gc = taps_z(g_ec[1:5, 1:9].reshape(32, 8, 128))
     acc = jnp.zeros((256, 384), F32)
     for a in range(3):
-        acc += dot_n(ge[a : a + 4].reshape(256, 384), w7[a])
+        acc += dot_n(ge[a : a + 4].reshape(256, 384), weights[W7 + 384 * a : W7 + 384 * a + 384])
     up = double_z(fold128(acc) * 0.125)
     up = jnp.concatenate([up[:, None], up[:, None]], axis=1).reshape(4, 16, 8, 128)
     for x in range(4):
@@ -415,7 +477,7 @@
     split_wire(wire, keep, send)
 
 
-def unpack(mine, other, d_df, d_dc, d_ef, d_ec, wire_a, wire_b):
+def unpack(mine, other, df_hbm, dc_hbm, ef_hbm, ec_hbm, wire_a, wire_b, d_df, d_dc, d_ef, d_ec, sem):
     core = lax.axis_index("core")
     for wire, first in ((wire_a, 0), (wire_b, ROWS_A // 128)):
         rows = wire.shape[0] // 2
@@ -424,9 +486,19 @@
         there = pl.ds(pl.multiple_of((1 - core) * rows, rows), rows)
         wire[here] = mine[:, first : first + each].reshape(rows, 128)
         wire[there] = other[:, first : first + each].reshape(rows, 128)
-    d_dc[...] = wire_a[A_COARSE:A_END].astype(F32).reshape(27, 128, 128)
-    d_ec[...] = wire_b[B_COARSE:B_END].astype(F32).reshape(27, 64, 128)
+    stores = []
+
+    def store(src, dst, rows):
+        stores.append(pltpu.make_async_copy(src.at[rows], dst.at[rows], sem.at[len(stores)]))
+        stores[-1].start()
+
     for a in range(3):
+        taps = pl.ds(9 * a, 9)
+        first = A_COARSE + 1152 * a
+        d_dc[taps] = wire_a[first : first + 1152].astype(F32).reshape(9, 128, 128)
+        store(d_dc, dc_hbm, taps)
+    for a in range(3):
+        taps = pl.ds(9 * a, 9)
         two = wire_a[A_SKIP + 192 * a : A_SKIP + 192 * a + 192].astype(F32)
         three = unhalve(wire_a[A_SKIP2 + 96 * a : A_SKIP2 + 96 * a + 96].astype(F32))
         skip = (two[:, :64], two[:, 64:], three)
@@ -439,20 +511,28 @@
                 d_df[k, :, :128] = wire_a[64 * k : 64 * k + 64].astype(F32)
                 d_df[k, :, 128:] = skip[b][64 * c : 64 * c + 64]
                 d_ef[k] = fine[c][64 * b : 64 * b + 64]
-
-
-def arrange(e1, e2, d3, d4, w1, w2, w3, w4l, w4e, w5l, w5s, w6, w7):
+        store(d_df, df_hbm, taps)
+        store(d_ef, ef_hbm, taps)
+        first = B_COARSE + 576 * a
+        d_ec[taps] = wire_b[first : first + 576].astype(F32).reshape(9, 64, 128)
+        store(d_ec, ec_hbm, taps)
+    for copy in stores:
+        copy.wait()
+
+
+def arrange(e1, e2, d3, d4, wf_hbm, wb, wf, sem):
     for a in range(3):
         for b in range(3):
-            fine, coarse = slice(64 * b, 64 * b + 64), slice(128 * b, 128 * b + 128)
+            coarse = slice(128 * b, 128 * b + 128)
             for c in range(3):
                 k = 9 * a + 3 * b + c
                 lanes = slice(128 * c, 128 * c + 128)
-                w2[a, fine, lanes] = e2[k]
-                w3[a, coarse, lanes] = d3[k]
-                w6[a, lanes, coarse] = d3[26 - k]
-                w7[a, 128 * c : 128 * c + 64, coarse] = e2[26 - k]
-                w7[a, 128 * c + 64 : 128 * c + 128, coarse] = e2[26 - k]
+                wf[W2 + 192 * a + 64 * b : W2 + 192 * a + 64 * b + 64, lanes] = e2[k]
+                wf[W3 + 384 * a + 128 * b : W3 + 384 * a + 128 * b + 128, lanes] = d3[k]
+                at = 384 * a + 128 * c
+                wb[W6 + at : W6 + at + 128, coarse] = d3[26 - k]
+                wb[W7 + at : W7 + at + 64, coarse] = e2[26 - k]
+                wb[W7 + at + 64 : W7 + at + 128, coarse] = e2[26 - k]
     none = jnp.zeros((64, 64), F32)
 
     def tap(ref, a, rest, lanes, turned=False):
@@ -468,26 +548,35 @@
                 rest = 3 * b + c
                 lanes = slice(128 * c, 128 * c + 128)
                 for q in range(2):
-                    rows = slice(384 * p + 128 * b + 64 * q, 384 * p + 128 * b + 64 * q + 64)
+                    at = 384 * p + 128 * b + 64 * q
                     a = 2 * p + q
-                    w1[rows, lanes] = beside(tap(e1, a, rest, all_), tap(e1, a - 1, rest, all_)).astype(BF16)
-                    w5s[rows, lanes] = beside(
+                    wf[W1 + at : W1 + at + 64, lanes] = beside(tap(e1, a, rest, all_), tap(e1, a - 1, rest, all_)).astype(BF16)
+                    wf[W5S + at : W5S + at + 64, lanes] = beside(
                         tap(d4, a, rest, high, True), tap(d4, a - 1, rest, high, True)
                     ).astype(BF16)
                     for o in range(2):
-                        cols = slice(128 * c + 64 * o, 128 * c + 64 * o + 64)
+                        to = W5L + 768 * o + at
+                        to2 = W4L + 384 * (2 * p + q) + 128 * c + 64 * o
                         coarse = slice(128 * b, 128 * b + 128)
                         if 0 <= a - o <= 2:
-                            w5l[o, rows, lanes] = d4[26 - 9 * (a - o) - rest, :, low]
-                            w4l[2 * p + q, cols, coarse] = d4[9 * (a - o) + rest, :, low]
+                            wf[to : to + 64, lanes] = d4[26 - 9 * (a - o) - rest, :, low]
+                            wf[to2 : to2 + 64, coarse] = d4[9 * (a - o) + rest, :, low]
                         else:
-                            w5l[o, rows, lanes] = jnp.zeros((64, 128), BF16)
-                            w4l[2 * p + q, cols, coarse] = jnp.zeros((64, 128), BF16)
+                            wf[to : to + 64, lanes] = jnp.zeros((64, 128), BF16)
+                            wf[to2 : to2 + 64, coarse] = jnp.zeros((64, 128), BF16)
                 for o in range(2):
-                    cols = slice(128 * c + 64 * o, 128 * c + 64 * o + 64)
-                    w4e[p, cols, 128 * b : 128 * b + 128] = beside(
+                    at = W4E + 384 * p + 128 * c + 64 * o
+                    wf[at : at + 64, 128 * b : 128 * b + 128] = beside(
                         tap(d4, 2 * p - o, rest, high), tap(d4, 2 * p + 1 - o, rest, high)
                     ).astype(BF16)
+    cuts = (W1, W2, W3, W4L, W4E, W5L, W5S, WF)
+    copies = []
+    for k in range(7):
+        rows = pl.ds(cuts[k], cuts[k + 1] - cuts[k])
+        copies.append(pltpu.make_async_copy(wf.at[rows], wf_hbm.at[rows], sem.at[k]))
+        copies[-1].start()
+    for copy in copies:
+        copy.wait()
 
 
 def swap(v, pairs):
@@ -512,20 +601,11 @@
 
     odd_r, odd_c = row % 2, core
     active = block_active.reshape(2)
-    w1, w2, w3, w4l, w4e, w5l, w5s, w6, w7 = call(
+    w_forward, w_backward = call(
         arrange,
-        [
-            ((768, 384), BF16),
-            ((3, 192, 384), BF16),
-            ((3, 384, 384), BF16),
-            ((4, 384, 384), BF16),
-            ((2, 384, 384), BF16),
-            ((2, 768, 384), BF16),
-            ((768, 384), BF16),
-            ((3, 384, 384), BF16),
-            ((3, 384, 384), BF16),
-        ],
-        n_in=4,
+        [((ROOM, 384), BF16, HB), ((WB, 384), BF16)],
+        [VM] * 4,
+        scratch=[pltpu.VMEM((WF, 384), BF16), pltpu.SemaphoreType.DMA((7,))],
     )(
         encode_fine.reshape(27, 64, 64),
         encode_coarse.reshape(27, 64, 128),
@@ -535,31 +615,40 @@
 
     feat = features.reshape(8, 128, 64)
     cot = out_cotangent.reshape(8, 128, 64)
-    p1, p2 = call(pack_x, [((528, 128), BF16)] * 2, n_in=3, n_scalar=1)(active, feat, cot)
+    p1, p2 = call(
+        pack_x,
+        [((528, 128), BF16)] * 2,
+        [HB] * 3,
+        scratch=[
+            pltpu.SMEM((2,), jnp.int32),
+            pltpu.VMEM((8, 128, 64), BF16),
+            pltpu.VMEM((2, 128, 64), BF16),
+            pltpu.SemaphoreType.DMA((11,)),
+        ],
+    )(active, feat, cot)
     rz, rxz = swap(p1, swap_z), swap(p2, swap_xz)
+    rz, w_forward, w_backward = lax.optimization_barrier((rz, w_forward, w_backward))
     xall, xmask, p3, p4 = call(
         pack_y,
         [((16, 128, 128), BF16), ((3, 16, 128), F32), ((768, 128), BF16), ((768, 128), BF16)],
-        n_in=5,
-        n_scalar=1,
-    )(active, feat, cot, rz, rxz)
+        [VM] * 5,
+        limit=8,
+    )(cot, p1, p2, rz, rxz)
     r3, r4 = swap(p3, swap_core), swap(p4, swap_yz)
 
-    decoded, slope_ef, g_skip, slope_ec, g_dc, s_in, s_pool, s_ec, s_lift, s_skip, gz = call(
+    decoded, slope_ef, g_skip, slope_ec, g_dc, s_in, s_pool, kept = call(
         forward,
         [
-            ((8, 128, 64), BF16),
+            ((8, 128, 64), BF16, HB),
             ((4, 128, 128), F32),
             ((4, 128, 128), F32),
             ((6, 80, 128), F32),
             ((4, 64, 128), BF16),
             ((5, 128, 384), BF16),
             ((6, 64, 192), BF16),
-            ((6, 64, 384), BF16),
-            ((6, 144, 384), BF16),
-            ((6, 144, 384), BF16),
-            ((5, 144, 384), BF16),
+            ((ROOM, 384), BF16, HB),
         ],
+        [VM] * 4 + [HB],
         scratch=[
             pltpu.VMEM((3, 28, 8, 128), F32),
             pltpu.VMEM((5, 18, 8, 128), F32),
@@ -570,10 +659,16 @@
             pltpu.VMEM((4, 8, 8, 128), F32),
             pltpu.VMEM((5, 128, 384), BF16),
             pltpu.VMEM((720, 384), F32),
+            pltpu.VMEM((2240, 384), F32),
+            pltpu.VMEM((WF, 384), BF16),
+            pltpu.VMEM((KEPT, 384), BF16),
+            pltpu.VMEM((8, 128, 64), BF16),
+            pltpu.SemaphoreType.DMA((7,)),
+            pltpu.SemaphoreType.DMA((4,)),
         ],
-        n_in=11,
         flops=4_000_000_000,
-    )(xall, xmask, r3, r4, w1, w2, w3, w4l, w4e, w5l, w5s)
+        limit=26,
+    )(xall, xmask, r3, r4, w_forward)
 
     is_odd = odd_r == 1
     q1 = swap(jnp.where(is_odd, g_dc[:2], g_dc[2:]), swap_z)
@@ -593,24 +688,31 @@
     keep_a, send_a = call(
         weights_decode,
         [((ROWS_A // 2, 128), BF16)] * 2,
-        scratch=[pltpu.VMEM((ROWS_A, 128), BF16)],
-        n_in=5,
+        [HB, VM],
+        scratch=[
+            pltpu.VMEM((ROWS_A, 128), BF16),
+            pltpu.VMEM((KEPT, 384), BF16),
+            pltpu.SemaphoreType.DMA((4,)),
+        ],
         flops=1_000_000_000,
-    )(s_lift, s_skip, gz, s_ec, g_dc)
+        limit=26,
+    )(kept, g_dc)
     got_a = swap(send_a, swap_core)
+    gx, keep_a = lax.optimization_barrier((gx, keep_a))
 
     keep_b, send_b = call(
         back_encode,
         [((ROWS_B // 2, 128), BF16)] * 2,
+        [VM] * 7,
         scratch=[
             pltpu.VMEM((8, 80, 384), BF16),
             pltpu.VMEM((6, 64, 384), BF16),
             pltpu.VMEM((4, 128, 384), BF16),
             pltpu.VMEM((ROWS_B, 128), BF16),
         ],
-        n_in=8,
         flops=500_000_000,
-    )(gx, slope_ec, s_pool, s_in, g_skip, slope_ef, w6, w7)
+        limit=20,
+    )(gx, slope_ec, s_pool, s_in, g_skip, slope_ef, w_backward)
     got_b = swap(send_b, swap_core)
 
     chips = ("row", "colh")
@@ -625,11 +727,15 @@
     total = jnp.sum(terms.astype(F32), axis=0).astype(BF16)
     mine = lax.all_to_all(jnp.broadcast_to(total[None], (64, CHUNK, 128)), chips, 0, 0, tiled=True)
     other = swap(mine, swap_core)
+    shapes = ((27, 64, 192), (27, 128, 128), (27, 64, 64), (27, 64, 128))
     d_df, d_dc, d_ef, d_ec = call(
         unpack,
-        [((27, 64, 192), F32), ((27, 128, 128), F32), ((27, 64, 64), F32), ((27, 64, 128), F32)],
-        scratch=[pltpu.VMEM((ROWS_A, 128), BF16), pltpu.VMEM((ROWS_B, 128), BF16)],
-        n_in=2,
+        [(shape, F32, HB) for shape in shapes],
+        [VM] * 2,
+        scratch=[pltpu.VMEM((ROWS_A, 128), BF16), pltpu.VMEM((ROWS_B, 128), BF16)]
+        + [pltpu.VMEM(shape, F32) for shape in shapes]
+        + [pltpu.SemaphoreType.DMA((12,))],
+        limit=24,
     )(mine, other)
     return (
         decoded.reshape(8, 16, 8, 64),

time: 125 us -> 115 us (0.920)
  local copies, waits for them, and re-layouts: 7.63 us -> 0.17 us
  starting transfers between devices: 27.4 us -> 21.5 us
  waiting for transfers between devices: 11.1 us -> 13 us
    unnamed x32 -> x8, local copies, waits for them, and re-layouts: 7.48 us -> 0.02 us
    ppermute x11, starting transfers between devices: 27.4 us -> 21.5 us  [swap(): return lax.ppermute(v, ('row', 'colh', 'core'), pairs)]
    ppermute x11, waiting for transfers between devices: 11.1 us -> 13 us  [swap(): return lax.ppermute(v, ('row', 'colh', 'core'), pairs)]
  transfers between devices with their start and end apart: 11 -> 11, of which waited for: 7 -> 6; matrix products, arithmetic and copies ran while one was open for 0% -> 0% of each run, Pallas kernels for 5% -> 9%
where the time goes in v2:
time: 115 us
  blocking collectives  48 us (42%)
  Pallas kernels  30.8 us (27%)
  starting transfers between devices  21.5 us (19%)
  waiting for transfers between devices  13 us (11%)
    all_to_all x1, blocking collectives, body(): terms = lax.all_to_all(half, chips, 0, 0, tiled=True)  25.1 us
    all_to_all x1, blocking collectives, body(): lax.all_to_all(jnp.broadcast_to(total[None], (64, CHUNK, 128)), chips, 0,...  22.9 us
    ppermute x11, starting transfers between devices, swap(): return lax.ppermute(v, ('row', 'colh', 'core'), pairs)  21.5 us
    ppermute x11, waiting for transfers between devices, swap(): return lax.ppermute(v, ('row', 'colh', 'core'), pairs)  13 us
    pallas_call x1, Pallas kernels, body(): call(forward, [((8, 128, 64), BF16, HB), ((4, 128, 128), F32), ((4, 128,...  12.8 us
    pallas_call x1, Pallas kernels, body(): call(arrange, [((ROOM, 384), BF16, HB), ((WB, 384), BF16)], [VM] * 4, scr...  6.66 us
    pallas_call x1, Pallas kernels, body(): call(weights_decode, [((ROWS_A // 2, 128), BF16)] * 2, [HB, VM], scratch=...  3.79 us
    pallas_call x1, Pallas kernels, body(): call(unpack, [(shape, F32, HB) for shape in shapes], [VM] * 2, scratch=[p...  2.83 us
  transfers between devices with their start and end apart: 11, of which 6 were waited for; matrix products, arithmetic and copies ran while one was open for 0% of the time, Pallas kernels for 9%

profile of v2, /device:TPU:1, one launch (start us, length us, event | category | flops | bytes accessed | tf_op | source)
XLA Modules:
  0.0 115.2 jit_solution(3761930521121242947)
XLA Ops:
  0.6 1.9 %shard_map.110 = (bf16[528,128]{1,0:T(8,128)(2,1)}, bf16[528,128]{1,0:T(8,128)(2,1)}) custom-call(s32[2]{0:T(128)} %bitcast.27, bf16[8,128,64]{2,1,0:T(8,128)(2,1)} %bitcast.26, bf16[8,128,64]{2,1,0:T(8,128)(2,1)} %bitcast.18), custom_call_target="tpu_custom_call" | custom-call | bytes 4000000 | tf_op jit(solution)/shard_map/pallas_call | solution.py:618
  2.5 0.0 copy-start.2
  2.5 2.5 %collective-permute-start = (bf16[528,128]{1,0:T(8,128)(2,1)}, bf16[528,128]{1,0:T(8,128)(2,1)S(1)}, u32[]{:S(2)}, u32[]{:S(2)}) collective-permute-start(bf16[528,128]{1,0:T(8,128)(2,1)} %get-tuple-element.34.p1), channel_id=1, source_target_pairs={{0,16},{1,17},{2,18},{3,19},{4,20},{5,21},{6,22},{7,23},{8,24},{9,... | collective-permute-start | bytes 405512 | tf_op jit(solution)/shard_map/ppermute | solution.py:583
  5.1 2.3 %collective-permute-start.1 = (bf16[528,128]{1,0:T(8,128)(2,1)}, bf16[528,128]{1,0:T(8,128)(2,1)S(1)}, u32[]{:S(2)}, u32[]{:S(2)}) collective-permute-start(bf16[528,128]{1,0:T(8,128)(2,1)} %get-tuple-element.35.p2), channel_id=1, source_target_pairs={{0,112},{1,113},{2,114},{3,115},{4,116},{5,117},{6,118},{7,119},{8... | collective-permute-start | bytes 405512 | tf_op jit(solution)/shard_map/ppermute | solution.py:583
  7.4 6.7 %shard_map.111 = (bf16[51200,384]{1,0:T(8,128)(2,1)}, bf16[2304,384]{1,0:T(8,128)(2,1)}) custom-call(bf16[27,64,64]{2,1,0:T(8,128)(2,1)} %bitcast.24, bf16[27,64,128]{2,1,0:T(8,128)(2,1)} %bitcast.25, bf16[27,128,128]{2,1,0:T(8,128)(2,1)} %bitcast.22, bf16[27,64,192]{2,1,0:T(8,128)(2,1)} %bitcast.23), custom_call_target="tpu_custom_call" | custom-call | bytes 4000000 | tf_op jit(solution)/shard_map/pallas_call | solution.py:604
  14.1 0.3 shard_map.112
  14.3 1.1 collective-permute-start.2
  15.4 3.6 %collective-permute-start.3 = (bf16[768,128]{1,0:T(8,128)(2,1)S(1)}, bf16[768,128]{1,0:T(8,128)(2,1)S(1)}, u32[]{:S(2)}, u32[]{:S(2)}) collective-permute-start(bf16[768,128]{1,0:T(8,128)(2,1)S(1)} %get-tuple-element.42), channel_id=1, source_target_pairs={{0,15},{1,2},{2,1},{3,4},{4,3},{5,6},{6,5},{7,8},{8,7},{9,10},{10,... | collective-permute-start | bytes 589832 | tf_op jit(solution)/shard_map/ppermute | solution.py:583
  19.0 4.7 %collective-permute-done.3.r4 = bf16[768,128]{1,0:T(8,128)(2,1)S(1)} collective-permute-done((bf16[768,128]{1,0:T(8,128)(2,1)S(1)}, bf16[768,128]{1,0:T(8,128)(2,1)S(1)}, u32[]{:S(2)}, u32[]{:S(2)}) %collective-permute-start.3) | collective-permute-done | bytes 196640 | tf_op jit(solution)/shard_map/ppermute | solution.py:583
  23.7 12.8 %shard_map.113 = (bf16[8,128,64]{2,1,0:T(8,128)(2,1)}, f32[4,128,128]{2,1,0:T(8,128)S(1)}, f32[4,128,128]{2,1,0:T(8,128)S(1)}, f32[6,80,128]{2,1,0:T(8,128)S(1)}...) custom-call(bf16[16,128,128]{2,1,0:T(8,128)(2,1)S(1)} %get-tuple-ele, ...), custom_call_target="tpu_custom_call" | custom-call | flops 4000000000 | bytes 4000000 | tf_op jit(solution)/shard_map/pallas_call | solution.py:639
  36.5 0.9 collective-permute-start.4
  37.4 1.3 %collective-permute-start.5 = (bf16[2,64,128]{2,1,0:T(8,128)(2,1)S(1)}, bf16[2,64,128]{2,1,0:T(8,128)(2,1)S(1)}, u32[]{:S(2)}, u32[]{:S(2)}) collective-permute-start(bf16[2,64,128]{2,1,0:T(8,128)(2,1)S(1)} %get-tuple-element.71), channel_id=1, source_target_pairs={{0,112},{1,113},{2,114},{3,115},{4,116},{5,117},{6,118},{7,119},{8... | collective-permute-start | bytes 98312 | tf_op jit(solution)/shard_map/ppermute | solution.py:583
  38.7 0.7 collective-permute-done.4
  39.4 2.9 %collective-permute-done.5 = bf16[2,64,128]{2,1,0:T(8,128)(2,1)S(1)} collective-permute-done((bf16[2,64,128]{2,1,0:T(8,128)(2,1)S(1)}, bf16[2,64,128]{2,1,0:T(8,128)(2,1)S(1)}, u32[]{:S(2)}, u32[]{:S(2)}) %collective-permute-start.5) | collective-permute-done | bytes 32800 | tf_op jit(solution)/shard_map/ppermute | solution.py:583
  42.3 4.8 %collective-permute-start.7 = (bf16[8,16,128]{2,1,0:T(8,128)(2,1)S(1)}, bf16[8,16,128]{2,1,0:T(8,128)(2,1)S(1)}, u32[]{:S(2)}, u32[]{:S(2)}) collective-permute-start(bf16[8,16,128]{2,1,0:T(8,128)(2,1)S(1)} %broadcast_select_fusion.2), channel_id=1, source_target_pairs={{0,15},{1,2},{2,1},{3,4},{4,3},{5,6},{6,5},{7,8},{8,7},{9,10},{10,... | collective-permute-start | bytes 98312 | tf_op jit(solution)/shard_map/ppermute | solution.py:583
  47.1 1.5 %collective-permute-start.6 = (bf16[8,16,128]{2,1,0:T(8,128)(2,1)S(1)}, bf16[8,16,128]{2,1,0:T(8,128)(2,1)S(1)}, u32[]{:S(2)}, u32[]{:S(2)}) collective-permute-start(bf16[8,16,128]{2,1,0:T(8,128)(2,1)S(1)} %get-tuple-element.63), channel_id=1, source_target_pairs={{0,1},{1,0},{2,3},{3,2},{4,5},{5,4},{6,7},{7,6},{8,9},{9,8},{10,11... | collective-permute-start | bytes 98312 | tf_op jit(solution)/shard_map/ppermute | solution.py:583
  48.6 3.8 %shard_map.114 = (bf16[3072,128]{1,0:T(8,128)(2,1)S(1)}, bf16[3072,128]{1,0:T(8,128)(2,1)S(1)}) custom-call(bf16[51200,384]{1,0:T(8,128)(2,1)} %get-tuple-element.46.kept_hbm, bf16[4,64,128]{2,1,0:T(8,128)(2,1)S(1)} %get-tuple-element.45.g_dc), custom_call_target="tpu_custom_call" | custom-call | flops 1000000000 | bytes 4000000 | tf_op jit(solution)/shard_map/pallas_call | solution.py:688
  52.5 2.6 %shard_map.115 = (bf16[1536,128]{1,0:T(8,128)(2,1)S(1)}, bf16[1536,128]{1,0:T(8,128)(2,1)S(1)}) custom-call(bf16[8,96,128]{2,1,0:T(8,128)(2,1)S(1)} %pad_maximum_fusion.1.gx, f32[6,80,128]{2,1,0:T(8,128)S(1)} %get-tuple-element.51.slope_ec, bf16[6,64,192]{2,1,0:T(8,128)(2,1)S(1)} %get-tuple-element.52.s_pool, ...), custom_call_target="tpu_custom_call" | custom-call | flops 500000000 | bytes 4000000 | tf_op jit(solution)/shard_map/pallas_call | solution.py:703
  55.0 0.3 collective-permute-start.9
  55.3 0.5 collective-permute-start.8
  55.8 1.2 %collective-permute-done.9 = bf16[1536,128]{1,0:T(8,128)(2,1)S(1)} collective-permute-done((bf16[1536,128]{1,0:T(8,128)(2,1)S(1)}, bf16[1536,128]{1,0:T(8,128)(2,1)S(1)}, u32[]{:S(2)}, u32[]{:S(2)}) %collective-permute-start.9) | collective-permute-done | bytes 393248 | tf_op jit(solution)/shard_map/ppermute | solution.py:583
  57.0 0.1 add_convert_fusion.1
  57.1 1.0 collective-permute-done.8
  58.1 0.2 add_convert_fusion
  58.4 0.1 pad_maximum_fusion
  58.5 25.1 %all_to_all.10 = bf16[64,72,128]{2,1,0:T(8,128)(2,1)S(1)} all-to-all(bf16[64,72,128]{2,1,0:T(8,128)(2,1)S(1)} %pad_maximum_fusion), channel_id=1, replica_groups=mesh['row'=8,'colh'=8,'core'=2] {'row','colh'}, dimensions={0} | all-to-all | bytes 2359296 | tf_op jit(solution)/shard_map/all_to_all | solution.py:726
  83.6 0.2 reduce_sum.12
  83.8 0.2 broadcast_in_dim.14
  83.9 22.9 %all_to_all.11.mine = bf16[64,72,128]{2,1,0:T(8,128)(2,1)S(1)} all-to-all(bf16[64,72,128]{2,1,0:T(8,128)(2,1)S(1)} %broadcast_in_dim.14), channel_id=1, replica_groups=mesh['row'=8,'colh'=8,'core'=2] {'row','colh'}, dimensions={0} | all-to-all | bytes 2359296 | tf_op jit(solution)/shard_map/all_to_all | solution.py:728
  106.8 2.9 %collective-permute-start.10 = (bf16[64,72,128]{2,1,0:T(8,128)(2,1)S(1)}, bf16[64,72,128]{2,1,0:T(8,128)(2,1)S(1)}, u32[]{:S(2)}, u32[]{:S(2)}) collective-permute-start(bf16[64,72,128]{2,1,0:T(8,128)(2,1)S(1)} %all_to_all.11.mine), channel_id=1, source_target_pairs={{0,1},{1,0},{2,3},{3,2},{4,5},{5,4},{6,7},{7,6},{8,9},{9,8},{10,11... | collective-permute-start | bytes 3538952 | tf_op jit(solution)/shard_map/ppermute | solution.py:583
  109.7 2.5 %collective-permute-done.10.other = bf16[64,72,128]{2,1,0:T(8,128)(2,1)S(1)} collective-permute-done((bf16[64,72,128]{2,1,0:T(8,128)(2,1)S(1)}, bf16[64,72,128]{2,1,0:T(8,128)(2,1)S(1)}, u32[]{:S(2)}, u32[]{:S(2)}) %collective-permute-start.10) | collective-permute-done | bytes 1179680 | tf_op jit(solution)/shard_map/ppermute | solution.py:583
  112.2 2.8 %shard_map.116 = (f32[27,64,192]{2,1,0:T(8,128)}, f32[27,128,128]{2,1,0:T(8,128)}, f32[27,64,64]{2,1,0:T(8,128)}, f32[27,64,128]{2,1,0:T(8,128)}) custom-call(bf16[64,72,128]{2,1,0:T(8,128)(2,1)S(1)} %all_to_all.11.mine, bf16[64,72,128]{2,1,0:T(8,128)(2,1)S(1)} %collective-permute-done.10.other), custom_call_target="tpu_custom_call" | custom-call | bytes 4000000 | tf_op jit(solution)/shard_map/pallas_call | solution.py:731
  (18 shorter events, 0.1 us)
Async XLA Ops:
  0.6 13.4 %copy-start.1 = (bf16[8,16,8,64]{3,2,1,0:T(8,128)(2,1)S(1)}, bf16[8,16,8,64]{3,2,1,0:T(8,128)(2,1)}, u32[]{:S(2)}) copy-start(bf16[8,16,8,64]{3,2,1,0:T(8,128)(2,1)} %param.13) | copy-start | bytes 393220
  2.5 11.6 %copy-start.2 = (bf16[528,128]{1,0:T(8,128)(2,1)S(1)}, bf16[528,128]{1,0:T(8,128)(2,1)}, u32[]{:S(2)}) copy-start(bf16[528,128]{1,0:T(8,128)(2,1)} %get-tuple-element.34.p1) | copy-start | bytes 405508
  2.5 11.6 %copy-start.3 = (bf16[528,128]{1,0:T(8,128)(2,1)S(1)}, bf16[528,128]{1,0:T(8,128)(2,1)}, u32[]{:S(2)}) copy-start(bf16[528,128]{1,0:T(8,128)(2,1)} %get-tuple-element.35.p2) | copy-start | bytes 405508
  2.5 11.5 %collective-permute-start = (bf16[528,128]{1,0:T(8,128)(2,1)}, bf16[528,128]{1,0:T(8,128)(2,1)S(1)}, u32[]{:S(2)}, u32[]{:S(2)}) collective-permute-start(bf16[528,128]{1,0:T(8,128)(2,1)} %get-tuple-element.34.p1), channel_id=1, source_target_pairs={{0,16},{1,17},{2,18},{3,19},{4,20},{5,21},{6,22},{7,23},{8,24},{9,... | collective-permute-start | bytes 405512 | tf_op jit(solution)/shard_map/ppermute | solution.py:583
  5.1 9.0 %collective-permute-start.1 = (bf16[528,128]{1,0:T(8,128)(2,1)}, bf16[528,128]{1,0:T(8,128)(2,1)S(1)}, u32[]{:S(2)}, u32[]{:S(2)}) collective-permute-start(bf16[528,128]{1,0:T(8,128)(2,1)} %get-tuple-element.35.p2), channel_id=1, source_target_pairs={{0,112},{1,113},{2,114},{3,115},{4,116},{5,117},{6,118},{7,119},{8... | collective-permute-start | bytes 405512 | tf_op jit(solution)/shard_map/ppermute | solution.py:583
  14.3 4.6 %collective-permute-start.2 = (bf16[768,128]{1,0:T(8,128)(2,1)S(1)}, bf16[768,128]{1,0:T(8,128)(2,1)S(1)}, u32[]{:S(2)}, u32[]{:S(2)}) collective-permute-start(bf16[768,128]{1,0:T(8,128)(2,1)S(1)} %get-tuple-element.41), channel_id=1, source_target_pairs={{0,1},{1,0},{2,3},{3,2},{4,5},{5,4},{6,7},{7,6},{8,9},{9,8},{10,11... | collective-permute-start | bytes 589832 | tf_op jit(solution)/shard_map/ppermute | solution.py:583
  15.4 8.3 %collective-permute-start.3 = (bf16[768,128]{1,0:T(8,128)(2,1)S(1)}, bf16[768,128]{1,0:T(8,128)(2,1)S(1)}, u32[]{:S(2)}, u32[]{:S(2)}) collective-permute-start(bf16[768,128]{1,0:T(8,128)(2,1)S(1)} %get-tuple-element.42), channel_id=1, source_target_pairs={{0,15},{1,2},{2,1},{3,4},{4,3},{5,6},{6,5},{7,8},{8,7},{9,10},{10,... | collective-permute-start | bytes 589832 | tf_op jit(solution)/shard_map/ppermute | solution.py:583
  36.5 2.8 %collective-permute-start.4 = (bf16[2,64,128]{2,1,0:T(8,128)(2,1)S(1)}, bf16[2,64,128]{2,1,0:T(8,128)(2,1)S(1)}, u32[]{:S(2)}, u32[]{:S(2)}) collective-permute-start(bf16[2,64,128]{2,1,0:T(8,128)(2,1)S(1)} %get-tuple-element.70), channel_id=1, source_target_pairs={{0,16},{1,17},{2,18},{3,19},{4,20},{5,21},{6,22},{7,23},{8,24},{9,... | collective-permute-start | bytes 98312 | tf_op jit(solution)/shard_map/ppermute | solution.py:583
  37.4 4.9 %collective-permute-start.5 = (bf16[2,64,128]{2,1,0:T(8,128)(2,1)S(1)}, bf16[2,64,128]{2,1,0:T(8,128)(2,1)S(1)}, u32[]{:S(2)}, u32[]{:S(2)}) collective-permute-start(bf16[2,64,128]{2,1,0:T(8,128)(2,1)S(1)} %get-tuple-element.71), channel_id=1, source_target_pairs={{0,112},{1,113},{2,114},{3,115},{4,116},{5,117},{6,118},{7,119},{8... | collective-permute-start | bytes 98312 | tf_op jit(solution)/shard_map/ppermute | solution.py:583
  42.3 10.1 %collective-permute-start.7 = (bf16[8,16,128]{2,1,0:T(8,128)(2,1)S(1)}, bf16[8,16,128]{2,1,0:T(8,128)(2,1)S(1)}, u32[]{:S(2)}, u32[]{:S(2)}) collective-permute-start(bf16[8,16,128]{2,1,0:T(8,128)(2,1)S(1)} %broadcast_select_fusion.2), channel_id=1, source_target_pairs={{0,15},{1,2},{2,1},{3,4},{4,3},{5,6},{6,5},{7,8},{8,7},{9,10},{10,... | collective-permute-start | bytes 98312 | tf_op jit(solution)/shard_map/ppermute | solution.py:583
  47.1 5.3 %collective-permute-start.6 = (bf16[8,16,128]{2,1,0:T(8,128)(2,1)S(1)}, bf16[8,16,128]{2,1,0:T(8,128)(2,1)S(1)}, u32[]{:S(2)}, u32[]{:S(2)}) collective-permute-start(bf16[8,16,128]{2,1,0:T(8,128)(2,1)S(1)} %get-tuple-element.63), channel_id=1, source_target_pairs={{0,1},{1,0},{2,3},{3,2},{4,5},{5,4},{6,7},{7,6},{8,9},{9,8},{10,11... | collective-permute-start | bytes 98312 | tf_op jit(solution)/shard_map/ppermute | solution.py:583
  48.6 3.9 %copy-start = (bf16[2304,384]{1,0:T(8,128)(2,1)S(1)}, bf16[2304,384]{1,0:T(8,128)(2,1)}, u32[]{:S(2)}) copy-start(bf16[2304,384]{1,0:T(8,128)(2,1)} %get-tuple-element.56.weights) | copy-start | bytes 5308420
  55.0 2.0 %collective-permute-start.9 = (bf16[1536,128]{1,0:T(8,128)(2,1)S(1)}, bf16[1536,128]{1,0:T(8,128)(2,1)S(1)}, u32[]{:S(2)}, u32[]{:S(2)}) collective-permute-start(bf16[1536,128]{1,0:T(8,128)(2,1)S(1)} %get-tuple-element.58), channel_id=1, source_target_pairs={{0,1},{1,0},{2,3},{3,2},{4,5},{5,4},{6,7},{7,6},{8,9},{9,8},{10,11... | collective-permute-start | bytes 1179656 | tf_op jit(solution)/shard_map/ppermute | solution.py:583
  55.3 2.8 %collective-permute-start.8 = (bf16[3072,128]{1,0:T(8,128)(2,1)S(1)}, bf16[3072,128]{1,0:T(8,128)(2,1)S(1)}, u32[]{:S(2)}, u32[]{:S(2)}) collective-permute-start(bf16[3072,128]{1,0:T(8,128)(2,1)S(1)} %get-tuple-element.49), channel_id=1, source_target_pairs={{0,1},{1,0},{2,3},{3,2},{4,5},{5,4},{6,7},{7,6},{8,9},{9,8},{10,11... | collective-permute-start | bytes 2359304 | tf_op jit(solution)/shard_map/ppermute | solution.py:583
  106.8 5.4 %collective-permute-start.10 = (bf16[64,72,128]{2,1,0:T(8,128)(2,1)S(1)}, bf16[64,72,128]{2,1,0:T(8,128)(2,1)S(1)}, u32[]{:S(2)}, u32[]{:S(2)}) collective-permute-start(bf16[64,72,128]{2,1,0:T(8,128)(2,1)S(1)} %all_to_all.11.mine), channel_id=1, source_target_pairs={{0,1},{1,0},{2,3},{3,2},{4,5},{5,4},{6,7},{7,6},{8,9},{9,8},{10,11... | collective-permute-start | bytes 3538952 | tf_op jit(solution)/shard_map/ppermute | solution.py:583

commit v3 on v2

--- a/solution.py
+++ b/solution.py
@@ -18,13 +18,14 @@
 ROWS_A, ROWS_B = 6144, 3072
 
 
-def call(kernel, outs, ins, scratch=(), flops=0, limit=58):
+def call(kernel, outs, ins, scratch=(), flops=0, limit=58, aliases=None):
     return pl.pallas_call(
         kernel,
         out_shape=[jax.ShapeDtypeStruct(o[0], o[1]) for o in outs],
         in_specs=list(ins),
         out_specs=[o[2] if len(o) > 2 else VM for o in outs],
         scratch_shapes=list(scratch),
+        input_output_aliases=aliases or {},
         compiler_params=pltpu.CompilerParams(vmem_limit_bytes=int(limit * MIB)),
         cost_estimate=pl.CostEstimate(flops=flops, bytes_accessed=4_000_000, transcendentals=0),
     )
@@ -68,6 +69,13 @@
     depth = v.shape[2]
     wide = jnp.concatenate([v[b : b + count] for b in range(3)], axis=2)
     return wide.reshape(count * 8, 3 * depth).astype(BF16)
+
+
+def put_taps(ref, at, v, count):
+    low = lax.broadcasted_iota(jnp.int32, (count, 8, 128), 2) < 64
+    two = jnp.where(low, v[:count], v[1 : count + 1])
+    ref[at, :, :128] = two.reshape(count * 8, 128).astype(BF16)
+    ref[at, :, 128:] = v[2 : count + 2].reshape(count * 8, 128).astype(BF16)[:, :64]
 
 
 def taps_z(g):
@@ -250,13 +258,13 @@
 
         s = v.reshape(14, 2, 8, 128)
         s = s[:, 0] + s[:, 1]
-        s = s[..., :64] + s[..., 64:]
+        s = s + pltpu.roll(s, 64, 2)
         v = bround(halve_z(s) * 0.125)
-        s2[i] = taps_y(v, 12)
+        put_taps(s2, i, v, 12)
 
         @pl.when(jnp.logical_and(i >= 2, i < 8))
         def _():
-            s_pool[i - 2] = taps_y(v[2:12], 8)
+            put_taps(s_pool, i - 2, v[2:12], 8)
 
         return 0
 
@@ -321,13 +329,14 @@
     store(LIFT, GRAD)
     loads[3].wait()
     loads[4].wait()
-    total = jnp.zeros((720, 384), F32)
-    for p in range(2):
-        for q in range(2):
-            at = W4L + 384 * (2 * p + q)
-            total += dot_n(kept[LIFT + 144 * p : LIFT + 144 * p + 720], weights[at : at + 384])
-        at = W4E + 384 * p
-        total += dot_n(kept[SKIP + 144 * p : SKIP + 144 * p + 720], weights[at : at + 384])
+    def both(first):
+        return jnp.concatenate([kept[first : first + 720], kept[first + 144 : first + 864]], axis=1)
+
+    def taps(first, step):
+        return jnp.concatenate([weights[first : first + 384], weights[first + step : first + step + 384]], axis=1)
+
+    lifted = both(LIFT)
+    total = dot_n(lifted, taps(W4L, 768)) + dot_n(lifted, taps(W4L + 384, 768)) + dot_n(both(SKIP), taps(W4E, 384))
     acc[...] = total
 
     def decode(i, _):
@@ -382,15 +391,32 @@
     return jnp.concatenate([both[:, :64], both[:, 64:]], axis=0)
 
 
-def split_wire(wire, keep, send):
-    rows = wire.shape[0] // 2
+A_LIFT, A_SKIP, A_SKIP2, A_END = 1728, 2592, 2880, 3024
+B_FINE, B_FINE2, B_END = 864, 1152, 1296
+
+
+def put_parts(wire, first, rows, block):
+    for h in range(2):
+        wire[h, first : first + rows] = block[rows * h : rows * h + rows]
+
+
+def put_three(wire, at, at2, taps):
+    lane = lax.broadcasted_iota(jnp.int32, (192, 128), 1)
+    two = jnp.where(lane < 64, taps[0][0], taps[1][1]).astype(BF16)
+    for k in range(3):
+        put_parts(wire, at + 32 * k, 32, two[64 * k : 64 * k + 64])
+    for h in range(2):
+        low = jnp.concatenate([taps[2][0][64 * k + 32 * h : 64 * k + 32 * h + 32] for k in range(3)], axis=0)
+        high = jnp.concatenate([taps[2][1][64 * k + 32 * h : 64 * k + 32 * h + 32] for k in range(3)], axis=0)
+        wire[h, at2 : at2 + 48] = jnp.where(lane[:48] < 64, low[:48], high[48:]).astype(BF16)
+
+
+def split_wire(wire, end, keep, send):
+    for h in range(2):
+        wire[h, end:] = jnp.zeros((wire.shape[1] - end, 128), BF16)
     core = lax.axis_index("core")
-    keep[...] = wire[pl.ds(pl.multiple_of(core * rows, rows), rows)]
-    send[...] = wire[pl.ds(pl.multiple_of((1 - core) * rows, rows), rows)]
-
-
-A_SKIP, A_SKIP2, A_COARSE, A_END = 1728, 2304, 2592, 6048
-B_FINE2, B_COARSE, B_END = 576, 864, 2592
+    keep[...] = wire[core]
+    send[...] = wire[1 - core]
 
 
 def weights_decode(kept_hbm, g_dc, keep, send, wire, kept, sem):
@@ -404,38 +430,32 @@
         copy.wait()
     grad = kept[GRAD:COARSE]
     gc = taps_z(g_dc[...].astype(F32).reshape(32, 8, 128))
-    wire[A_END:] = jnp.zeros((wire.shape[0] - A_END, 128), BF16)
     up = [(dot_t(grad, kept[LIFT + 144 * p : LIFT + 144 * p + 720]) * FACTOR).reshape(3, 2, 64, 384) for p in range(2)]
     same = [(dot_t(grad, kept[SKIP + 144 * p : SKIP + 144 * p + 720]) * FACTOR).reshape(3, 2, 64, 384) for p in range(2)]
     for a, (p, q) in enumerate(((0, 0), (0, 1), (1, 0))):
         p2, q2 = (0, 1) if a == 0 else (1, a - 1)
         lifted = (up[p][:, 0] + up[p2][:, 1]).reshape(192, 384).astype(BF16)
         for b in range(3):
-            at = 64 * (9 * a + 3 * b)
-            wire[at : at + 192] = lifted[:, 128 * b : 128 * b + 128]
+            for c in range(3):
+                at = A_LIFT + 32 * (9 * a + 3 * b + c)
+                put_parts(wire, at, 32, lifted[64 * c : 64 * c + 64, 128 * b : 128 * b + 128])
         taps = []
         for b in range(3):
             lanes = slice(128 * b, 128 * b + 128)
             taps.append(add_halves(same[p][:, 0, :, lanes].reshape(192, 128), q, same[p2][:, 1, :, lanes].reshape(192, 128), q2))
-        put_three(wire, A_SKIP + 192 * a, A_SKIP2 + 96 * a, taps)
+        put_three(wire, A_SKIP + 96 * a, A_SKIP2 + 48 * a, taps)
         res = (dot_t(kept[COARSE + 64 * a : COARSE + 64 * a + 256], gc) * FACTOR).astype(BF16)
         for b in range(3):
             for c in range(3):
-                at = A_COARSE + 128 * (9 * a + 3 * b + c)
-                wire[at : at + 128] = res[128 * b : 128 * b + 128, 128 * c : 128 * c + 128]
-    split_wire(wire, keep, send)
+                at = 64 * (9 * a + 3 * b + c)
+                put_parts(wire, at, 64, res[128 * b : 128 * b + 128, 128 * c : 128 * c + 128])
+    split_wire(wire, A_END, keep, send)
 
 
 def add_halves(first, q, second, q2):
     low = (first if q == 0 else pltpu.roll(first, 64, 1)) + (second if q2 == 0 else pltpu.roll(second, 64, 1))
     high = (first if q == 1 else pltpu.roll(first, 64, 1)) + (second if q2 == 1 else pltpu.roll(second, 64, 1))
     return low, high
-
-
-def put_three(wire, at, at2, taps):
-    lane = lax.broadcasted_iota(jnp.int32, (192, 128), 1)
-    wire[at : at + 192] = jnp.where(lane < 64, taps[0][0], taps[1][1]).astype(BF16)
-    wire[at2 : at2 + 96] = jnp.where(lane[:96] < 64, taps[2][0][:96], taps[2][1][96:]).astype(BF16)
 
 
 def back_encode(gx, slope_ec, s_pool, s_in, g_skip, slope_ef, weights, keep, send, s5, ge, gz, wire):
@@ -460,7 +480,6 @@
         g = (g_skip[x].reshape(16, 8, 128) + up[x]) * slope_ef[x].reshape(16, 8, 128)
         gz[x] = taps_z(bround(g))
     gf = gz[...].reshape(512, 384)
-    wire[B_END:] = jnp.zeros((wire.shape[0] - B_END, 128), BF16)
     parts = [(dot_t(s_in[p : p + 4].reshape(512, 384), gf) * FACTOR).reshape(3, 2, 64, 384) for p in range(2)]
     for a, (p, q) in enumerate(((0, 0), (0, 1), (1, 0))):
         p2, q2 = (0, 1) if a == 0 else (1, a - 1)
@@ -468,59 +487,68 @@
         for c in range(3):
             lanes = slice(128 * c, 128 * c + 128)
             taps.append(add_halves(parts[p][:, q, :, lanes].reshape(192, 128), 0, parts[p2][:, q2, :, lanes].reshape(192, 128), 1))
-        put_three(wire, 192 * a, B_FINE2 + 96 * a, taps)
+        put_three(wire, B_FINE + 96 * a, B_FINE2 + 48 * a, taps)
         res = (dot_t(s_pool[a : a + 4].reshape(256, 192), gc) * FACTOR).astype(BF16)
         for b in range(3):
             for c in range(3):
-                at = B_COARSE + 64 * (9 * a + 3 * b + c)
-                wire[at : at + 64] = res[64 * b : 64 * b + 64, 128 * c : 128 * c + 128]
-    split_wire(wire, keep, send)
-
-
-def unpack(mine, other, df_hbm, dc_hbm, ef_hbm, ec_hbm, wire_a, wire_b, d_df, d_dc, d_ef, d_ec, sem):
+                at = 32 * (9 * a + 3 * b + c)
+                put_parts(wire, at, 32, res[64 * b : 64 * b + 64, 128 * c : 128 * c + 128])
+    split_wire(wire, B_END, keep, send)
+
+
+def unpack(of_this_core, total, *refs):
+    df_hbm, dc_hbm, ef_hbm, ec_hbm, d_df, d_dc, d_ef, d_ec, sem = refs[-9:]
     core = lax.axis_index("core")
-    for wire, first in ((wire_a, 0), (wire_b, ROWS_A // 128)):
-        rows = wire.shape[0] // 2
-        each = rows // 64
-        here = pl.ds(pl.multiple_of(core * rows, rows), rows)
-        there = pl.ds(pl.multiple_of((1 - core) * rows, rows), rows)
-        wire[here] = mine[:, first : first + each].reshape(rows, 128)
-        wire[there] = other[:, first : first + each].reshape(rows, 128)
+    half = core if of_this_core else 1 - core
+    wire_a = total[:, : ROWS_A // 128].reshape(ROWS_A // 2, 128)
+    wire_b = total[:, ROWS_A // 128 :].reshape(ROWS_B // 2, 128)
     stores = []
 
-    def store(src, dst, rows):
-        stores.append(pltpu.make_async_copy(src.at[rows], dst.at[rows], sem.at[len(stores)]))
+    def store(src, dst, a):
+        rows = src.shape[1]
+        at = pl.ds(pl.multiple_of(half * rows, rows), rows)
+        taps = pl.ds(9 * a, 9)
+        stores.append(pltpu.make_async_copy(src.at[taps], dst.at[taps, at], sem.at[len(stores)]))
         stores[-1].start()
 
+    def three(wire, at, at2):
+        two = wire[at : at + 96].astype(F32)
+        return two[:, :64], two[:, 64:], unhalve(wire[at2 : at2 + 48].astype(F32))
+
     for a in range(3):
-        taps = pl.ds(9 * a, 9)
-        first = A_COARSE + 1152 * a
-        d_dc[taps] = wire_a[first : first + 1152].astype(F32).reshape(9, 128, 128)
-        store(d_dc, dc_hbm, taps)
-    for a in range(3):
-        taps = pl.ds(9 * a, 9)
-        two = wire_a[A_SKIP + 192 * a : A_SKIP + 192 * a + 192].astype(F32)
-        three = unhalve(wire_a[A_SKIP2 + 96 * a : A_SKIP2 + 96 * a + 96].astype(F32))
-        skip = (two[:, :64], two[:, 64:], three)
-        two = wire_b[192 * a : 192 * a + 192].astype(F32)
-        three = unhalve(wire_b[B_FINE2 + 96 * a : B_FINE2 + 96 * a + 96].astype(F32))
-        fine = (two[:, :64], two[:, 64:], three)
+        taps = slice(9 * a, 9 * a + 9)
+        d_dc[taps] = wire_a[576 * a : 576 * a + 576].astype(F32).reshape(9, 64, 128)
+        store(d_dc, dc_hbm, a)
+        skip = three(wire_a, A_SKIP + 96 * a, A_SKIP2 + 48 * a)
+        fine = three(wire_b, B_FINE + 96 * a, B_FINE2 + 48 * a)
+        first = A_LIFT + 288 * a
+        d_df[taps, :, :128] = wire_a[first : first + 288].astype(F32).reshape(9, 32, 128)
         for b in range(3):
             for c in range(3):
                 k = 9 * a + 3 * b + c
-                d_df[k, :, :128] = wire_a[64 * k : 64 * k + 64].astype(F32)
-                d_df[k, :, 128:] = skip[b][64 * c : 64 * c + 64]
-                d_ef[k] = fine[c][64 * b : 64 * b + 64]
-        store(d_df, df_hbm, taps)
-        store(d_ef, ef_hbm, taps)
-        first = B_COARSE + 576 * a
-        d_ec[taps] = wire_b[first : first + 576].astype(F32).reshape(9, 64, 128)
-        store(d_ec, ec_hbm, taps)
+                d_df[k, :, 128:] = skip[b][32 * c : 32 * c + 32]
+                d_ef[k] = fine[c][32 * b : 32 * b + 32]
+        store(d_df, df_hbm, a)
+        store(d_ef, ef_hbm, a)
+        d_ec[taps] = wire_b[288 * a : 288 * a + 288].astype(F32).reshape(9, 32, 128)
+        store(d_ec, ec_hbm, a)
     for copy in stores:
         copy.wait()
 
 
-def arrange(e1, e2, d3, d4, wf_hbm, wb, wf, sem):
+def arrange_back(e2, d3, wb):
+    for a in range(3):
+        for b in range(3):
+            coarse = slice(128 * b, 128 * b + 128)
+            for c in range(3):
+                k = 9 * a + 3 * b + c
+                at = 384 * a + 128 * c
+                wb[W6 + at : W6 + at + 128, coarse] = d3[26 - k]
+                wb[W7 + at : W7 + at + 64, coarse] = e2[26 - k]
+                wb[W7 + at + 64 : W7 + at + 128, coarse] = e2[26 - k]
+
+
+def arrange(e1, e2, d3, d4, wf_hbm, wf, sem):
     for a in range(3):
         for b in range(3):
             coarse = slice(128 * b, 128 * b + 128)
@@ -529,10 +557,6 @@
                 lanes = slice(128 * c, 128 * c + 128)
                 wf[W2 + 192 * a + 64 * b : W2 + 192 * a + 64 * b + 64, lanes] = e2[k]
                 wf[W3 + 384 * a + 128 * b : W3 + 384 * a + 128 * b + 128, lanes] = d3[k]
-                at = 384 * a + 128 * c
-                wb[W6 + at : W6 + at + 128, coarse] = d3[26 - k]
-                wb[W7 + at : W7 + at + 64, coarse] = e2[26 - k]
-                wb[W7 + at + 64 : W7 + at + 128, coarse] = e2[26 - k]
     none = jnp.zeros((64, 64), F32)
 
     def tap(ref, a, rest, lanes, turned=False):
@@ -601,17 +625,16 @@
 
     odd_r, odd_c = row % 2, core
     active = block_active.reshape(2)
-    w_forward, w_backward = call(
+    e2 = encode_coarse.reshape(27, 64, 128)
+    d3 = decode_coarse.reshape(27, 128, 128)
+    d4 = jnp.transpose(decode_fine, (0, 1, 2, 4, 3)).reshape(27, 64, 192)
+    (w_forward,) = call(
         arrange,
-        [((ROOM, 384), BF16, HB), ((WB, 384), BF16)],
+        [((ROOM, 384), BF16, HB)],
         [VM] * 4,
         scratch=[pltpu.VMEM((WF, 384), BF16), pltpu.SemaphoreType.DMA((7,))],
-    )(
-        encode_fine.reshape(27, 64, 64),
-        encode_coarse.reshape(27, 64, 128),
-        decode_coarse.reshape(27, 128, 128),
-        jnp.transpose(decode_fine, (0, 1, 2, 4, 3)).reshape(27, 64, 192),
-    )
+    )(encode_fine.reshape(27, 64, 64), e2, d3, d4)
+    (w_backward,) = call(arrange_back, [((WB, 384), BF16)], [VM] * 2)(e2, d3)
 
     feat = features.reshape(8, 128, 64)
     cot = out_cotangent.reshape(8, 128, 64)
@@ -627,7 +650,7 @@
         ],
     )(active, feat, cot)
     rz, rxz = swap(p1, swap_z), swap(p2, swap_xz)
-    rz, w_forward, w_backward = lax.optimization_barrier((rz, w_forward, w_backward))
+    rz, w_forward = lax.optimization_barrier((rz, w_forward))
     xall, xmask, p3, p4 = call(
         pack_y,
         [((16, 128, 128), BF16), ((3, 16, 128), F32), ((768, 128), BF16), ((768, 128), BF16)],
@@ -635,6 +658,7 @@
         limit=8,
     )(cot, p1, p2, rz, rxz)
     r3, r4 = swap(p3, swap_core), swap(p4, swap_yz)
+    r3, w_backward = lax.optimization_barrier((r3, w_backward))
 
     decoded, slope_ef, g_skip, slope_ec, g_dc, s_in, s_pool, kept = call(
         forward,
@@ -670,6 +694,9 @@
         limit=26,
     )(xall, xmask, r3, r4, w_forward)
 
+    def add(keep, got):
+        return (keep.astype(F32) + got.astype(F32)).astype(BF16).reshape(64, -1, 128)
+
     is_odd = odd_r == 1
     q1 = swap(jnp.where(is_odd, g_dc[:2], g_dc[2:]), swap_z)
     q2 = swap(jnp.where(is_odd, g_dc[2:], g_dc[:2]), swap_xz)
@@ -690,14 +717,14 @@
         [((ROWS_A // 2, 128), BF16)] * 2,
         [HB, VM],
         scratch=[
-            pltpu.VMEM((ROWS_A, 128), BF16),
+            pltpu.VMEM((2, ROWS_A // 2, 128), BF16),
             pltpu.VMEM((KEPT, 384), BF16),
             pltpu.SemaphoreType.DMA((4,)),
         ],
         flops=1_000_000_000,
         limit=26,
     )(kept, g_dc)
-    got_a = swap(send_a, swap_core)
+    half_a = add(keep_a, swap(send_a, swap_core))
     gx, keep_a = lax.optimization_barrier((gx, keep_a))
 
     keep_b, send_b = call(
@@ -708,35 +735,32 @@
             pltpu.VMEM((8, 80, 384), BF16),
             pltpu.VMEM((6, 64, 384), BF16),
             pltpu.VMEM((4, 128, 384), BF16),
-            pltpu.VMEM((ROWS_B, 128), BF16),
+            pltpu.VMEM((2, ROWS_B // 2, 128), BF16),
         ],
         flops=500_000_000,
         limit=20,
     )(gx, slope_ec, s_pool, s_in, g_skip, slope_ef, w_backward)
-    got_b = swap(send_b, swap_core)
+    half_b = add(keep_b, swap(send_b, swap_core))
 
     chips = ("row", "colh")
-    half = jnp.concatenate(
-        [
-            (keep.astype(F32) + got.astype(F32)).astype(BF16).reshape(64, -1, 128)
-            for keep, got in ((keep_a, got_a), (keep_b, got_b))
-        ],
-        axis=1,
-    )
+    half = jnp.concatenate([half_a, half_b], axis=1)
     terms = lax.all_to_all(half, chips, 0, 0, tiled=True)
     total = jnp.sum(terms.astype(F32), axis=0).astype(BF16)
     mine = lax.all_to_all(jnp.broadcast_to(total[None], (64, CHUNK, 128)), chips, 0, 0, tiled=True)
     other = swap(mine, swap_core)
     shapes = ((27, 64, 192), (27, 128, 128), (27, 64, 64), (27, 64, 128))
-    d_df, d_dc, d_ef, d_ec = call(
-        unpack,
-        [(shape, F32, HB) for shape in shapes],
-        [VM] * 2,
-        scratch=[pltpu.VMEM((ROWS_A, 128), BF16), pltpu.VMEM((ROWS_B, 128), BF16)]
-        + [pltpu.VMEM(shape, F32) for shape in shapes]
-        + [pltpu.SemaphoreType.DMA((12,))],
-        limit=24,
-    )(mine, other)
+    halves = ((27, 32, 192), (27, 64, 128), (27, 32, 64), (27, 32, 128))
+    grads = []
+    for of_this_core, values in ((True, mine), (False, other)):
+        grads = call(
+            functools.partial(unpack, of_this_core),
+            [(shape, F32, HB) for shape in shapes],
+            [VM] + [HB] * len(grads),
+            scratch=[pltpu.VMEM(shape, F32) for shape in halves] + [pltpu.SemaphoreType.DMA((12,))],
+            limit=24,
+            aliases={1 + k: k for k in range(len(grads))},
+        )(values, *grads)
+    d_df, d_dc, d_ef, d_ec = grads
     return (
         decoded.reshape(8, 16, 8, 64),
         d_ef.reshape(3, 3, 3, 64, 64),

time: 115 us -> 112 us (0.974)
  waiting for transfers between devices: 13 us -> 7.6 us
    ppermute x11, waiting for transfers between devices: 13 us -> 7.6 us  [swap(): return lax.ppermute(v, ('row', 'colh', 'core'), pairs)]
    pallas_call x2 -> x4, Pallas kernels: 9.49 us -> 11.3 us  [the longest x1 5.24 us: body(): call(arrange, [((ROOM, 384), BF16, HB)], [VM] * 4, scratch=[pltpu.VMEM((W...]
    pallas_call x1, Pallas kernels: 12.8 us -> 11.6 us  [body(): call(forward, [((8, 128, 64), BF16, HB), ((4, 128, 128), F32), ((4, 128,...]
  transfers between devices with their start and end apart: 11 -> 11, of which waited for: 6 -> 5; matrix products, arithmetic and copies ran while one was open for 0% -> 0% of each run, Pallas kernels for 9% -> 12%
where the time goes in v3:
time: 112 us
  blocking collectives  48.4 us (43%)
  Pallas kernels  31.2 us (28%)
  starting transfers between devices  22.5 us (20%)
  waiting for transfers between devices  7.6 us (7%)
    all_to_all x1, blocking collectives, body(): terms = lax.all_to_all(half, chips, 0, 0, tiled=True)  25.6 us
    all_to_all x1, blocking collectives, body(): lax.all_to_all(jnp.broadcast_to(total[None], (64, CHUNK, 128)), chips, 0,...  22.9 us
    ppermute x11, starting transfers between devices, swap(): return lax.ppermute(v, ('row', 'colh', 'core'), pairs)  22.5 us
    pallas_call x1, Pallas kernels, body(): call(forward, [((8, 128, 64), BF16, HB), ((4, 128, 128), F32), ((4, 128,...  11.6 us
    ppermute x11, waiting for transfers between devices, swap(): return lax.ppermute(v, ('row', 'colh', 'core'), pairs)  7.6 us
    pallas_call x1, Pallas kernels, body(): call(arrange, [((ROOM, 384), BF16, HB)], [VM] * 4, scratch=[pltpu.VMEM((W...  5.24 us
    pallas_call x1, Pallas kernels, body(): call(weights_decode, [((ROWS_A // 2, 128), BF16)] * 2, [HB, VM], scratch=...  3.69 us
    pallas_call x2, Pallas kernels, body(): call(functools.partial(unpack, of_this_core), [(shape, F32, HB) for shape...  3.26 us
  transfers between devices with their start and end apart: 11, of which 5 were waited for; matrix products, arithmetic and copies ran while one was open for 0% of the time, Pallas kernels for 12%

profile of v3, /device:TPU:1, one launch (start us, length us, event | category | flops | bytes accessed | tf_op | source)
XLA Modules:
  0.0 111.5 jit_solution(9385903700554118431)
XLA Ops:
  0.6 1.8 %shard_map.110 = (bf16[528,128]{1,0:T(8,128)(2,1)}, bf16[528,128]{1,0:T(8,128)(2,1)}) custom-call(s32[2]{0:T(128)} %bitcast.33, bf16[8,128,64]{2,1,0:T(8,128)(2,1)} %bitcast.32, bf16[8,128,64]{2,1,0:T(8,128)(2,1)} %bitcast.18), custom_call_target="tpu_custom_call" | custom-call | bytes 4000000 | tf_op jit(solution)/shard_map/pallas_call | solution.py:641
  2.5 2.5 %collective-permute-start = (bf16[528,128]{1,0:T(8,128)(2,1)}, bf16[528,128]{1,0:T(8,128)(2,1)S(1)}, u32[]{:S(2)}, u32[]{:S(2)}) collective-permute-start(bf16[528,128]{1,0:T(8,128)(2,1)} %get-tuple-element.36.p1), channel_id=1, source_target_pairs={{0,16},{1,17},{2,18},{3,19},{4,20},{5,21},{6,22},{7,23},{8,24},{9,... | collective-permute-start | bytes 405512 | tf_op jit(solution)/shard_map/ppermute | solution.py:607
  5.0 2.3 %collective-permute-start.1 = (bf16[528,128]{1,0:T(8,128)(2,1)}, bf16[528,128]{1,0:T(8,128)(2,1)S(1)}, u32[]{:S(2)}, u32[]{:S(2)}) collective-permute-start(bf16[528,128]{1,0:T(8,128)(2,1)} %get-tuple-element.37.p2), channel_id=1, source_target_pairs={{0,112},{1,113},{2,114},{3,115},{4,116},{5,117},{6,118},{7,119},{8... | collective-permute-start | bytes 405512 | tf_op jit(solution)/shard_map/ppermute | solution.py:607
  7.3 5.2 %shard_map.111.weights_hbm = bf16[51200,384]{1,0:T(8,128)(2,1)} custom-call(bf16[27,64,64]{2,1,0:T(8,128)(2,1)} %bitcast.31, bf16[27,64,128]{2,1,0:T(8,128)(2,1)} %bitcast.23, bf16[27,128,128]{2,1,0:T(8,128)(2,1)} %bitcast.20, bf16[27,64,192]{2,1,0:T(8,128)(2,1)} %bitcast.30), custom_call_target="tpu_custom_call" | custom-call | bytes 4000000 | tf_op jit(solution)/shard_map/pallas_call | solution.py:631
  12.6 0.3 shard_map.112
  12.9 1.1 collective-permute-start.2
  13.9 3.6 %collective-permute-start.3 = (bf16[768,128]{1,0:T(8,128)(2,1)S(1)}, bf16[768,128]{1,0:T(8,128)(2,1)S(1)}, u32[]{:S(2)}, u32[]{:S(2)}) collective-permute-start(bf16[768,128]{1,0:T(8,128)(2,1)S(1)} %get-tuple-element.43), channel_id=1, source_target_pairs={{0,15},{1,2},{2,1},{3,4},{4,3},{5,6},{6,5},{7,8},{8,7},{9,10},{10,... | collective-permute-start | bytes 589832 | tf_op jit(solution)/shard_map/ppermute | solution.py:607
  17.5 2.8 %shard_map.113.weights = bf16[2304,384]{1,0:T(8,128)(2,1)} custom-call(bf16[27,64,128]{2,1,0:T(8,128)(2,1)} %bitcast.24, bf16[27,128,128]{2,1,0:T(8,128)(2,1)} %bitcast.21), custom_call_target="tpu_custom_call" | custom-call | bytes 4000000 | tf_op jit(solution)/shard_map/pallas_call | solution.py:637
  20.3 1.9 %collective-permute-done.3.r4 = bf16[768,128]{1,0:T(8,128)(2,1)S(1)} collective-permute-done((bf16[768,128]{1,0:T(8,128)(2,1)S(1)}, bf16[768,128]{1,0:T(8,128)(2,1)S(1)}, u32[]{:S(2)}, u32[]{:S(2)}) %collective-permute-start.3) | collective-permute-done | bytes 196640 | tf_op jit(solution)/shard_map/ppermute | solution.py:607
  22.2 11.6 %shard_map.114 = (bf16[8,128,64]{2,1,0:T(8,128)(2,1)}, f32[4,128,128]{2,1,0:T(8,128)S(1)}, f32[4,128,128]{2,1,0:T(8,128)S(1)}, f32[6,80,128]{2,1,0:T(8,128)S(1)}...) custom-call(bf16[16,128,128]{2,1,0:T(8,128)(2,1)S(1)} %get-tuple-ele, ...), custom_call_target="tpu_custom_call" | custom-call | flops 4000000000 | bytes 4000000 | tf_op jit(solution)/shard_map/pallas_call | solution.py:663
  33.8 1.0 collective-permute-start.5
  34.9 2.3 %collective-permute-start.6 = (bf16[2,64,128]{2,1,0:T(8,128)(2,1)S(1)}, bf16[2,64,128]{2,1,0:T(8,128)(2,1)S(1)}, u32[]{:S(2)}, u32[]{:S(2)}) collective-permute-start(bf16[2,64,128]{2,1,0:T(8,128)(2,1)S(1)} %get-tuple-element.75), channel_id=1, source_target_pairs={{0,112},{1,113},{2,114},{3,115},{4,116},{5,117},{6,118},{7,119},{8... | collective-permute-start | bytes 98312 | tf_op jit(solution)/shard_map/ppermute | solution.py:607
  37.2 2.6 %collective-permute-done.6 = bf16[2,64,128]{2,1,0:T(8,128)(2,1)S(1)} collective-permute-done((bf16[2,64,128]{2,1,0:T(8,128)(2,1)S(1)}, bf16[2,64,128]{2,1,0:T(8,128)(2,1)S(1)}, u32[]{:S(2)}, u32[]{:S(2)}) %collective-permute-start.6) | collective-permute-done | bytes 32800 | tf_op jit(solution)/shard_map/ppermute | solution.py:607
  39.8 4.8 %collective-permute-start.8 = (bf16[8,16,128]{2,1,0:T(8,128)(2,1)S(1)}, bf16[8,16,128]{2,1,0:T(8,128)(2,1)S(1)}, u32[]{:S(2)}, u32[]{:S(2)}) collective-permute-start(bf16[8,16,128]{2,1,0:T(8,128)(2,1)S(1)} %broadcast_select_fusion.2), channel_id=1, source_target_pairs={{0,15},{1,2},{2,1},{3,4},{4,3},{5,6},{6,5},{7,8},{8,7},{9,10},{10,... | collective-permute-start | bytes 98312 | tf_op jit(solution)/shard_map/ppermute | solution.py:607
  44.6 1.4 %collective-permute-start.7 = (bf16[8,16,128]{2,1,0:T(8,128)(2,1)S(1)}, bf16[8,16,128]{2,1,0:T(8,128)(2,1)S(1)}, u32[]{:S(2)}, u32[]{:S(2)}) collective-permute-start(bf16[8,16,128]{2,1,0:T(8,128)(2,1)S(1)} %get-tuple-element.67), channel_id=1, source_target_pairs={{0,1},{1,0},{2,3},{3,2},{4,5},{5,4},{6,7},{7,6},{8,9},{9,8},{10,11... | collective-permute-start | bytes 98312 | tf_op jit(solution)/shard_map/ppermute | solution.py:607
  46.0 3.7 %shard_map.115 = (bf16[3072,128]{1,0:T(8,128)(2,1)S(1)}, bf16[3072,128]{1,0:T(8,128)(2,1)S(1)}) custom-call(bf16[51200,384]{1,0:T(8,128)(2,1)} %get-tuple-element.46.kept_hbm, bf16[4,64,128]{2,1,0:T(8,128)(2,1)S(1)} %get-tuple-element.47.g_dc), custom_call_target="tpu_custom_call" | custom-call | flops 1000000000 | bytes 4000000 | tf_op jit(solution)/shard_map/pallas_call | solution.py:715
  49.8 2.5 %shard_map.116 = (bf16[1536,128]{1,0:T(8,128)(2,1)S(1)}, bf16[1536,128]{1,0:T(8,128)(2,1)S(1)}) custom-call(bf16[8,96,128]{2,1,0:T(8,128)(2,1)S(1)} %pad_maximum_fusion.1.gx, f32[6,80,128]{2,1,0:T(8,128)S(1)} %get-tuple-element.51.slope_ec, bf16[6,64,192]{2,1,0:T(8,128)(2,1)S(1)} %get-tuple-element.52.s_pool, ...), custom_call_target="tpu_custom_call" | custom-call | flops 500000000 | bytes 4000000 | tf_op jit(solution)/shard_map/pallas_call | solution.py:730
  52.3 0.1 collective-permute-start.9
  52.4 0.5 collective-permute-start.4
  52.9 1.2 %collective-permute-done.9 = bf16[1536,128]{1,0:T(8,128)(2,1)S(1)} collective-permute-done((bf16[1536,128]{1,0:T(8,128)(2,1)S(1)}, bf16[1536,128]{1,0:T(8,128)(2,1)S(1)}, u32[]{:S(2)}, u32[]{:S(2)}) %collective-permute-start.9) | collective-permute-done | bytes 393248 | tf_op jit(solution)/shard_map/ppermute | solution.py:607
  54.1 0.1 add_convert_fusion.1
  54.2 1.0 collective-permute-done.4
  55.3 0.2 add_convert_fusion
  55.5 0.1 pad_maximum_fusion
  55.6 25.6 %all_to_all.10 = bf16[64,72,128]{2,1,0:T(8,128)(2,1)S(1)} all-to-all(bf16[64,72,128]{2,1,0:T(8,128)(2,1)S(1)} %pad_maximum_fusion), channel_id=1, replica_groups=mesh['row'=8,'colh'=8,'core'=2] {'row','colh'}, dimensions={0} | all-to-all | bytes 2359296 | tf_op jit(solution)/shard_map/all_to_all | solution.py:747
  81.1 0.2 reduce_sum.12
  81.3 0.2 broadcast_in_dim.14
  81.5 22.9 %all_to_all.11.total = bf16[64,72,128]{2,1,0:T(8,128)(2,1)S(1)} all-to-all(bf16[64,72,128]{2,1,0:T(8,128)(2,1)S(1)} %broadcast_in_dim.14), channel_id=1, replica_groups=mesh['row'=8,'colh'=8,'core'=2] {'row','colh'}, dimensions={0} | all-to-all | bytes 2359296 | tf_op jit(solution)/shard_map/all_to_all | solution.py:749
  104.3 2.9 %collective-permute-start.10 = (bf16[64,72,128]{2,1,0:T(8,128)(2,1)S(1)}, bf16[64,72,128]{2,1,0:T(8,128)(2,1)S(1)}, u32[]{:S(2)}, u32[]{:S(2)}) collective-permute-start(bf16[64,72,128]{2,1,0:T(8,128)(2,1)S(1)} %all_to_all.11.total), channel_id=1, source_target_pairs={{0,1},{1,0},{2,3},{3,2},{4,5},{5,4},{6,7},{7,6},{8,9},{9,8},{10,11... | collective-permute-start | bytes 3538952 | tf_op jit(solution)/shard_map/ppermute | solution.py:607
  107.3 1.6 %shard_map.117 = (f32[27,64,192]{2,1,0:T(8,128)}, f32[27,128,128]{2,1,0:T(8,128)}, f32[27,64,64]{2,1,0:T(8,128)}, f32[27,64,128]{2,1,0:T(8,128)}) custom-call(bf16[64,72,128]{2,1,0:T(8,128)(2,1)S(1)} %all_to_all.11.total), custom_call_target="tpu_custom_call" | custom-call | bytes 4000000 | tf_op jit(solution)/shard_map/pallas_call | solution.py:755
  108.9 0.8 collective-permute-done.10.total
  109.7 1.6 %shard_map.118 = (f32[27,64,192]{2,1,0:T(8,128)}, f32[27,128,128]{2,1,0:T(8,128)}, f32[27,64,64]{2,1,0:T(8,128)}, f32[27,64,128]{2,1,0:T(8,128)}) custom-call(bf16[64,72,128]{2,1,0:T(8,128)(2,1)S(1)} %collective-permute-done.10.total, ...), custom_call_target="tpu_custom_call", output_to_operand_aliasing={{0}: (1, {}), {1}: (2, {}), {2}: (3, {}), {3}: (4, {})} | custom-call | bytes 4000000 | tf_op jit(solution)/shard_map/pallas_call | solution.py:755
  (20 shorter events, 0.1 us)
Async XLA Ops:
  2.5 10.1 %collective-permute-start = (bf16[528,128]{1,0:T(8,128)(2,1)}, bf16[528,128]{1,0:T(8,128)(2,1)S(1)}, u32[]{:S(2)}, u32[]{:S(2)}) collective-permute-start(bf16[528,128]{1,0:T(8,128)(2,1)} %get-tuple-element.36.p1), channel_id=1, source_target_pairs={{0,16},{1,17},{2,18},{3,19},{4,20},{5,21},{6,22},{7,23},{8,24},{9,... | collective-permute-start | bytes 405512 | tf_op jit(solution)/shard_map/ppermute | solution.py:607
  5.0 7.6 %collective-permute-start.1 = (bf16[528,128]{1,0:T(8,128)(2,1)}, bf16[528,128]{1,0:T(8,128)(2,1)S(1)}, u32[]{:S(2)}, u32[]{:S(2)}) collective-permute-start(bf16[528,128]{1,0:T(8,128)(2,1)} %get-tuple-element.37.p2), channel_id=1, source_target_pairs={{0,112},{1,113},{2,114},{3,115},{4,116},{5,117},{6,118},{7,119},{8... | collective-permute-start | bytes 405512 | tf_op jit(solution)/shard_map/ppermute | solution.py:607
  7.3 5.3 %copy-start.1 = (bf16[8,16,8,64]{3,2,1,0:T(8,128)(2,1)S(1)}, bf16[8,16,8,64]{3,2,1,0:T(8,128)(2,1)}, u32[]{:S(2)}) copy-start(bf16[8,16,8,64]{3,2,1,0:T(8,128)(2,1)} %param.13) | copy-start | bytes 393220
  7.3 5.3 %copy-start.2 = (bf16[528,128]{1,0:T(8,128)(2,1)S(1)}, bf16[528,128]{1,0:T(8,128)(2,1)}, u32[]{:S(2)}) copy-start(bf16[528,128]{1,0:T(8,128)(2,1)} %get-tuple-element.36.p1) | copy-start | bytes 405508
  7.3 5.3 %copy-start.3 = (bf16[528,128]{1,0:T(8,128)(2,1)S(1)}, bf16[528,128]{1,0:T(8,128)(2,1)}, u32[]{:S(2)}) copy-start(bf16[528,128]{1,0:T(8,128)(2,1)} %get-tuple-element.37.p2) | copy-start | bytes 405508
  12.9 7.4 %collective-permute-start.2 = (bf16[768,128]{1,0:T(8,128)(2,1)S(1)}, bf16[768,128]{1,0:T(8,128)(2,1)S(1)}, u32[]{:S(2)}, u32[]{:S(2)}) collective-permute-start(bf16[768,128]{1,0:T(8,128)(2,1)S(1)} %get-tuple-element.41), channel_id=1, source_target_pairs={{0,1},{1,0},{2,3},{3,2},{4,5},{5,4},{6,7},{7,6},{8,9},{9,8},{10,11... | collective-permute-start | bytes 589832 | tf_op jit(solution)/shard_map/ppermute | solution.py:607
  13.9 8.3 %collective-permute-start.3 = (bf16[768,128]{1,0:T(8,128)(2,1)S(1)}, bf16[768,128]{1,0:T(8,128)(2,1)S(1)}, u32[]{:S(2)}, u32[]{:S(2)}) collective-permute-start(bf16[768,128]{1,0:T(8,128)(2,1)S(1)} %get-tuple-element.43), channel_id=1, source_target_pairs={{0,15},{1,2},{2,1},{3,4},{4,3},{5,6},{6,5},{7,8},{8,7},{9,10},{10,... | collective-permute-start | bytes 589832 | tf_op jit(solution)/shard_map/ppermute | solution.py:607
  33.8 3.3 %collective-permute-start.5 = (bf16[2,64,128]{2,1,0:T(8,128)(2,1)S(1)}, bf16[2,64,128]{2,1,0:T(8,128)(2,1)S(1)}, u32[]{:S(2)}, u32[]{:S(2)}) collective-permute-start(bf16[2,64,128]{2,1,0:T(8,128)(2,1)S(1)} %get-tuple-element.74), channel_id=1, source_target_pairs={{0,16},{1,17},{2,18},{3,19},{4,20},{5,21},{6,22},{7,23},{8,24},{9,... | collective-permute-start | bytes 98312 | tf_op jit(solution)/shard_map/ppermute | solution.py:607
  34.9 4.9 %collective-permute-start.6 = (bf16[2,64,128]{2,1,0:T(8,128)(2,1)S(1)}, bf16[2,64,128]{2,1,0:T(8,128)(2,1)S(1)}, u32[]{:S(2)}, u32[]{:S(2)}) collective-permute-start(bf16[2,64,128]{2,1,0:T(8,128)(2,1)S(1)} %get-tuple-element.75), channel_id=1, source_target_pairs={{0,112},{1,113},{2,114},{3,115},{4,116},{5,117},{6,118},{7,119},{8... | collective-permute-start | bytes 98312 | tf_op jit(solution)/shard_map/ppermute | solution.py:607
  39.8 9.9 %collective-permute-start.8 = (bf16[8,16,128]{2,1,0:T(8,128)(2,1)S(1)}, bf16[8,16,128]{2,1,0:T(8,128)(2,1)S(1)}, u32[]{:S(2)}, u32[]{:S(2)}) collective-permute-start(bf16[8,16,128]{2,1,0:T(8,128)(2,1)S(1)} %broadcast_select_fusion.2), channel_id=1, source_target_pairs={{0,15},{1,2},{2,1},{3,4},{4,3},{5,6},{6,5},{7,8},{8,7},{9,10},{10,... | collective-permute-start | bytes 98312 | tf_op jit(solution)/shard_map/ppermute | solution.py:607
  44.6 5.2 %collective-permute-start.7 = (bf16[8,16,128]{2,1,0:T(8,128)(2,1)S(1)}, bf16[8,16,128]{2,1,0:T(8,128)(2,1)S(1)}, u32[]{:S(2)}, u32[]{:S(2)}) collective-permute-start(bf16[8,16,128]{2,1,0:T(8,128)(2,1)S(1)} %get-tuple-element.67), channel_id=1, source_target_pairs={{0,1},{1,0},{2,3},{3,2},{4,5},{5,4},{6,7},{7,6},{8,9},{9,8},{10,11... | collective-permute-start | bytes 98312 | tf_op jit(solution)/shard_map/ppermute | solution.py:607
  46.0 3.8 %copy-start = (bf16[2304,384]{1,0:T(8,128)(2,1)S(1)}, bf16[2304,384]{1,0:T(8,128)(2,1)}, u32[]{:S(2)}) copy-start(bf16[2304,384]{1,0:T(8,128)(2,1)} %shard_map.113.weights) | copy-start | bytes 5308420
  52.3 1.8 %collective-permute-start.9 = (bf16[1536,128]{1,0:T(8,128)(2,1)S(1)}, bf16[1536,128]{1,0:T(8,128)(2,1)S(1)}, u32[]{:S(2)}, u32[]{:S(2)}) collective-permute-start(bf16[1536,128]{1,0:T(8,128)(2,1)S(1)} %get-tuple-element.58), channel_id=1, source_target_pairs={{0,1},{1,0},{2,3},{3,2},{4,5},{5,4},{6,7},{7,6},{8,9},{9,8},{10,11... | collective-permute-start | bytes 1179656 | tf_op jit(solution)/shard_map/ppermute | solution.py:607
  52.4 2.8 %collective-permute-start.4 = (bf16[3072,128]{1,0:T(8,128)(2,1)S(1)}, bf16[3072,128]{1,0:T(8,128)(2,1)S(1)}, u32[]{:S(2)}, u32[]{:S(2)}) collective-permute-start(bf16[3072,128]{1,0:T(8,128)(2,1)S(1)} %get-tuple-element.49), channel_id=1, source_target_pairs={{0,1},{1,0},{2,3},{3,2},{4,5},{5,4},{6,7},{7,6},{8,9},{9,8},{10,11... | collective-permute-start | bytes 2359304 | tf_op jit(solution)/shard_map/ppermute | solution.py:607
  104.3 5.4 %collective-permute-start.10 = (bf16[64,72,128]{2,1,0:T(8,128)(2,1)S(1)}, bf16[64,72,128]{2,1,0:T(8,128)(2,1)S(1)}, u32[]{:S(2)}, u32[]{:S(2)}) collective-permute-start(bf16[64,72,128]{2,1,0:T(8,128)(2,1)S(1)} %all_to_all.11.total), channel_id=1, source_target_pairs={{0,1},{1,0},{2,3},{3,2},{4,5},{5,4},{6,7},{7,6},{8,9},{9,8},{10,11... | collective-permute-start | bytes 3538952 | tf_op jit(solution)/shard_map/ppermute | solution.py:607

commit v4 on v3

--- a/solution.py
+++ b/solution.py
@@ -12,10 +12,11 @@
 BF16 = jnp.bfloat16
 MIB = 1024 * 1024
 VM = pl.BlockSpec(memory_space=pltpu.VMEM)
+SM = pl.BlockSpec(memory_space=pltpu.SMEM)
 HB = pl.BlockSpec(memory_space=pltpu.HBM)
 FACTOR = 1.0 / math.sqrt(64 * 256 * 8)
 CHUNK = 72
-ROWS_A, ROWS_B = 6144, 3072
+ROWS_F, ROWS_C, ROWS_B = 1296, 1728, 1296
 
 
 def call(kernel, outs, ins, scratch=(), flops=0, limit=58, aliases=None):
@@ -75,7 +76,7 @@
     low = lax.broadcasted_iota(jnp.int32, (count, 8, 128), 2) < 64
     two = jnp.where(low, v[:count], v[1 : count + 1])
     ref[at, :, :128] = two.reshape(count * 8, 128).astype(BF16)
-    ref[at, :, 128:] = v[2 : count + 2].reshape(count * 8, 128).astype(BF16)[:, :64]
+    ref[at, :, 128:] = v[2 : count + 2].reshape(count * 8, 128).astype(BF16)
 
 
 def taps_z(g):
@@ -106,9 +107,14 @@
     return act, lambda: sigma + act * (1.0 - sigma)
 
 
-W1, W2, W3, W4L, W4E, W5L, W5S, WF = 0, 768, 1344, 2496, 4032, 4800, 6336, 7104
+def own(at, first, count):
+    return jnp.where(jnp.logical_and(at >= first, at < first + count), at - first, count)
+
+
+W1, W2, W3, W4L, W4E, W5L, W5S, WF = 0, 768, 1536, 2688, 4224, 4992, 6528, 7296
 W6, W7, WB = 0, 1152, 2304
 LIFT, SKIP, GRAD, COARSE, KEPT = 0, 864, 1728, 2448, 2832
+SPARE = 2832
 ROOM = 51200
 
 
@@ -187,7 +193,7 @@
 def forward(
     xall, xmask, r3, r4, weights_hbm,
     decoded_hbm, slope_ef, g_skip, slope_ec, g_dc, s_in, s_pool, kept_hbm,
-    mm, cc, s1, ee, s2, s3, slope_dc, s4, acc, acc1, weights, kept, decoded, w_sem, out_sem,
+    mm, cc, s1, ee, s2, s3, slope_dc, s4, acc, weights, kept, decoded, w_sem, out_sem,
 ):
     cuts = (W1, W2, W3, W4L, W4E, W5L, W5S, WF)
     loads = []
@@ -228,33 +234,20 @@
         v = jnp.concatenate([lo(at, 64), xall[i].astype(F32).reshape(16, 8, 128), hi(at, 64)], axis=0)
         s1[i] = taps_y(v[1:31], 28)
 
-        @pl.when(jnp.logical_and(i >= 3, i < 8))
-        def _():
-            s_in[i - 3] = taps_y(v[7:25], 16)
-
+        s_in[own(i, 3, 5)] = taps_y(v[7:25], 16)
         return 0
 
     lax.fori_loop(0, 11, spread, 0)
 
     loads[0].wait()
 
-    def encode_dots(i, _):
-        wide = jnp.concatenate([s1[pl.ds(5 * i, 5)], s1[pl.ds(5 * i + 1, 5)]], axis=2)
-        acc1[pl.ds(pl.multiple_of(1120 * i, 1120), 1120)] = dot(wide.reshape(1120, 768), weights[W1:W2])
-        return 0
-
-    lax.fori_loop(0, 2, encode_dots, 0)
-
-    def encode(i, _):
-        pre = fold128(acc1[pl.ds(pl.multiple_of(224 * i, 224), 224)])
+    def encode(i, pre):
         mask = mm[jnp.where(i < 3, 0, jnp.where(i < 7, 1, 2))]
         act, slope = silu_parts(pre)
         v = bround(act * mask)
         ee[i] = v
 
-        @pl.when(jnp.logical_and(i >= 3, i < 7))
-        def _():
-            slope_ef[i - 3] = (slope() * mask)[6:22].reshape(128, 128)
+        slope_ef[own(i, 3, 4)] = (slope() * mask)[6:22].reshape(128, 128)
 
         s = v.reshape(14, 2, 8, 128)
         s = s[:, 0] + s[:, 1]
@@ -262,13 +255,16 @@
         v = bround(halve_z(s) * 0.125)
         put_taps(s2, i, v, 12)
 
-        @pl.when(jnp.logical_and(i >= 2, i < 8))
-        def _():
-            put_taps(s_pool, i - 2, v[2:12], 8)
-
+        put_taps(s_pool, own(i, 2, 6), v[2:12], 8)
+
+    def encode_two(j, _):
+        wide = jnp.concatenate([s1[pl.ds(2 * j, 2)], s1[pl.ds(2 * j + 1, 2)]], axis=2).reshape(448, 768)
+        pre = fold128(dot(wide, weights[W1:W2])).reshape(2, 28, 8, 128)
+        for k in range(2):
+            encode(2 * j + k, pre[k])
         return 0
 
-    lax.fori_loop(0, 10, encode, 0)
+    lax.fori_loop(0, 5, encode_two, 0, unroll=True)
 
     def mask_coarse(block, first, count):
         m = mm[block].reshape(14, 2, 8, 128)[first : first + count, 0]
@@ -277,10 +273,8 @@
     loads[1].wait()
 
     def encode2(i, _):
-        pre = jnp.zeros((384, 384), F32)
-        for a in range(3):
-            pre += dot(s2[pl.ds(4 * i + a, 4)].reshape(384, 192), weights[W2 + 192 * a : W2 + 192 * a + 192])
-        pre = fold128(pre).reshape(4, 12, 8, 128)
+        wide = jnp.concatenate([s2[pl.ds(4 * i + a, 4)] for a in range(3)], axis=2).reshape(384, 768)
+        pre = fold128(dot(wide, weights[W2:W3])).reshape(4, 12, 8, 128)
         for k in range(4):
             x = 4 * i + k
             mask = mask_coarse(jnp.where(x < 2, 0, jnp.where(x < 6, 1, 2)), 1, 12)
@@ -288,22 +282,17 @@
             v = bround(act * mask)
             s3[x] = taps_y(v, 10)
 
-            @pl.when(jnp.logical_and(x >= 1, x < 7))
-            def _():
-                slope_ec[x - 1] = (slope() * mask)[1:11].reshape(80, 128)
-                kept[pl.ds(pl.multiple_of(COARSE + 64 * (x - 1), 64), 64)] = taps_y(v[1:11], 8)
-
+            slope_ec[own(x, 1, 6)] = (slope() * mask)[1:11].reshape(80, 128)
+            kept[pl.ds(pl.multiple_of(COARSE + 64 * own(x, 1, 6), 16), 64)] = taps_y(v[1:11], 8)
         return 0
 
-    lax.fori_loop(0, 2, encode2, 0)
+    lax.fori_loop(0, 2, encode2, 0, unroll=True)
     store(COARSE, KEPT)
     loads[2].wait()
 
     def decode2(i, _):
-        pre = jnp.zeros((240, 384), F32)
-        for a in range(3):
-            pre += dot(s3[pl.ds(3 * i + a, 3)].reshape(240, 384), weights[W3 + 384 * a : W3 + 384 * a + 384])
-        pre = fold128(pre).reshape(3, 10, 8, 128)
+        wide = jnp.concatenate([s3[pl.ds(3 * i + a, 3)] for a in range(3)], axis=2).reshape(240, 1152)
+        pre = fold128(dot(wide, weights[W3:W4L])).reshape(3, 10, 8, 128)
         for k in range(3):
             x = 3 * i + k
             mask = mask_coarse(jnp.where(x < 1, 0, jnp.where(x < 5, 1, 2)), 2, 10)
@@ -312,19 +301,16 @@
             up = jnp.concatenate([v[:, None], v[:, None]], axis=1).reshape(20, 8, 128)
             kept[pl.ds(pl.multiple_of(LIFT + 144 * x, 144), 144)] = taps_y(up, 18)
 
-            @pl.when(jnp.logical_and(x >= 1, x < 5))
-            def _():
-                slope_dc[x - 1] = (slope() * mask)[1:9]
-
+            slope_dc[own(x, 1, 4)] = (slope() * mask)[1:9]
         return 0
 
-    lax.fori_loop(0, 2, decode2, 0)
+    lax.fori_loop(0, 2, decode2, 0, unroll=True)
 
     def skip(i, _):
         kept[pl.ds(pl.multiple_of(SKIP + 144 * i, 144), 144)] = taps_y(ee[i + 2, 4:24], 18)
         return 0
 
-    lax.fori_loop(0, 6, skip, 0)
+    lax.fori_loop(0, 6, skip, 0, unroll=True)
 
     store(LIFT, GRAD)
     loads[3].wait()
@@ -336,8 +322,8 @@
         return jnp.concatenate([weights[first : first + 384], weights[first + step : first + step + 384]], axis=1)
 
     lifted = both(LIFT)
-    total = dot_n(lifted, taps(W4L, 768)) + dot_n(lifted, taps(W4L + 384, 768)) + dot_n(both(SKIP), taps(W4E, 384))
-    acc[...] = total
+    wide = jnp.concatenate([lifted, lifted, both(SKIP)], axis=1)
+    acc[...] = dot_n(wide, jnp.concatenate([taps(W4L, 768), taps(W4L + 384, 768), taps(W4E, 384)], axis=1))
 
     def decode(i, _):
         pre = fold128(acc[pl.ds(pl.multiple_of(144 * i, 144), 144)])
@@ -349,25 +335,19 @@
         s4[i] = taps_y(g, 16)
         out = (act * mask)[1:17].reshape(128, 128).astype(BF16)
 
-        @pl.when(i > 0)
-        def _():
-            decoded[2 * i - 1] = out[:, :64]
-
-        @pl.when(i < 4)
-        def _():
-            decoded[2 * i] = out[:, 64:]
-
-        own = jnp.logical_and(jnp.logical_or(lane >= 64, i > 0), jnp.logical_or(lane < 64, i < 4))
-        g = jnp.where(own, g, 0.0)
+        decoded[own(2 * i - 1, 0, 8)] = out[:, :64]
+        decoded[own(2 * i, 0, 8)] = out[:, 64:]
+        inside = jnp.logical_and(jnp.logical_or(lane >= 64, i > 0), jnp.logical_or(lane < 64, i < 4))
+        g = jnp.where(inside, g, 0.0)
         zero = jnp.zeros((1, 8, 128), F32)
         kept[pl.ds(pl.multiple_of(GRAD + 144 * i, 144), 144)] = taps_z(
             jnp.concatenate([zero, g[1:17], zero], axis=0)
         )
         return 0
 
-    lax.fori_loop(0, 5, decode, 0)
+    lax.fori_loop(0, 5, decode, 0, unroll=True)
     store(GRAD, COARSE)
-    stores.append(pltpu.make_async_copy(decoded, decoded_hbm, out_sem.at[3]))
+    stores.append(pltpu.make_async_copy(decoded.at[pl.ds(0, 8)], decoded_hbm, out_sem.at[3]))
     stores[-1].start()
     loads[5].wait()
     loads[6].wait()
@@ -382,7 +362,7 @@
         g_dc[pl.ds(2 * i, 2)] = g.reshape(2, 64, 128).astype(BF16)
         return 0
 
-    lax.fori_loop(0, 2, back, 0)
+    lax.fori_loop(0, 2, back, 0, unroll=True)
     for copy in stores:
         copy.wait()
 
@@ -391,8 +371,8 @@
     return jnp.concatenate([both[:, :64], both[:, 64:]], axis=0)
 
 
-A_LIFT, A_SKIP, A_SKIP2, A_END = 1728, 2592, 2880, 3024
-B_FINE, B_FINE2, B_END = 864, 1152, 1296
+A_SKIP, A_SKIP2 = 864, 1152
+B_FINE, B_FINE2 = 864, 1152
 
 
 def put_parts(wire, first, rows, block):
@@ -411,25 +391,26 @@
         wire[h, at2 : at2 + 48] = jnp.where(lane[:48] < 64, low[:48], high[48:]).astype(BF16)
 
 
-def split_wire(wire, end, keep, send):
-    for h in range(2):
-        wire[h, end:] = jnp.zeros((wire.shape[1] - end, 128), BF16)
+def split_wire(wire, keep, send):
     core = lax.axis_index("core")
     keep[...] = wire[core]
     send[...] = wire[1 - core]
 
 
-def weights_decode(kept_hbm, g_dc, keep, send, wire, kept, sem):
-    copies = []
-    cuts = (LIFT, SKIP, GRAD, COARSE, KEPT)
-    for k in range(4):
-        rows = pl.ds(cuts[k], cuts[k + 1] - cuts[k])
-        copies.append(pltpu.make_async_copy(kept_hbm.at[rows], kept.at[rows], sem.at[k]))
-        copies[-1].start()
+def fetch(kept_hbm, kept, first, end, sem):
+    copy = pltpu.make_async_copy(kept_hbm.at[pl.ds(first, end - first)], kept, sem)
+    copy.start()
+    return copy
+
+
+def weights_fine(kept_hbm, keep, send, token, wire, kept, sem):
+    copies = [
+        fetch(kept_hbm, kept.at[pl.ds(first, end - first)], first, end, sem.at[k])
+        for k, (first, end) in enumerate(((LIFT, SKIP), (SKIP, GRAD), (GRAD, COARSE)))
+    ]
     for copy in copies:
         copy.wait()
     grad = kept[GRAD:COARSE]
-    gc = taps_z(g_dc[...].astype(F32).reshape(32, 8, 128))
     up = [(dot_t(grad, kept[LIFT + 144 * p : LIFT + 144 * p + 720]) * FACTOR).reshape(3, 2, 64, 384) for p in range(2)]
     same = [(dot_t(grad, kept[SKIP + 144 * p : SKIP + 144 * p + 720]) * FACTOR).reshape(3, 2, 64, 384) for p in range(2)]
     for a, (p, q) in enumerate(((0, 0), (0, 1), (1, 0))):
@@ -437,19 +418,28 @@
         lifted = (up[p][:, 0] + up[p2][:, 1]).reshape(192, 384).astype(BF16)
         for b in range(3):
             for c in range(3):
-                at = A_LIFT + 32 * (9 * a + 3 * b + c)
+                at = 32 * (9 * a + 3 * b + c)
                 put_parts(wire, at, 32, lifted[64 * c : 64 * c + 64, 128 * b : 128 * b + 128])
         taps = []
         for b in range(3):
             lanes = slice(128 * b, 128 * b + 128)
             taps.append(add_halves(same[p][:, 0, :, lanes].reshape(192, 128), q, same[p2][:, 1, :, lanes].reshape(192, 128), q2))
         put_three(wire, A_SKIP + 96 * a, A_SKIP2 + 48 * a, taps)
-        res = (dot_t(kept[COARSE + 64 * a : COARSE + 64 * a + 256], gc) * FACTOR).astype(BF16)
+    split_wire(wire, keep, send)
+    token[0, 0] = jnp.int32(0)
+
+
+def weights_coarse(kept_hbm, g_dc, keep, send, wire, kept, sem):
+    copy = fetch(kept_hbm, kept, COARSE, KEPT, sem.at[0])
+    gc = taps_z(g_dc[...].astype(F32).reshape(32, 8, 128))
+    copy.wait()
+    for a in range(3):
+        res = (dot_t(kept[64 * a : 64 * a + 256], gc) * FACTOR).astype(BF16)
         for b in range(3):
             for c in range(3):
                 at = 64 * (9 * a + 3 * b + c)
                 put_parts(wire, at, 64, res[128 * b : 128 * b + 128, 128 * c : 128 * c + 128])
-    split_wire(wire, A_END, keep, send)
+    split_wire(wire, keep, send)
 
 
 def add_halves(first, q, second, q2):
@@ -464,16 +454,16 @@
         return 0
 
     lax.fori_loop(0, 8, spread, 0)
-    acc = jnp.zeros((480, 384), F32)
-    for a in range(3):
-        acc += dot_n(s5[a : a + 6].reshape(480, 384), weights[W6 + 384 * a : W6 + 384 * a + 384])
-    g_ec = bround(fold128(acc) * slope_ec[...].reshape(60, 8, 128)).reshape(6, 10, 8, 128)
+
+    def taps(first):
+        return jnp.concatenate([weights[first + 384 * a : first + 384 * a + 384] for a in range(3)], axis=1)
+
+    acc = dot_n(jnp.concatenate([s5[a : a + 6] for a in range(3)], axis=2).reshape(480, 1152), taps(W6))
+    g_ec = bround(fold128(acc) * slope_ec[0:6].reshape(60, 8, 128)).reshape(6, 10, 8, 128)
     for x in range(6):
         ge[x] = taps_y(g_ec[x], 8)
     gc = taps_z(g_ec[1:5, 1:9].reshape(32, 8, 128))
-    acc = jnp.zeros((256, 384), F32)
-    for a in range(3):
-        acc += dot_n(ge[a : a + 4].reshape(256, 384), weights[W7 + 384 * a : W7 + 384 * a + 384])
+    acc = dot_n(jnp.concatenate([ge[a : a + 4] for a in range(3)], axis=2).reshape(256, 1152), taps(W7))
     up = double_z(fold128(acc) * 0.125)
     up = jnp.concatenate([up[:, None], up[:, None]], axis=1).reshape(4, 16, 8, 128)
     for x in range(4):
@@ -488,20 +478,20 @@
             lanes = slice(128 * c, 128 * c + 128)
             taps.append(add_halves(parts[p][:, q, :, lanes].reshape(192, 128), 0, parts[p2][:, q2, :, lanes].reshape(192, 128), 1))
         put_three(wire, B_FINE + 96 * a, B_FINE2 + 48 * a, taps)
-        res = (dot_t(s_pool[a : a + 4].reshape(256, 192), gc) * FACTOR).astype(BF16)
+        res = (dot_t(s_pool[a : a + 4].reshape(256, 256), gc) * FACTOR).astype(BF16)
         for b in range(3):
             for c in range(3):
                 at = 32 * (9 * a + 3 * b + c)
                 put_parts(wire, at, 32, res[64 * b : 64 * b + 64, 128 * c : 128 * c + 128])
-    split_wire(wire, B_END, keep, send)
+    split_wire(wire, keep, send)
 
 
 def unpack(of_this_core, total, *refs):
     df_hbm, dc_hbm, ef_hbm, ec_hbm, d_df, d_dc, d_ef, d_ec, sem = refs[-9:]
     core = lax.axis_index("core")
     half = core if of_this_core else 1 - core
-    wire_a = total[:, : ROWS_A // 128].reshape(ROWS_A // 2, 128)
-    wire_b = total[:, ROWS_A // 128 :].reshape(ROWS_B // 2, 128)
+    wire = total[...].reshape(64 * CHUNK, 128)
+    wire_a, wire_c, wire_b = wire[:ROWS_F], wire[ROWS_F : ROWS_F + ROWS_C], wire[ROWS_F + ROWS_C :]
     stores = []
 
     def store(src, dst, a):
@@ -517,12 +507,11 @@
 
     for a in range(3):
         taps = slice(9 * a, 9 * a + 9)
-        d_dc[taps] = wire_a[576 * a : 576 * a + 576].astype(F32).reshape(9, 64, 128)
+        d_dc[taps] = wire_c[576 * a : 576 * a + 576].astype(F32).reshape(9, 64, 128)
         store(d_dc, dc_hbm, a)
         skip = three(wire_a, A_SKIP + 96 * a, A_SKIP2 + 48 * a)
         fine = three(wire_b, B_FINE + 96 * a, B_FINE2 + 48 * a)
-        first = A_LIFT + 288 * a
-        d_df[taps, :, :128] = wire_a[first : first + 288].astype(F32).reshape(9, 32, 128)
+        d_df[taps, :, :128] = wire_a[288 * a : 288 * a + 288].astype(F32).reshape(9, 32, 128)
         for b in range(3):
             for c in range(3):
                 k = 9 * a + 3 * b + c
@@ -555,8 +544,17 @@
             for c in range(3):
                 k = 9 * a + 3 * b + c
                 lanes = slice(128 * c, 128 * c + 128)
-                wf[W2 + 192 * a + 64 * b : W2 + 192 * a + 64 * b + 64, lanes] = e2[k]
+                wf[W2 + 256 * a + 64 * b : W2 + 256 * a + 64 * b + 64, lanes] = e2[k]
                 wf[W3 + 384 * a + 128 * b : W3 + 384 * a + 128 * b + 128, lanes] = d3[k]
+        wf[W2 + 256 * a + 192 : W2 + 256 * a + 256] = jnp.zeros((64, 384), BF16)
+    copies = []
+
+    def copy_out(first, rows):
+        at = pl.ds(first, rows)
+        copies.append(pltpu.make_async_copy(wf.at[at], wf_hbm.at[at], sem.at[len(copies)]))
+        copies[-1].start()
+
+    copy_out(W2, W4L - W2)
     none = jnp.zeros((64, 64), F32)
 
     def tap(ref, a, rest, lanes, turned=False):
@@ -593,12 +591,8 @@
                     wf[at : at + 64, 128 * b : 128 * b + 128] = beside(
                         tap(d4, 2 * p - o, rest, high), tap(d4, 2 * p + 1 - o, rest, high)
                     ).astype(BF16)
-    cuts = (W1, W2, W3, W4L, W4E, W5L, W5S, WF)
-    copies = []
-    for k in range(7):
-        rows = pl.ds(cuts[k], cuts[k + 1] - cuts[k])
-        copies.append(pltpu.make_async_copy(wf.at[rows], wf_hbm.at[rows], sem.at[k]))
-        copies[-1].start()
+        for first, rows in ((W1, 384), (W4L, 768), (W4E, 384), (W5L, 384), (W5L + 384, 384), (W5S, 384)):
+            copy_out(first + rows * p if first != W5L + 384 else W5L + 768 + 384 * p, rows)
     for copy in copies:
         copy.wait()
 
@@ -632,7 +626,7 @@
         arrange,
         [((ROOM, 384), BF16, HB)],
         [VM] * 4,
-        scratch=[pltpu.VMEM((WF, 384), BF16), pltpu.SemaphoreType.DMA((7,))],
+        scratch=[pltpu.VMEM((WF, 384), BF16), pltpu.SemaphoreType.DMA((13,))],
     )(encode_fine.reshape(27, 64, 64), e2, d3, d4)
     (w_backward,) = call(arrange_back, [((WB, 384), BF16)], [VM] * 2)(e2, d3)
 
@@ -664,12 +658,12 @@
         forward,
         [
             ((8, 128, 64), BF16, HB),
+            ((5, 128, 128), F32),
             ((4, 128, 128), F32),
-            ((4, 128, 128), F32),
-            ((6, 80, 128), F32),
+            ((7, 80, 128), F32),
             ((4, 64, 128), BF16),
-            ((5, 128, 384), BF16),
-            ((6, 64, 192), BF16),
+            ((6, 128, 384), BF16),
+            ((7, 64, 256), BF16),
             ((ROOM, 384), BF16, HB),
         ],
         [VM] * 4 + [HB],
@@ -678,15 +672,14 @@
             pltpu.VMEM((5, 18, 8, 128), F32),
             pltpu.VMEM((11, 224, 384), BF16),
             pltpu.VMEM((10, 28, 8, 128), F32),
-            pltpu.VMEM((10, 96, 192), BF16),
+            pltpu.VMEM((10, 96, 256), BF16),
             pltpu.VMEM((8, 80, 384), BF16),
-            pltpu.VMEM((4, 8, 8, 128), F32),
+            pltpu.VMEM((5, 8, 8, 128), F32),
             pltpu.VMEM((5, 128, 384), BF16),
             pltpu.VMEM((720, 384), F32),
-            pltpu.VMEM((2240, 384), F32),
             pltpu.VMEM((WF, 384), BF16),
-            pltpu.VMEM((KEPT, 384), BF16),
-            pltpu.VMEM((8, 128, 64), BF16),
+            pltpu.VMEM((SPARE + 64, 384), BF16),
+            pltpu.VMEM((9, 128, 64), BF16),
             pltpu.SemaphoreType.DMA((7,)),
             pltpu.SemaphoreType.DMA((4,)),
         ],
@@ -695,7 +688,32 @@
     )(xall, xmask, r3, r4, w_forward)
 
     def add(keep, got):
-        return (keep.astype(F32) + got.astype(F32)).astype(BF16).reshape(64, -1, 128)
+        return (keep.astype(F32) + got.astype(F32)).astype(BF16)
+
+    keep_f, send_f, token = call(
+        weights_fine,
+        [((ROWS_F, 128), BF16), ((ROWS_F, 128), BF16), ((1, 1), jnp.int32, SM)],
+        [HB],
+        scratch=[
+            pltpu.VMEM((2, ROWS_F, 128), BF16),
+            pltpu.VMEM((COARSE, 384), BF16),
+            pltpu.SemaphoreType.DMA((3,)),
+        ],
+        flops=1_000_000_000,
+        limit=26,
+    )(kept)
+    keep_c, send_c = call(
+        weights_coarse,
+        [((ROWS_C, 128), BF16)] * 2,
+        [HB, VM],
+        scratch=[
+            pltpu.VMEM((2, ROWS_C, 128), BF16),
+            pltpu.VMEM((KEPT - COARSE, 384), BF16),
+            pltpu.SemaphoreType.DMA((1,)),
+        ],
+        flops=300_000_000,
+        limit=26,
+    )(kept, g_dc)
 
     is_odd = odd_r == 1
     q1 = swap(jnp.where(is_odd, g_dc[:2], g_dc[2:]), swap_z)
@@ -704,6 +722,7 @@
     before = jnp.where(row > 0, jnp.where(is_odd, q1, q2), zero)
     after = jnp.where(row < 7, jnp.where(is_odd, q2, q1), zero)
     gx = jnp.concatenate([before, g_dc, after], axis=0)
+    odd_c, token = lax.optimization_barrier((odd_c, token))
     is_odd = odd_c == 1
     q3 = swap(jnp.where(is_odd, gx[:, :16], gx[:, 48:]), swap_core)
     q4 = swap(jnp.where(is_odd, gx[:, 48:], gx[:, :16]), swap_yz)
@@ -711,39 +730,26 @@
     before = jnp.where(col > 0, jnp.where(is_odd, q3, q4), zero)
     after = jnp.where(col < 15, jnp.where(is_odd, q4, q3), zero)
     gx = jnp.concatenate([before, gx, after], axis=1)
-
-    keep_a, send_a = call(
-        weights_decode,
-        [((ROWS_A // 2, 128), BF16)] * 2,
-        [HB, VM],
-        scratch=[
-            pltpu.VMEM((2, ROWS_A // 2, 128), BF16),
-            pltpu.VMEM((KEPT, 384), BF16),
-            pltpu.SemaphoreType.DMA((4,)),
-        ],
-        flops=1_000_000_000,
-        limit=26,
-    )(kept, g_dc)
-    half_a = add(keep_a, swap(send_a, swap_core))
-    gx, keep_a = lax.optimization_barrier((gx, keep_a))
+    gx, keep_c = lax.optimization_barrier((gx, keep_c))
+
 
     keep_b, send_b = call(
         back_encode,
-        [((ROWS_B // 2, 128), BF16)] * 2,
+        [((ROWS_B, 128), BF16)] * 2,
         [VM] * 7,
         scratch=[
             pltpu.VMEM((8, 80, 384), BF16),
             pltpu.VMEM((6, 64, 384), BF16),
             pltpu.VMEM((4, 128, 384), BF16),
-            pltpu.VMEM((2, ROWS_B // 2, 128), BF16),
+            pltpu.VMEM((2, ROWS_B, 128), BF16),
         ],
         flops=500_000_000,
         limit=20,
     )(gx, slope_ec, s_pool, s_in, g_skip, slope_ef, w_backward)
-    half_b = add(keep_b, swap(send_b, swap_core))
+    sums = [add(keep, swap(send, swap_core)) for keep, send in ((keep_f, send_f), (keep_c, send_c), (keep_b, send_b))]
 
     chips = ("row", "colh")
-    half = jnp.concatenate([half_a, half_b], axis=1)
+    half = jnp.pad(jnp.concatenate(sums, axis=0), ((0, 64 * CHUNK - 4320), (0, 0))).reshape(64, CHUNK, 128)
     terms = lax.all_to_all(half, chips, 0, 0, tiled=True)
     total = jnp.sum(terms.astype(F32), axis=0).astype(BF16)
     mine = lax.all_to_all(jnp.broadcast_to(total[None], (64, CHUNK, 128)), chips, 0, 0, tiled=True)

time: 112 us -> 108 us (0.964)
  Pallas kernels: 31.2 us -> 27.9 us
  blocking collectives: 48.4 us -> 46.7 us
  starting transfers between devices: 22.5 us -> 24.1 us
    pallas_call x3 -> x4, Pallas kernels: 17.8 us -> 15.3 us  [the longest x1 8.44 us: body(): call(forward, [((8, 128, 64), BF16, HB), ((5, 128, 128), F32), ((4, 128,...]
    ppermute x11 -> x12, starting transfers between devices: 22.5 us -> 24.1 us  [swap(): return lax.ppermute(v, ('row', 'colh', 'core'), pairs)]
    all_to_all x1, blocking collectives: 25.6 us -> 24.3 us  [body(): terms = lax.all_to_all(half, chips, 0, 0, tiled=True)]
    ppermute x11 -> x12, waiting for transfers between devices: 7.6 us -> 6.79 us  [swap(): return lax.ppermute(v, ('row', 'colh', 'core'), pairs)]
  transfers between devices with their start and end apart: 11 -> 12, of which waited for: 5 -> 4; matrix products, arithmetic and copies ran while one was open for 0% -> 0% of each run, Pallas kernels for 12% -> 15%
where the time goes in v4:
time: 108 us; the launch traced here: 107 us
  blocking collectives  46.7 us (43%)
  Pallas kernels  27.9 us (26%)
  starting transfers between devices  24.1 us (22%)
  waiting for transfers between devices  6.79 us (6%)
    all_to_all x1, blocking collectives, body(): terms = lax.all_to_all(half, chips, 0, 0, tiled=True)  24.3 us
    ppermute x12, starting transfers between devices, swap(): return lax.ppermute(v, ('row', 'colh', 'core'), pairs)  24.1 us
    all_to_all x1, blocking collectives, body(): lax.all_to_all(jnp.broadcast_to(total[None], (64, CHUNK, 128)), chips, 0,...  22.5 us
    pallas_call x1, Pallas kernels, body(): call(forward, [((8, 128, 64), BF16, HB), ((5, 128, 128), F32), ((4, 128,...  8.44 us
    ppermute x12, waiting for transfers between devices, swap(): return lax.ppermute(v, ('row', 'colh', 'core'), pairs)  6.79 us
    pallas_call x1, Pallas kernels, body(): call(arrange, [((ROOM, 384), BF16, HB)], [VM] * 4, scratch=[pltpu.VMEM((W...  4.49 us
    pallas_call x2, Pallas kernels, body(): call(functools.partial(unpack, of_this_core), [(shape, F32, HB) for shape...  3.26 us
    pallas_call x1, Pallas kernels, body(): call(weights_fine, [((ROWS_F, 128), BF16), ((ROWS_F, 128), BF16), ((1, 1)...  3.05 us
  transfers between devices with their start and end apart: 12, of which 4 were waited for; matrix products, arithmetic and copies ran while one was open for 0% of the time, Pallas kernels for 15%

profile of v4, /device:TPU:1, one launch (start us, length us, event | category | flops | bytes accessed | tf_op | source)
XLA Modules:
  0.0 107.3 jit_solution(11852716040769852187)
XLA Ops:
  0.6 1.8 %shard_map.110 = (bf16[528,128]{1,0:T(8,128)(2,1)}, bf16[528,128]{1,0:T(8,128)(2,1)}) custom-call(s32[2]{0:T(128)} %bitcast.31, bf16[8,128,64]{2,1,0:T(8,128)(2,1)} %bitcast.30, bf16[8,128,64]{2,1,0:T(8,128)(2,1)} %bitcast.17), custom_call_target="tpu_custom_call" | custom-call | bytes 4000000 | tf_op jit(solution)/shard_map/pallas_call | solution.py:635
  2.5 2.5 %collective-permute-start = (bf16[528,128]{1,0:T(8,128)(2,1)}, bf16[528,128]{1,0:T(8,128)(2,1)S(1)}, u32[]{:S(2)}, u32[]{:S(2)}) collective-permute-start(bf16[528,128]{1,0:T(8,128)(2,1)} %get-tuple-element.39.p1), channel_id=1, source_target_pairs={{0,16},{1,17},{2,18},{3,19},{4,20},{5,21},{6,22},{7,23},{8,24},{9,... | collective-permute-start | bytes 405512 | tf_op jit(solution)/shard_map/ppermute | solution.py:601
  5.0 2.3 %collective-permute-start.1 = (bf16[528,128]{1,0:T(8,128)(2,1)}, bf16[528,128]{1,0:T(8,128)(2,1)S(1)}, u32[]{:S(2)}, u32[]{:S(2)}) collective-permute-start(bf16[528,128]{1,0:T(8,128)(2,1)} %get-tuple-element.40.p2), channel_id=1, source_target_pairs={{0,112},{1,113},{2,114},{3,115},{4,116},{5,117},{6,118},{7,119},{8... | collective-permute-start | bytes 405512 | tf_op jit(solution)/shard_map/ppermute | solution.py:601
  7.3 4.5 %shard_map.111.weights_hbm = bf16[51200,384]{1,0:T(8,128)(2,1)} custom-call(bf16[27,64,64]{2,1,0:T(8,128)(2,1)} %bitcast.29, bf16[27,64,128]{2,1,0:T(8,128)(2,1)} %bitcast.22, bf16[27,128,128]{2,1,0:T(8,128)(2,1)} %bitcast.20, bf16[27,64,192]{2,1,0:T(8,128)(2,1)} %bitcast.28), custom_call_target="tpu_custom_call" | custom-call | bytes 4000000 | tf_op jit(solution)/shard_map/pallas_call | solution.py:625
  11.8 0.3 shard_map.112
  12.1 1.6 %collective-permute-start.2 = (bf16[768,128]{1,0:T(8,128)(2,1)S(1)}, bf16[768,128]{1,0:T(8,128)(2,1)S(1)}, u32[]{:S(2)}, u32[]{:S(2)}) collective-permute-start(bf16[768,128]{1,0:T(8,128)(2,1)S(1)} %get-tuple-element.44), channel_id=1, source_target_pairs={{0,1},{1,0},{2,3},{3,2},{4,5},{5,4},{6,7},{7,6},{8,9},{9,8},{10,11... | collective-permute-start | bytes 589832 | tf_op jit(solution)/shard_map/ppermute | solution.py:601
  13.7 3.3 %collective-permute-start.3 = (bf16[768,128]{1,0:T(8,128)(2,1)S(1)}, bf16[768,128]{1,0:T(8,128)(2,1)S(1)}, u32[]{:S(2)}, u32[]{:S(2)}) collective-permute-start(bf16[768,128]{1,0:T(8,128)(2,1)S(1)} %get-tuple-element.46), channel_id=1, source_target_pairs={{0,15},{1,2},{2,1},{3,4},{4,3},{5,6},{6,5},{7,8},{8,7},{9,10},{10,... | collective-permute-start | bytes 589832 | tf_op jit(solution)/shard_map/ppermute | solution.py:601
  16.9 2.8 %shard_map.113.weights = bf16[2304,384]{1,0:T(8,128)(2,1)} custom-call(bf16[27,64,128]{2,1,0:T(8,128)(2,1)} %bitcast.23, bf16[27,128,128]{2,1,0:T(8,128)(2,1)} %bitcast.21), custom_call_target="tpu_custom_call" | custom-call | bytes 4000000 | tf_op jit(solution)/shard_map/pallas_call | solution.py:631
  19.7 1.9 %collective-permute-done.3.r4 = bf16[768,128]{1,0:T(8,128)(2,1)S(1)} collective-permute-done((bf16[768,128]{1,0:T(8,128)(2,1)S(1)}, bf16[768,128]{1,0:T(8,128)(2,1)S(1)}, u32[]{:S(2)}, u32[]{:S(2)}) %collective-permute-start.3) | collective-permute-done | bytes 196640 | tf_op jit(solution)/shard_map/ppermute | solution.py:601
  21.7 8.4 %shard_map.114 = (bf16[8,128,64]{2,1,0:T(8,128)(2,1)}, f32[5,128,128]{2,1,0:T(8,128)S(1)}, f32[4,128,128]{2,1,0:T(8,128)S(1)}, f32[7,80,128]{2,1,0:T(8,128)S(1)}...) custom-call(bf16[16,128,128]{2,1,0:T(8,128)(2,1)S(1)} %get-tuple-ele, ...), custom_call_target="tpu_custom_call" | custom-call | flops 4000000000 | bytes 4000000 | tf_op jit(solution)/shard_map/pallas_call | solution.py:657
  30.1 1.6 %collective-permute-start.5 = (bf16[2,64,128]{2,1,0:T(8,128)(2,1)S(1)}, bf16[2,64,128]{2,1,0:T(8,128)(2,1)S(1)}, u32[]{:S(2)}, u32[]{:S(2)}) collective-permute-start(bf16[2,64,128]{2,1,0:T(8,128)(2,1)S(1)} %get-tuple-element.80), channel_id=1, source_target_pairs={{0,16},{1,17},{2,18},{3,19},{4,20},{5,21},{6,22},{7,23},{8,24},{9,... | collective-permute-start | bytes 98312 | tf_op jit(solution)/shard_map/ppermute | solution.py:601
  31.7 2.3 %collective-permute-start.6 = (bf16[2,64,128]{2,1,0:T(8,128)(2,1)S(1)}, bf16[2,64,128]{2,1,0:T(8,128)(2,1)S(1)}, u32[]{:S(2)}, u32[]{:S(2)}) collective-permute-start(bf16[2,64,128]{2,1,0:T(8,128)(2,1)S(1)} %get-tuple-element.81), channel_id=1, source_target_pairs={{0,112},{1,113},{2,114},{3,115},{4,116},{5,117},{6,118},{7,119},{8... | collective-permute-start | bytes 98312 | tf_op jit(solution)/shard_map/ppermute | solution.py:601
  34.0 2.6 %collective-permute-done.6 = bf16[2,64,128]{2,1,0:T(8,128)(2,1)S(1)} collective-permute-done((bf16[2,64,128]{2,1,0:T(8,128)(2,1)S(1)}, bf16[2,64,128]{2,1,0:T(8,128)(2,1)S(1)}, u32[]{:S(2)}, u32[]{:S(2)}) %collective-permute-start.6) | collective-permute-done | bytes 32800 | tf_op jit(solution)/shard_map/ppermute | solution.py:601
  36.7 4.8 %collective-permute-start.8 = (bf16[8,16,128]{2,1,0:T(8,128)(2,1)S(1)}, bf16[8,16,128]{2,1,0:T(8,128)(2,1)S(1)}, u32[]{:S(2)}, u32[]{:S(2)}) collective-permute-start(bf16[8,16,128]{2,1,0:T(8,128)(2,1)S(1)} %broadcast_select_fusion.2), channel_id=1, source_target_pairs={{0,15},{1,2},{2,1},{3,4},{4,3},{5,6},{6,5},{7,8},{8,7},{9,10},{10,... | collective-permute-start | bytes 98312 | tf_op jit(solution)/shard_map/ppermute | solution.py:601
  41.4 1.4 %collective-permute-start.7 = (bf16[8,16,128]{2,1,0:T(8,128)(2,1)S(1)}, bf16[8,16,128]{2,1,0:T(8,128)(2,1)S(1)}, u32[]{:S(2)}, u32[]{:S(2)}) collective-permute-start(bf16[8,16,128]{2,1,0:T(8,128)(2,1)S(1)} %get-tuple-element.73), channel_id=1, source_target_pairs={{0,1},{1,0},{2,3},{3,2},{4,5},{5,4},{6,7},{7,6},{8,9},{9,8},{10,11... | collective-permute-start | bytes 98312 | tf_op jit(solution)/shard_map/ppermute | solution.py:601
  42.9 3.0 %shard_map.115 = (bf16[1296,128]{1,0:T(8,128)(2,1)S(1)}, bf16[1296,128]{1,0:T(8,128)(2,1)S(1)}, s32[1,1]{1,0:T(1,128)}) custom-call(bf16[51200,384]{1,0:T(8,128)(2,1)} %get-tuple-element.49.kept_hbm), custom_call_target="tpu_custom_call" | custom-call | flops 1000000000 | bytes 4000000 | tf_op jit(solution)/shard_map/pallas_call | solution.py:693
  46.0 1.6 %shard_map.116 = (bf16[1728,128]{1,0:T(8,128)(2,1)S(1)}, bf16[1728,128]{1,0:T(8,128)(2,1)S(1)}) custom-call(bf16[51200,384]{1,0:T(8,128)(2,1)} %get-tuple-element.49.kept_hbm, bf16[4,64,128]{2,1,0:T(8,128)(2,1)S(1)} %get-tuple-element.52.g_dc), custom_call_target="tpu_custom_call" | custom-call | flops 300000000 | bytes 4000000 | tf_op jit(solution)/shard_map/pallas_call | solution.py:705
  47.7 0.6 collective-permute-start.9
  48.4 2.2 %shard_map.117 = (bf16[1296,128]{1,0:T(8,128)(2,1)S(1)}, bf16[1296,128]{1,0:T(8,128)(2,1)S(1)}) custom-call(bf16[8,96,128]{2,1,0:T(8,128)(2,1)S(1)} %pad_maximum_fusion.gx, f32[7,80,128]{2,1,0:T(8,128)S(1)} %get-tuple-element.57.slope_ec, bf16[7,64,256]{2,1,0:T(8,128)(2,1)S(1)} %get-tuple-element.58.s_pool, bf16[6,128,384]{2,1,0:T(8,128)(2,1)S(1)} %get-tuple-element.59.s_in, ...), custom_call_target="tpu_custom_call" | custom-call | flops 500000000 | bytes 4000000 | tf_op jit(solution)/shard_map/pallas_call | solution.py:736
  50.6 0.2 collective-permute-start.10
  50.8 0.1 add_convert_fusion.2
  50.9 1.4 %collective-permute-done.10 = bf16[1296,128]{1,0:T(8,128)(2,1)S(1)} collective-permute-done((bf16[1296,128]{1,0:T(8,128)(2,1)S(1)}, bf16[1296,128]{1,0:T(8,128)(2,1)S(1)}, u32[]{:S(2)}, u32[]{:S(2)}) %collective-permute-start.10) | collective-permute-done | bytes 331808 | tf_op jit(solution)/shard_map/ppermute | solution.py:601
  52.3 0.1 add_convert_fusion.1
  52.4 0.1 add_convert_fusion
  52.6 24.3 %all_to_all.10 = bf16[64,72,128]{2,1,0:T(8,128)(2,1)S(1)} all-to-all(bf16[64,72,128]{2,1,0:T(8,128)(2,1)S(1)} %bitcast.19), channel_id=1, replica_groups=mesh['row'=8,'colh'=8,'core'=2] {'row','colh'}, dimensions={0} | all-to-all | bytes 2359296 | tf_op jit(solution)/shard_map/all_to_all | solution.py:753
  76.9 0.2 reduce_sum.12
  77.1 0.2 broadcast_in_dim.14
  77.2 22.5 %all_to_all.11.total = bf16[64,72,128]{2,1,0:T(8,128)(2,1)S(1)} all-to-all(bf16[64,72,128]{2,1,0:T(8,128)(2,1)S(1)} %broadcast_in_dim.14), channel_id=1, replica_groups=mesh['row'=8,'colh'=8,'core'=2] {'row','colh'}, dimensions={0} | all-to-all | bytes 2359296 | tf_op jit(solution)/shard_map/all_to_all | solution.py:755
  99.7 3.4 %collective-permute-start.11 = (bf16[64,72,128]{2,1,0:T(8,128)(2,1)S(1)}, bf16[64,72,128]{2,1,0:T(8,128)(2,1)S(1)}, u32[]{:S(2)}, u32[]{:S(2)}) collective-permute-start(bf16[64,72,128]{2,1,0:T(8,128)(2,1)S(1)} %all_to_all.11.total), channel_id=1, source_target_pairs={{0,1},{1,0},{2,3},{3,2},{4,5},{5,4},{6,7},{7,6},{8,9},{9,8},{10,11... | collective-permute-start | bytes 3538952 | tf_op jit(solution)/shard_map/ppermute | solution.py:601
  103.1 1.6 %shard_map.118 = (f32[27,64,192]{2,1,0:T(8,128)}, f32[27,128,128]{2,1,0:T(8,128)}, f32[27,64,64]{2,1,0:T(8,128)}, f32[27,64,128]{2,1,0:T(8,128)}) custom-call(bf16[64,72,128]{2,1,0:T(8,128)(2,1)S(1)} %all_to_all.11.total), custom_call_target="tpu_custom_call" | custom-call | bytes 4000000 | tf_op jit(solution)/shard_map/pallas_call | solution.py:761
  104.7 0.8 collective-permute-done.11.total
  105.5 1.6 %shard_map.119 = (f32[27,64,192]{2,1,0:T(8,128)}, f32[27,128,128]{2,1,0:T(8,128)}, f32[27,64,64]{2,1,0:T(8,128)}, f32[27,64,128]{2,1,0:T(8,128)}) custom-call(bf16[64,72,128]{2,1,0:T(8,128)(2,1)S(1)} %collective-permute-done.11.total, ...), custom_call_target="tpu_custom_call", output_to_operand_aliasing={{0}: (1, {}), {1}: (2, {}), {2}: (3, {}), {3}: (4, {})} | custom-call | bytes 4000000 | tf_op jit(solution)/shard_map/pallas_call | solution.py:761
  (24 shorter events, 0.3 us)
Async XLA Ops:
  2.5 9.3 %collective-permute-start = (bf16[528,128]{1,0:T(8,128)(2,1)}, bf16[528,128]{1,0:T(8,128)(2,1)S(1)}, u32[]{:S(2)}, u32[]{:S(2)}) collective-permute-start(bf16[528,128]{1,0:T(8,128)(2,1)} %get-tuple-element.39.p1), channel_id=1, source_target_pairs={{0,16},{1,17},{2,18},{3,19},{4,20},{5,21},{6,22},{7,23},{8,24},{9,... | collective-permute-start | bytes 405512 | tf_op jit(solution)/shard_map/ppermute | solution.py:601
  5.0 6.8 %collective-permute-start.1 = (bf16[528,128]{1,0:T(8,128)(2,1)}, bf16[528,128]{1,0:T(8,128)(2,1)S(1)}, u32[]{:S(2)}, u32[]{:S(2)}) collective-permute-start(bf16[528,128]{1,0:T(8,128)(2,1)} %get-tuple-element.40.p2), channel_id=1, source_target_pairs={{0,112},{1,113},{2,114},{3,115},{4,116},{5,117},{6,118},{7,119},{8... | collective-permute-start | bytes 405512 | tf_op jit(solution)/shard_map/ppermute | solution.py:601
  7.3 4.5 %copy-start.1 = (bf16[8,16,8,64]{3,2,1,0:T(8,128)(2,1)S(1)}, bf16[8,16,8,64]{3,2,1,0:T(8,128)(2,1)}, u32[]{:S(2)}) copy-start(bf16[8,16,8,64]{3,2,1,0:T(8,128)(2,1)} %param.13) | copy-start | bytes 393220
  7.3 4.5 %copy-start.2 = (bf16[528,128]{1,0:T(8,128)(2,1)S(1)}, bf16[528,128]{1,0:T(8,128)(2,1)}, u32[]{:S(2)}) copy-start(bf16[528,128]{1,0:T(8,128)(2,1)} %get-tuple-element.39.p1) | copy-start | bytes 405508
  7.3 4.5 %copy-start.3 = (bf16[528,128]{1,0:T(8,128)(2,1)S(1)}, bf16[528,128]{1,0:T(8,128)(2,1)}, u32[]{:S(2)}) copy-start(bf16[528,128]{1,0:T(8,128)(2,1)} %get-tuple-element.40.p2) | copy-start | bytes 405508
  12.1 7.6 %collective-permute-start.2 = (bf16[768,128]{1,0:T(8,128)(2,1)S(1)}, bf16[768,128]{1,0:T(8,128)(2,1)S(1)}, u32[]{:S(2)}, u32[]{:S(2)}) collective-permute-start(bf16[768,128]{1,0:T(8,128)(2,1)S(1)} %get-tuple-element.44), channel_id=1, source_target_pairs={{0,1},{1,0},{2,3},{3,2},{4,5},{5,4},{6,7},{7,6},{8,9},{9,8},{10,11... | collective-permute-start | bytes 589832 | tf_op jit(solution)/shard_map/ppermute | solution.py:601
  13.7 8.0 %collective-permute-start.3 = (bf16[768,128]{1,0:T(8,128)(2,1)S(1)}, bf16[768,128]{1,0:T(8,128)(2,1)S(1)}, u32[]{:S(2)}, u32[]{:S(2)}) collective-permute-start(bf16[768,128]{1,0:T(8,128)(2,1)S(1)} %get-tuple-element.46), channel_id=1, source_target_pairs={{0,15},{1,2},{2,1},{3,4},{4,3},{5,6},{6,5},{7,8},{8,7},{9,10},{10,... | collective-permute-start | bytes 589832 | tf_op jit(solution)/shard_map/ppermute | solution.py:601
  30.1 3.9 %collective-permute-start.5 = (bf16[2,64,128]{2,1,0:T(8,128)(2,1)S(1)}, bf16[2,64,128]{2,1,0:T(8,128)(2,1)S(1)}, u32[]{:S(2)}, u32[]{:S(2)}) collective-permute-start(bf16[2,64,128]{2,1,0:T(8,128)(2,1)S(1)} %get-tuple-element.80), channel_id=1, source_target_pairs={{0,16},{1,17},{2,18},{3,19},{4,20},{5,21},{6,22},{7,23},{8,24},{9,... | collective-permute-start | bytes 98312 | tf_op jit(solution)/shard_map/ppermute | solution.py:601
  31.7 4.9 %collective-permute-start.6 = (bf16[2,64,128]{2,1,0:T(8,128)(2,1)S(1)}, bf16[2,64,128]{2,1,0:T(8,128)(2,1)S(1)}, u32[]{:S(2)}, u32[]{:S(2)}) collective-permute-start(bf16[2,64,128]{2,1,0:T(8,128)(2,1)S(1)} %get-tuple-element.81), channel_id=1, source_target_pairs={{0,112},{1,113},{2,114},{3,115},{4,116},{5,117},{6,118},{7,119},{8... | collective-permute-start | bytes 98312 | tf_op jit(solution)/shard_map/ppermute | solution.py:601
  36.7 11.7 %collective-permute-start.8 = (bf16[8,16,128]{2,1,0:T(8,128)(2,1)S(1)}, bf16[8,16,128]{2,1,0:T(8,128)(2,1)S(1)}, u32[]{:S(2)}, u32[]{:S(2)}) collective-permute-start(bf16[8,16,128]{2,1,0:T(8,128)(2,1)S(1)} %broadcast_select_fusion.2), channel_id=1, source_target_pairs={{0,15},{1,2},{2,1},{3,4},{4,3},{5,6},{6,5},{7,8},{8,7},{9,10},{10,... | collective-permute-start | bytes 98312 | tf_op jit(solution)/shard_map/ppermute | solution.py:601
  41.4 6.9 %collective-permute-start.7 = (bf16[8,16,128]{2,1,0:T(8,128)(2,1)S(1)}, bf16[8,16,128]{2,1,0:T(8,128)(2,1)S(1)}, u32[]{:S(2)}, u32[]{:S(2)}) collective-permute-start(bf16[8,16,128]{2,1,0:T(8,128)(2,1)S(1)} %get-tuple-element.73), channel_id=1, source_target_pairs={{0,1},{1,0},{2,3},{3,2},{4,5},{5,4},{6,7},{7,6},{8,9},{9,8},{10,11... | collective-permute-start | bytes 98312 | tf_op jit(solution)/shard_map/ppermute | solution.py:601
  45.9 2.4 %copy-start = (bf16[2304,384]{1,0:T(8,128)(2,1)S(1)}, bf16[2304,384]{1,0:T(8,128)(2,1)}, u32[]{:S(2)}) copy-start(bf16[2304,384]{1,0:T(8,128)(2,1)} %shard_map.113.weights) | copy-start | bytes 5308420
  45.9 4.8 %collective-permute-start.4 = (bf16[1296,128]{1,0:T(8,128)(2,1)S(1)}, bf16[1296,128]{1,0:T(8,128)(2,1)S(1)}, u32[]{:S(2)}, u32[]{:S(2)}) collective-permute-start(bf16[1296,128]{1,0:T(8,128)(2,1)S(1)} %get-tuple-element.51), channel_id=1, source_target_pairs={{0,1},{1,0},{2,3},{3,2},{4,5},{5,4},{6,7},{7,6},{8,9},{9,8},{10,11... | collective-permute-start | bytes 995336 | tf_op jit(solution)/shard_map/ppermute | solution.py:601
  47.7 4.7 %collective-permute-start.9 = (bf16[1728,128]{1,0:T(8,128)(2,1)S(1)}, bf16[1728,128]{1,0:T(8,128)(2,1)S(1)}, u32[]{:S(2)}, u32[]{:S(2)}) collective-permute-start(bf16[1728,128]{1,0:T(8,128)(2,1)S(1)} %get-tuple-element.55), channel_id=1, source_target_pairs={{0,1},{1,0},{2,3},{3,2},{4,5},{5,4},{6,7},{7,6},{8,9},{9,8},{10,11... | collective-permute-start | bytes 1327112 | tf_op jit(solution)/shard_map/ppermute | solution.py:601
  50.6 1.7 %collective-permute-start.10 = (bf16[1296,128]{1,0:T(8,128)(2,1)S(1)}, bf16[1296,128]{1,0:T(8,128)(2,1)S(1)}, u32[]{:S(2)}, u32[]{:S(2)}) collective-permute-start(bf16[1296,128]{1,0:T(8,128)(2,1)S(1)} %get-tuple-element.64), channel_id=1, source_target_pairs={{0,1},{1,0},{2,3},{3,2},{4,5},{5,4},{6,7},{7,6},{8,9},{9,8},{10,11... | collective-permute-start | bytes 995336 | tf_op jit(solution)/shard_map/ppermute | solution.py:601
  99.7 5.8 %collective-permute-start.11 = (bf16[64,72,128]{2,1,0:T(8,128)(2,1)S(1)}, bf16[64,72,128]{2,1,0:T(8,128)(2,1)S(1)}, u32[]{:S(2)}, u32[]{:S(2)}) collective-permute-start(bf16[64,72,128]{2,1,0:T(8,128)(2,1)S(1)} %all_to_all.11.total), channel_id=1, source_target_pairs={{0,1},{1,0},{2,3},{3,2},{4,5},{5,4},{6,7},{7,6},{8,9},{9,8},{10,11... | collective-permute-start | bytes 3538952 | tf_op jit(solution)/shard_map/ppermute | solution.py:601

commit v5 on v4

--- a/solution.py
+++ b/solution.py
@@ -200,7 +200,7 @@
     for k in range(7):
         rows = pl.ds(cuts[k], cuts[k + 1] - cuts[k])
         loads.append(pltpu.make_async_copy(weights_hbm.at[rows], weights.at[rows], w_sem.at[k]))
-        loads[-1].start()
+    loads[0].start()
     stores = []
 
     def store(first, end):
@@ -237,7 +237,9 @@
         s_in[own(i, 3, 5)] = taps_y(v[7:25], 16)
         return 0
 
-    lax.fori_loop(0, 11, spread, 0)
+    lax.fori_loop(0, 11, spread, 0, unroll=True)
+    for copy in loads[1:]:
+        copy.start()
 
     loads[0].wait()
 
@@ -403,7 +405,7 @@
     return copy
 
 
-def weights_fine(kept_hbm, keep, send, token, wire, kept, sem):
+def weights_fine(kept_hbm, keep, send, wire, kept, sem):
     copies = [
         fetch(kept_hbm, kept.at[pl.ds(first, end - first)], first, end, sem.at[k])
         for k, (first, end) in enumerate(((LIFT, SKIP), (SKIP, GRAD), (GRAD, COARSE)))
@@ -426,10 +428,9 @@
             taps.append(add_halves(same[p][:, 0, :, lanes].reshape(192, 128), q, same[p2][:, 1, :, lanes].reshape(192, 128), q2))
         put_three(wire, A_SKIP + 96 * a, A_SKIP2 + 48 * a, taps)
     split_wire(wire, keep, send)
-    token[0, 0] = jnp.int32(0)
-
-
-def weights_coarse(kept_hbm, g_dc, keep, send, wire, kept, sem):
+
+
+def weights_coarse(kept_hbm, g_dc, keep, send, token, wire, kept, sem):
     copy = fetch(kept_hbm, kept, COARSE, KEPT, sem.at[0])
     gc = taps_z(g_dc[...].astype(F32).reshape(32, 8, 128))
     copy.wait()
@@ -440,6 +441,7 @@
                 at = 64 * (9 * a + 3 * b + c)
                 put_parts(wire, at, 64, res[128 * b : 128 * b + 128, 128 * c : 128 * c + 128])
     split_wire(wire, keep, send)
+    token[0, 0] = jnp.int32(0)
 
 
 def add_halves(first, q, second, q2):
@@ -449,11 +451,8 @@
 
 
 def back_encode(gx, slope_ec, s_pool, s_in, g_skip, slope_ef, weights, keep, send, s5, ge, gz, wire):
-    def spread(x, _):
+    for x in range(8):
         s5[x] = taps_y(gx[x].astype(F32).reshape(12, 8, 128), 10)
-        return 0
-
-    lax.fori_loop(0, 8, spread, 0)
 
     def taps(first):
         return jnp.concatenate([weights[first + 384 * a : first + 384 * a + 384] for a in range(3)], axis=1)
@@ -643,7 +642,8 @@
             pltpu.SemaphoreType.DMA((11,)),
         ],
     )(active, feat, cot)
-    rz, rxz = swap(p1, swap_z), swap(p2, swap_xz)
+    rxz = swap(p2, swap_xz)
+    rz = swap(p1, swap_z)
     rz, w_forward = lax.optimization_barrier((rz, w_forward))
     xall, xmask, p3, p4 = call(
         pack_y,
@@ -651,7 +651,8 @@
         [VM] * 5,
         limit=8,
     )(cot, p1, p2, rz, rxz)
-    r3, r4 = swap(p3, swap_core), swap(p4, swap_yz)
+    r4 = swap(p4, swap_yz)
+    r3 = swap(p3, swap_core)
     r3, w_backward = lax.optimization_barrier((r3, w_backward))
 
     decoded, slope_ef, g_skip, slope_ec, g_dc, s_in, s_pool, kept = call(
@@ -690,9 +691,9 @@
     def add(keep, got):
         return (keep.astype(F32) + got.astype(F32)).astype(BF16)
 
-    keep_f, send_f, token = call(
+    keep_f, send_f = call(
         weights_fine,
-        [((ROWS_F, 128), BF16), ((ROWS_F, 128), BF16), ((1, 1), jnp.int32, SM)],
+        [((ROWS_F, 128), BF16)] * 2,
         [HB],
         scratch=[
             pltpu.VMEM((2, ROWS_F, 128), BF16),
@@ -702,9 +703,9 @@
         flops=1_000_000_000,
         limit=26,
     )(kept)
-    keep_c, send_c = call(
+    keep_c, send_c, token = call(
         weights_coarse,
-        [((ROWS_C, 128), BF16)] * 2,
+        [((ROWS_C, 128), BF16), ((ROWS_C, 128), BF16), ((1, 1), jnp.int32, SM)],
         [HB, VM],
         scratch=[
             pltpu.VMEM((2, ROWS_C, 128), BF16),
@@ -716,21 +717,20 @@
     )(kept, g_dc)
 
     is_odd = odd_r == 1
+    q2 = swap(jnp.where(is_odd, g_dc[2:], g_dc[:2]), swap_xz)
     q1 = swap(jnp.where(is_odd, g_dc[:2], g_dc[2:]), swap_z)
-    q2 = swap(jnp.where(is_odd, g_dc[2:], g_dc[:2]), swap_xz)
     zero = jnp.zeros_like(q1)
     before = jnp.where(row > 0, jnp.where(is_odd, q1, q2), zero)
     after = jnp.where(row < 7, jnp.where(is_odd, q2, q1), zero)
     gx = jnp.concatenate([before, g_dc, after], axis=0)
-    odd_c, token = lax.optimization_barrier((odd_c, token))
-    is_odd = odd_c == 1
+    is_odd = odd_c + token[0, 0] == 1
+    q4 = swap(jnp.where(is_odd, gx[:, 48:], gx[:, :16]), swap_yz)
     q3 = swap(jnp.where(is_odd, gx[:, :16], gx[:, 48:]), swap_core)
-    q4 = swap(jnp.where(is_odd, gx[:, 48:], gx[:, :16]), swap_yz)
     zero = jnp.zeros_like(q3)
     before = jnp.where(col > 0, jnp.where(is_odd, q3, q4), zero)
     after = jnp.where(col < 15, jnp.where(is_odd, q4, q3), zero)
     gx = jnp.concatenate([before, gx, after], axis=1)
-    gx, keep_c = lax.optimization_barrier((gx, keep_c))
+    gx, keep_f = lax.optimization_barrier((gx, keep_f))
 
 
     keep_b, send_b = call(

time: 108 us -> 108 us (level)
  blocking collectives: 46.7 us -> 49.2 us
  waiting for transfers between devices: 6.79 us -> 4.36 us
    ppermute x12, waiting for transfers between devices: 6.79 us -> 4.36 us  [swap(): return lax.ppermute(v, ('row', 'colh', 'core'), pairs)]
    all_to_all x1, blocking collectives: 24.3 us -> 26.3 us  [body(): terms = lax.all_to_all(half, chips, 0, 0, tiled=True)]
where the time goes in v5:
time: 108 us; the launch traced here: 107 us
  blocking collectives  49.2 us (46%)
  Pallas kernels  27.8 us (26%)
  starting transfers between devices  23.6 us (22%)
  waiting for transfers between devices  4.36 us (4%)
  between operations  1.64 us (2%)
    all_to_all x1, blocking collectives, body(): terms = lax.all_to_all(half, chips, 0, 0, tiled=True)  26.3 us
    ppermute x12, starting transfers between devices, swap(): return lax.ppermute(v, ('row', 'colh', 'core'), pairs)  23.6 us
    all_to_all x1, blocking collectives, body(): lax.all_to_all(jnp.broadcast_to(total[None], (64, CHUNK, 128)), chips, 0,...  22.9 us
    pallas_call x1, Pallas kernels, body(): call(forward, [((8, 128, 64), BF16, HB), ((5, 128, 128), F32), ((4, 128,...  8.44 us
    pallas_call x1, Pallas kernels, body(): call(arrange, [((ROOM, 384), BF16, HB)], [VM] * 4, scratch=[pltpu.VMEM((W...  4.49 us
    ppermute x12, waiting for transfers between devices, swap(): return lax.ppermute(v, ('row', 'colh', 'core'), pairs)  4.36 us
    pallas_call x2, Pallas kernels, body(): call(functools.partial(unpack, of_this_core), [(shape, F32, HB) for shape...  3.26 us
    pallas_call x1, Pallas kernels, body(): call(weights_fine, [((ROWS_F, 128), BF16)] * 2, [HB], scratch=[pltpu.VMEM...  3.04 us
  transfers between devices with their start and end apart: 12, of which 4 were waited for; matrix products, arithmetic and copies ran while one was open for 0% of the time, Pallas kernels for 15%

profile of v5, /device:TPU:1, one launch (start us, length us, event | category | flops | bytes accessed | tf_op | source)
XLA Modules:
  0.0 107.4 jit_solution(13015782688526248589)
XLA Ops:
  0.6 1.8 %shard_map.110 = (bf16[528,128]{1,0:T(8,128)(2,1)}, bf16[528,128]{1,0:T(8,128)(2,1)}) custom-call(s32[2]{0:T(128)} %bitcast.32, bf16[8,128,64]{2,1,0:T(8,128)(2,1)} %bitcast.31, bf16[8,128,64]{2,1,0:T(8,128)(2,1)} %bitcast.18), custom_call_target="tpu_custom_call" | custom-call | bytes 4000000 | tf_op jit(solution)/shard_map/pallas_call | solution.py:634
  2.5 2.5 %collective-permute-start = (bf16[528,128]{1,0:T(8,128)(2,1)}, bf16[528,128]{1,0:T(8,128)(2,1)S(1)}, u32[]{:S(2)}, u32[]{:S(2)}) collective-permute-start(bf16[528,128]{1,0:T(8,128)(2,1)} %get-tuple-element.40.p1), channel_id=1, source_target_pairs={{0,16},{1,17},{2,18},{3,19},{4,20},{5,21},{6,22},{7,23},{8,24},{9,... | collective-permute-start | bytes 405512 | tf_op jit(solution)/shard_map/ppermute | solution.py:600
  5.0 2.3 %collective-permute-start.1 = (bf16[528,128]{1,0:T(8,128)(2,1)}, bf16[528,128]{1,0:T(8,128)(2,1)S(1)}, u32[]{:S(2)}, u32[]{:S(2)}) collective-permute-start(bf16[528,128]{1,0:T(8,128)(2,1)} %get-tuple-element.41.p2), channel_id=1, source_target_pairs={{0,112},{1,113},{2,114},{3,115},{4,116},{5,117},{6,118},{7,119},{8... | collective-permute-start | bytes 405512 | tf_op jit(solution)/shard_map/ppermute | solution.py:600
  7.3 4.5 %shard_map.111.weights_hbm = bf16[51200,384]{1,0:T(8,128)(2,1)} custom-call(bf16[27,64,64]{2,1,0:T(8,128)(2,1)} %bitcast.30, bf16[27,64,128]{2,1,0:T(8,128)(2,1)} %bitcast.23, bf16[27,128,128]{2,1,0:T(8,128)(2,1)} %bitcast.21, bf16[27,64,192]{2,1,0:T(8,128)(2,1)} %bitcast.29), custom_call_target="tpu_custom_call" | custom-call | bytes 4000000 | tf_op jit(solution)/shard_map/pallas_call | solution.py:624
  11.8 0.3 shard_map.112
  12.1 1.6 %collective-permute-start.2 = (bf16[768,128]{1,0:T(8,128)(2,1)S(1)}, bf16[768,128]{1,0:T(8,128)(2,1)S(1)}, u32[]{:S(2)}, u32[]{:S(2)}) collective-permute-start(bf16[768,128]{1,0:T(8,128)(2,1)S(1)} %get-tuple-element.45), channel_id=1, source_target_pairs={{0,1},{1,0},{2,3},{3,2},{4,5},{5,4},{6,7},{7,6},{8,9},{9,8},{10,11... | collective-permute-start | bytes 589832 | tf_op jit(solution)/shard_map/ppermute | solution.py:600
  13.7 3.3 %collective-permute-start.3 = (bf16[768,128]{1,0:T(8,128)(2,1)S(1)}, bf16[768,128]{1,0:T(8,128)(2,1)S(1)}, u32[]{:S(2)}, u32[]{:S(2)}) collective-permute-start(bf16[768,128]{1,0:T(8,128)(2,1)S(1)} %get-tuple-element.47), channel_id=1, source_target_pairs={{0,15},{1,2},{2,1},{3,4},{4,3},{5,6},{6,5},{7,8},{8,7},{9,10},{10,... | collective-permute-start | bytes 589832 | tf_op jit(solution)/shard_map/ppermute | solution.py:600
  16.9 2.8 %shard_map.113.weights = bf16[2304,384]{1,0:T(8,128)(2,1)} custom-call(bf16[27,64,128]{2,1,0:T(8,128)(2,1)} %bitcast.24, bf16[27,128,128]{2,1,0:T(8,128)(2,1)} %bitcast.22), custom_call_target="tpu_custom_call" | custom-call | bytes 4000000 | tf_op jit(solution)/shard_map/pallas_call | solution.py:630
  19.7 1.9 %collective-permute-done.3.r4 = bf16[768,128]{1,0:T(8,128)(2,1)S(1)} collective-permute-done((bf16[768,128]{1,0:T(8,128)(2,1)S(1)}, bf16[768,128]{1,0:T(8,128)(2,1)S(1)}, u32[]{:S(2)}, u32[]{:S(2)}) %collective-permute-start.3) | collective-permute-done | bytes 196640 | tf_op jit(solution)/shard_map/ppermute | solution.py:600
  21.7 8.4 %shard_map.114 = (bf16[8,128,64]{2,1,0:T(8,128)(2,1)}, f32[5,128,128]{2,1,0:T(8,128)S(1)}, f32[4,128,128]{2,1,0:T(8,128)S(1)}, f32[7,80,128]{2,1,0:T(8,128)S(1)}...) custom-call(bf16[16,128,128]{2,1,0:T(8,128)(2,1)S(1)} %get-tuple-ele, ...), custom_call_target="tpu_custom_call" | custom-call | flops 4000000000 | bytes 4000000 | tf_op jit(solution)/shard_map/pallas_call | solution.py:658
  30.1 1.6 %collective-permute-start.4 = (bf16[2,64,128]{2,1,0:T(8,128)(2,1)S(1)}, bf16[2,64,128]{2,1,0:T(8,128)(2,1)S(1)}, u32[]{:S(2)}, u32[]{:S(2)}) collective-permute-start(bf16[2,64,128]{2,1,0:T(8,128)(2,1)S(1)} %get-tuple-element.82), channel_id=1, source_target_pairs={{0,16},{1,17},{2,18},{3,19},{4,20},{5,21},{6,22},{7,23},{8,24},{9,... | collective-permute-start | bytes 98312 | tf_op jit(solution)/shard_map/ppermute | solution.py:600
  31.7 2.3 %collective-permute-start.5 = (bf16[2,64,128]{2,1,0:T(8,128)(2,1)S(1)}, bf16[2,64,128]{2,1,0:T(8,128)(2,1)S(1)}, u32[]{:S(2)}, u32[]{:S(2)}) collective-permute-start(bf16[2,64,128]{2,1,0:T(8,128)(2,1)S(1)} %get-tuple-element.83), channel_id=1, source_target_pairs={{0,112},{1,113},{2,114},{3,115},{4,116},{5,117},{6,118},{7,119},{8... | collective-permute-start | bytes 98312 | tf_op jit(solution)/shard_map/ppermute | solution.py:600
  34.0 1.5 %shard_map.115 = (bf16[1728,128]{1,0:T(8,128)(2,1)S(1)}, bf16[1728,128]{1,0:T(8,128)(2,1)S(1)}, s32[1,1]{1,0:T(1,128)}) custom-call(bf16[51200,384]{1,0:T(8,128)(2,1)} %get-tuple-element.50.kept_hbm, bf16[4,64,128]{2,1,0:T(8,128)(2,1)S(1)} %get-tuple-element.51.g_dc), custom_call_target="tpu_custom_call" | custom-call | flops 300000000 | bytes 4000000 | tf_op jit(solution)/shard_map/pallas_call | solution.py:706
  36.2 0.4 collective-permute-done.5
  36.6 1.8 %collective-permute-start.6 = (bf16[8,16,128]{2,1,0:T(8,128)(2,1)S(1)}, bf16[8,16,128]{2,1,0:T(8,128)(2,1)S(1)}, u32[]{:S(2)}, u32[]{:S(2)}) collective-permute-start(bf16[8,16,128]{2,1,0:T(8,128)(2,1)S(1)} %get-tuple-element.75), channel_id=1, source_target_pairs={{0,1},{1,0},{2,3},{3,2},{4,5},{5,4},{6,7},{7,6},{8,9},{9,8},{10,11... | collective-permute-start | bytes 98312 | tf_op jit(solution)/shard_map/ppermute | solution.py:600
  38.4 3.1 %collective-permute-start.7 = (bf16[8,16,128]{2,1,0:T(8,128)(2,1)S(1)}, bf16[8,16,128]{2,1,0:T(8,128)(2,1)S(1)}, u32[]{:S(2)}, u32[]{:S(2)}) collective-permute-start(bf16[8,16,128]{2,1,0:T(8,128)(2,1)S(1)} %broadcast_select_fusion.2), channel_id=1, source_target_pairs={{0,15},{1,2},{2,1},{3,4},{4,3},{5,6},{6,5},{7,8},{8,7},{9,10},{10,... | collective-permute-start | bytes 98312 | tf_op jit(solution)/shard_map/ppermute | solution.py:600
  41.5 3.0 %shard_map.116 = (bf16[1296,128]{1,0:T(8,128)(2,1)S(1)}, bf16[1296,128]{1,0:T(8,128)(2,1)S(1)}) custom-call(bf16[51200,384]{1,0:T(8,128)(2,1)} %get-tuple-element.50.kept_hbm), custom_call_target="tpu_custom_call" | custom-call | flops 1000000000 | bytes 4000000 | tf_op jit(solution)/shard_map/pallas_call | solution.py:694
  44.6 1.7 %collective-permute-start.9 = (bf16[1728,128]{1,0:T(8,128)(2,1)S(1)}, bf16[1728,128]{1,0:T(8,128)(2,1)S(1)}, u32[]{:S(2)}, u32[]{:S(2)}) collective-permute-start(bf16[1728,128]{1,0:T(8,128)(2,1)S(1)} %get-tuple-element.57), channel_id=1, source_target_pairs={{0,1},{1,0},{2,3},{3,2},{4,5},{5,4},{6,7},{7,6},{8,9},{9,8},{10,11... | collective-permute-start | bytes 1327112 | tf_op jit(solution)/shard_map/ppermute | solution.py:600
  46.3 0.1 collective-permute-start.8
  46.4 2.2 %shard_map.117 = (bf16[1296,128]{1,0:T(8,128)(2,1)S(1)}, bf16[1296,128]{1,0:T(8,128)(2,1)S(1)}) custom-call(bf16[8,96,128]{2,1,0:T(8,128)(2,1)S(1)} %pad_maximum_fusion.gx, f32[7,80,128]{2,1,0:T(8,128)S(1)} %get-tuple-element.59.slope_ec, bf16[7,64,256]{2,1,0:T(8,128)(2,1)S(1)} %get-tuple-element.60.s_pool, bf16[6,128,384]{2,1,0:T(8,128)(2,1)S(1)} %get-tuple-element.61.s_in, ...), custom_call_target="tpu_custom_call" | custom-call | flops 500000000 | bytes 4000000 | tf_op jit(solution)/shard_map/pallas_call | solution.py:736
  48.6 0.5 collective-permute-start.10
  49.1 0.1 add_convert_fusion.2
  49.2 1.2 %collective-permute-done.10 = bf16[1296,128]{1,0:T(8,128)(2,1)S(1)} collective-permute-done((bf16[1296,128]{1,0:T(8,128)(2,1)S(1)}, bf16[1296,128]{1,0:T(8,128)(2,1)S(1)}, u32[]{:S(2)}, u32[]{:S(2)}) %collective-permute-start.10) | collective-permute-done | bytes 331808 | tf_op jit(solution)/shard_map/ppermute | solution.py:600
  50.5 0.1 add_convert_fusion
  50.7 26.3 %all_to_all.10 = bf16[64,72,128]{2,1,0:T(8,128)(2,1)S(1)} all-to-all(bf16[64,72,128]{2,1,0:T(8,128)(2,1)S(1)} %bitcast.20), channel_id=1, replica_groups=mesh['row'=8,'colh'=8,'core'=2] {'row','colh'}, dimensions={0} | all-to-all | bytes 2359296 | tf_op jit(solution)/shard_map/all_to_all | solution.py:753
  77.0 0.2 reduce_sum.12
  77.2 0.2 broadcast_in_dim.14
  77.3 22.9 %all_to_all.11.total = bf16[64,72,128]{2,1,0:T(8,128)(2,1)S(1)} all-to-all(bf16[64,72,128]{2,1,0:T(8,128)(2,1)S(1)} %broadcast_in_dim.14), channel_id=1, replica_groups=mesh['row'=8,'colh'=8,'core'=2] {'row','colh'}, dimensions={0} | all-to-all | bytes 2359296 | tf_op jit(solution)/shard_map/all_to_all | solution.py:755
  100.2 2.9 %collective-permute-start.11 = (bf16[64,72,128]{2,1,0:T(8,128)(2,1)S(1)}, bf16[64,72,128]{2,1,0:T(8,128)(2,1)S(1)}, u32[]{:S(2)}, u32[]{:S(2)}) collective-permute-start(bf16[64,72,128]{2,1,0:T(8,128)(2,1)S(1)} %all_to_all.11.total), channel_id=1, source_target_pairs={{0,1},{1,0},{2,3},{3,2},{4,5},{5,4},{6,7},{7,6},{8,9},{9,8},{10,11... | collective-permute-start | bytes 3538952 | tf_op jit(solution)/shard_map/ppermute | solution.py:600
  103.1 1.6 %shard_map.118 = (f32[27,64,192]{2,1,0:T(8,128)}, f32[27,128,128]{2,1,0:T(8,128)}, f32[27,64,64]{2,1,0:T(8,128)}, f32[27,64,128]{2,1,0:T(8,128)}) custom-call(bf16[64,72,128]{2,1,0:T(8,128)(2,1)S(1)} %all_to_all.11.total), custom_call_target="tpu_custom_call" | custom-call | bytes 4000000 | tf_op jit(solution)/shard_map/pallas_call | solution.py:761
  104.8 0.8 collective-permute-done.11.total
  105.6 1.6 %shard_map.119 = (f32[27,64,192]{2,1,0:T(8,128)}, f32[27,128,128]{2,1,0:T(8,128)}, f32[27,64,64]{2,1,0:T(8,128)}, f32[27,64,128]{2,1,0:T(8,128)}) custom-call(bf16[64,72,128]{2,1,0:T(8,128)(2,1)S(1)} %collective-permute-done.11.total, ...), custom_call_target="tpu_custom_call", output_to_operand_aliasing={{0}: (1, {}), {1}: (2, {}), {2}: (3, {}), {3}: (4, {})} | custom-call | bytes 4000000 | tf_op jit(solution)/shard_map/pallas_call | solution.py:761
  (24 shorter events, 0.3 us)
Async XLA Ops:
  2.5 9.3 %collective-permute-start = (bf16[528,128]{1,0:T(8,128)(2,1)}, bf16[528,128]{1,0:T(8,128)(2,1)S(1)}, u32[]{:S(2)}, u32[]{:S(2)}) collective-permute-start(bf16[528,128]{1,0:T(8,128)(2,1)} %get-tuple-element.40.p1), channel_id=1, source_target_pairs={{0,16},{1,17},{2,18},{3,19},{4,20},{5,21},{6,22},{7,23},{8,24},{9,... | collective-permute-start | bytes 405512 | tf_op jit(solution)/shard_map/ppermute | solution.py:600
  5.0 6.8 %collective-permute-start.1 = (bf16[528,128]{1,0:T(8,128)(2,1)}, bf16[528,128]{1,0:T(8,128)(2,1)S(1)}, u32[]{:S(2)}, u32[]{:S(2)}) collective-permute-start(bf16[528,128]{1,0:T(8,128)(2,1)} %get-tuple-element.41.p2), channel_id=1, source_target_pairs={{0,112},{1,113},{2,114},{3,115},{4,116},{5,117},{6,118},{7,119},{8... | collective-permute-start | bytes 405512 | tf_op jit(solution)/shard_map/ppermute | solution.py:600
  7.3 4.5 %copy-start.1 = (bf16[8,16,8,64]{3,2,1,0:T(8,128)(2,1)S(1)}, bf16[8,16,8,64]{3,2,1,0:T(8,128)(2,1)}, u32[]{:S(2)}) copy-start(bf16[8,16,8,64]{3,2,1,0:T(8,128)(2,1)} %param.13) | copy-start | bytes 393220
  7.3 4.5 %copy-start.2 = (bf16[528,128]{1,0:T(8,128)(2,1)S(1)}, bf16[528,128]{1,0:T(8,128)(2,1)}, u32[]{:S(2)}) copy-start(bf16[528,128]{1,0:T(8,128)(2,1)} %get-tuple-element.40.p1) | copy-start | bytes 405508
  7.3 4.5 %copy-start.3 = (bf16[528,128]{1,0:T(8,128)(2,1)S(1)}, bf16[528,128]{1,0:T(8,128)(2,1)}, u32[]{:S(2)}) copy-start(bf16[528,128]{1,0:T(8,128)(2,1)} %get-tuple-element.41.p2) | copy-start | bytes 405508
  12.1 7.6 %collective-permute-start.2 = (bf16[768,128]{1,0:T(8,128)(2,1)S(1)}, bf16[768,128]{1,0:T(8,128)(2,1)S(1)}, u32[]{:S(2)}, u32[]{:S(2)}) collective-permute-start(bf16[768,128]{1,0:T(8,128)(2,1)S(1)} %get-tuple-element.45), channel_id=1, source_target_pairs={{0,1},{1,0},{2,3},{3,2},{4,5},{5,4},{6,7},{7,6},{8,9},{9,8},{10,11... | collective-permute-start | bytes 589832 | tf_op jit(solution)/shard_map/ppermute | solution.py:600
  13.7 8.0 %collective-permute-start.3 = (bf16[768,128]{1,0:T(8,128)(2,1)S(1)}, bf16[768,128]{1,0:T(8,128)(2,1)S(1)}, u32[]{:S(2)}, u32[]{:S(2)}) collective-permute-start(bf16[768,128]{1,0:T(8,128)(2,1)S(1)} %get-tuple-element.47), channel_id=1, source_target_pairs={{0,15},{1,2},{2,1},{3,4},{4,3},{5,6},{6,5},{7,8},{8,7},{9,10},{10,... | collective-permute-start | bytes 589832 | tf_op jit(solution)/shard_map/ppermute | solution.py:600
  30.1 6.1 %collective-permute-start.4 = (bf16[2,64,128]{2,1,0:T(8,128)(2,1)S(1)}, bf16[2,64,128]{2,1,0:T(8,128)(2,1)S(1)}, u32[]{:S(2)}, u32[]{:S(2)}) collective-permute-start(bf16[2,64,128]{2,1,0:T(8,128)(2,1)S(1)} %get-tuple-element.82), channel_id=1, source_target_pairs={{0,16},{1,17},{2,18},{3,19},{4,20},{5,21},{6,22},{7,23},{8,24},{9,... | collective-permute-start | bytes 98312 | tf_op jit(solution)/shard_map/ppermute | solution.py:600
  31.7 4.9 %collective-permute-start.5 = (bf16[2,64,128]{2,1,0:T(8,128)(2,1)S(1)}, bf16[2,64,128]{2,1,0:T(8,128)(2,1)S(1)}, u32[]{:S(2)}, u32[]{:S(2)}) collective-permute-start(bf16[2,64,128]{2,1,0:T(8,128)(2,1)S(1)} %get-tuple-element.83), channel_id=1, source_target_pairs={{0,112},{1,113},{2,114},{3,115},{4,116},{5,117},{6,118},{7,119},{8... | collective-permute-start | bytes 98312 | tf_op jit(solution)/shard_map/ppermute | solution.py:600
  36.6 9.8 %collective-permute-start.6 = (bf16[8,16,128]{2,1,0:T(8,128)(2,1)S(1)}, bf16[8,16,128]{2,1,0:T(8,128)(2,1)S(1)}, u32[]{:S(2)}, u32[]{:S(2)}) collective-permute-start(bf16[8,16,128]{2,1,0:T(8,128)(2,1)S(1)} %get-tuple-element.75), channel_id=1, source_target_pairs={{0,1},{1,0},{2,3},{3,2},{4,5},{5,4},{6,7},{7,6},{8,9},{9,8},{10,11... | collective-permute-start | bytes 98312 | tf_op jit(solution)/shard_map/ppermute | solution.py:600
  38.4 8.0 %copy-start = (bf16[2304,384]{1,0:T(8,128)(2,1)S(1)}, bf16[2304,384]{1,0:T(8,128)(2,1)}, u32[]{:S(2)}) copy-start(bf16[2304,384]{1,0:T(8,128)(2,1)} %shard_map.113.weights) | copy-start | bytes 5308420
  38.4 7.9 %collective-permute-start.7 = (bf16[8,16,128]{2,1,0:T(8,128)(2,1)S(1)}, bf16[8,16,128]{2,1,0:T(8,128)(2,1)S(1)}, u32[]{:S(2)}, u32[]{:S(2)}) collective-permute-start(bf16[8,16,128]{2,1,0:T(8,128)(2,1)S(1)} %broadcast_select_fusion.2), channel_id=1, source_target_pairs={{0,15},{1,2},{2,1},{3,4},{4,3},{5,6},{6,5},{7,8},{8,7},{9,10},{10,... | collective-permute-start | bytes 98312 | tf_op jit(solution)/shard_map/ppermute | solution.py:600
  44.6 5.9 %collective-permute-start.9 = (bf16[1728,128]{1,0:T(8,128)(2,1)S(1)}, bf16[1728,128]{1,0:T(8,128)(2,1)S(1)}, u32[]{:S(2)}, u32[]{:S(2)}) collective-permute-start(bf16[1728,128]{1,0:T(8,128)(2,1)S(1)} %get-tuple-element.57), channel_id=1, source_target_pairs={{0,1},{1,0},{2,3},{3,2},{4,5},{5,4},{6,7},{7,6},{8,9},{9,8},{10,11... | collective-permute-start | bytes 1327112 | tf_op jit(solution)/shard_map/ppermute | solution.py:600
  46.3 2.8 %collective-permute-start.8 = (bf16[1296,128]{1,0:T(8,128)(2,1)S(1)}, bf16[1296,128]{1,0:T(8,128)(2,1)S(1)}, u32[]{:S(2)}, u32[]{:S(2)}) collective-permute-start(bf16[1296,128]{1,0:T(8,128)(2,1)S(1)} %get-tuple-element.55), channel_id=1, source_target_pairs={{0,1},{1,0},{2,3},{3,2},{4,5},{5,4},{6,7},{7,6},{8,9},{9,8},{10,11... | collective-permute-start | bytes 995336 | tf_op jit(solution)/shard_map/ppermute | solution.py:600
  48.6 1.7 %collective-permute-start.10 = (bf16[1296,128]{1,0:T(8,128)(2,1)S(1)}, bf16[1296,128]{1,0:T(8,128)(2,1)S(1)}, u32[]{:S(2)}, u32[]{:S(2)}) collective-permute-start(bf16[1296,128]{1,0:T(8,128)(2,1)S(1)} %get-tuple-element.66), channel_id=1, source_target_pairs={{0,1},{1,0},{2,3},{3,2},{4,5},{5,4},{6,7},{7,6},{8,9},{9,8},{10,11... | collective-permute-start | bytes 995336 | tf_op jit(solution)/shard_map/ppermute | solution.py:600
  100.2 5.4 %collective-permute-start.11 = (bf16[64,72,128]{2,1,0:T(8,128)(2,1)S(1)}, bf16[64,72,128]{2,1,0:T(8,128)(2,1)S(1)}, u32[]{:S(2)}, u32[]{:S(2)}) collective-permute-start(bf16[64,72,128]{2,1,0:T(8,128)(2,1)S(1)} %all_to_all.11.total), channel_id=1, source_target_pairs={{0,1},{1,0},{2,3},{3,2},{4,5},{5,4},{6,7},{7,6},{8,9},{9,8},{10,11... | collective-permute-start | bytes 3538952 | tf_op jit(solution)/shard_map/ppermute | solution.py:600

commit v6 on v5

--- a/solution.py
+++ b/solution.py
@@ -135,16 +135,19 @@
     copies += [pltpu.make_async_copy(cot_hbm.at[7 * k], cot.at[k], sem.at[9 + k]) for k in range(2)]
     for copy in copies:
         copy.start()
-    for copy in copies:
-        copy.wait()
+    copies[0].wait()
     row = lax.broadcasted_iota(jnp.int32, (128, 64), 0)
     mask = jnp.where(row < 64, active[0], active[1]).astype(F32)
     row = lax.broadcasted_iota(jnp.int32, (16, 128), 0)
     ends = jnp.where(row < 8, active[0], active[1]).astype(F32).astype(BF16)
     for k in range(3):
+        copies[2 + 2 * k].wait()
+        copies[3 + 2 * k].wait()
         pair = beside(feat[2 * k + 1].astype(F32) * mask, feat[2 * k + 2].astype(F32) * mask).astype(BF16)
         p1[128 * k : 128 * k + 128] = pair
         p2[128 * k : 128 * k + 128] = pair
+    for k in (1, 8, 9, 10):
+        copies[k].wait()
     for p, edge in ((p1, jnp.where(odd, 0, 1)), (p2, jnp.where(odd, 1, 0))):
         p[384:512] = beside(feat[7 * edge].astype(F32) * mask, cot[edge]).astype(BF16)
         p[512:528] = ends
@@ -325,7 +328,9 @@
 
     lifted = both(LIFT)
     wide = jnp.concatenate([lifted, lifted, both(SKIP)], axis=1)
-    acc[...] = dot_n(wide, jnp.concatenate([taps(W4L, 768), taps(W4L + 384, 768), taps(W4E, 384)], axis=1))
+    wide_taps = jnp.concatenate([taps(W4L, 768), taps(W4L + 384, 768), taps(W4E, 384)], axis=1)
+    acc[0:288] = dot_n(wide[0:288], wide_taps)
+    acc[288:720] = dot_n(wide[288:720], wide_taps)
 
     def decode(i, _):
         pre = fold128(acc[pl.ds(pl.multiple_of(144 * i, 144), 144)])
@@ -408,12 +413,13 @@
 def weights_fine(kept_hbm, keep, send, wire, kept, sem):
     copies = [
         fetch(kept_hbm, kept.at[pl.ds(first, end - first)], first, end, sem.at[k])
-        for k, (first, end) in enumerate(((LIFT, SKIP), (SKIP, GRAD), (GRAD, COARSE)))
+        for k, (first, end) in enumerate(((GRAD, COARSE), (LIFT, SKIP), (SKIP, GRAD)))
     ]
-    for copy in copies:
-        copy.wait()
+    copies[0].wait()
+    copies[1].wait()
     grad = kept[GRAD:COARSE]
     up = [(dot_t(grad, kept[LIFT + 144 * p : LIFT + 144 * p + 720]) * FACTOR).reshape(3, 2, 64, 384) for p in range(2)]
+    copies[2].wait()
     same = [(dot_t(grad, kept[SKIP + 144 * p : SKIP + 144 * p + 720]) * FACTOR).reshape(3, 2, 64, 384) for p in range(2)]
     for a, (p, q) in enumerate(((0, 0), (0, 1), (1, 0))):
         p2, q2 = (0, 1) if a == 0 else (1, a - 1)

time: 108 us -> 108 us (level)
  no operation moved by 1% of the time
where the time goes in v6:
time: 108 us
  blocking collectives  49.3 us (46%)
  Pallas kernels  27.9 us (26%)
  starting transfers between devices  23.7 us (22%)
  waiting for transfers between devices  4.35 us (4%)
  between operations  1.64 us (2%)
    all_to_all x1, blocking collectives, body(): terms = lax.all_to_all(half, chips, 0, 0, tiled=True)  26.4 us
    ppermute x12, starting transfers between devices, swap(): return lax.ppermute(v, ('row', 'colh', 'core'), pairs)  23.7 us
    all_to_all x1, blocking collectives, body(): lax.all_to_all(jnp.broadcast_to(total[None], (64, CHUNK, 128)), chips, 0,...  22.9 us
    pallas_call x1, Pallas kernels, body(): call(forward, [((8, 128, 64), BF16, HB), ((5, 128, 128), F32), ((4, 128,...  8.4 us
    pallas_call x1, Pallas kernels, body(): call(arrange, [((ROOM, 384), BF16, HB)], [VM] * 4, scratch=[pltpu.VMEM((W...  4.49 us
    ppermute x12, waiting for transfers between devices, swap(): return lax.ppermute(v, ('row', 'colh', 'core'), pairs)  4.35 us
    pallas_call x2, Pallas kernels, body(): call(functools.partial(unpack, of_this_core), [(shape, F32, HB) for shape...  3.26 us
    pallas_call x1, Pallas kernels, body(): call(weights_fine, [((ROWS_F, 128), BF16)] * 2, [HB], scratch=[pltpu.VMEM...  3.11 us
  transfers between devices with their start and end apart: 12, of which 4 were waited for; matrix products, arithmetic and copies ran while one was open for 0% of the time, Pallas kernels for 15%

profile of v6, /device:TPU:1, one launch (start us, length us, event | category | flops | bytes accessed | tf_op | source)
XLA Modules:
  0.0 107.6 jit_solution(6091396109040041346)
XLA Ops:
  0.6 1.9 %shard_map.110 = (bf16[528,128]{1,0:T(8,128)(2,1)}, bf16[528,128]{1,0:T(8,128)(2,1)}) custom-call(s32[2]{0:T(128)} %bitcast.32, bf16[8,128,64]{2,1,0:T(8,128)(2,1)} %bitcast.31, bf16[8,128,64]{2,1,0:T(8,128)(2,1)} %bitcast.18), custom_call_target="tpu_custom_call" | custom-call | bytes 4000000 | tf_op jit(solution)/shard_map/pallas_call | solution.py:640
  2.6 2.5 %collective-permute-start = (bf16[528,128]{1,0:T(8,128)(2,1)}, bf16[528,128]{1,0:T(8,128)(2,1)S(1)}, u32[]{:S(2)}, u32[]{:S(2)}) collective-permute-start(bf16[528,128]{1,0:T(8,128)(2,1)} %get-tuple-element.40.p1), channel_id=1, source_target_pairs={{0,16},{1,17},{2,18},{3,19},{4,20},{5,21},{6,22},{7,23},{8,24},{9,... | collective-permute-start | bytes 405512 | tf_op jit(solution)/shard_map/ppermute | solution.py:606
  5.1 2.3 %collective-permute-start.1 = (bf16[528,128]{1,0:T(8,128)(2,1)}, bf16[528,128]{1,0:T(8,128)(2,1)S(1)}, u32[]{:S(2)}, u32[]{:S(2)}) collective-permute-start(bf16[528,128]{1,0:T(8,128)(2,1)} %get-tuple-element.41.p2), channel_id=1, source_target_pairs={{0,112},{1,113},{2,114},{3,115},{4,116},{5,117},{6,118},{7,119},{8... | collective-permute-start | bytes 405512 | tf_op jit(solution)/shard_map/ppermute | solution.py:606
  7.4 4.5 %shard_map.111.weights_hbm = bf16[51200,384]{1,0:T(8,128)(2,1)} custom-call(bf16[27,64,64]{2,1,0:T(8,128)(2,1)} %bitcast.30, bf16[27,64,128]{2,1,0:T(8,128)(2,1)} %bitcast.23, bf16[27,128,128]{2,1,0:T(8,128)(2,1)} %bitcast.21, bf16[27,64,192]{2,1,0:T(8,128)(2,1)} %bitcast.29), custom_call_target="tpu_custom_call" | custom-call | bytes 4000000 | tf_op jit(solution)/shard_map/pallas_call | solution.py:630
  11.9 0.3 shard_map.112
  12.2 1.6 %collective-permute-start.2 = (bf16[768,128]{1,0:T(8,128)(2,1)S(1)}, bf16[768,128]{1,0:T(8,128)(2,1)S(1)}, u32[]{:S(2)}, u32[]{:S(2)}) collective-permute-start(bf16[768,128]{1,0:T(8,128)(2,1)S(1)} %get-tuple-element.45), channel_id=1, source_target_pairs={{0,1},{1,0},{2,3},{3,2},{4,5},{5,4},{6,7},{7,6},{8,9},{9,8},{10,11... | collective-permute-start | bytes 589832 | tf_op jit(solution)/shard_map/ppermute | solution.py:606
  13.8 3.3 %collective-permute-start.3 = (bf16[768,128]{1,0:T(8,128)(2,1)S(1)}, bf16[768,128]{1,0:T(8,128)(2,1)S(1)}, u32[]{:S(2)}, u32[]{:S(2)}) collective-permute-start(bf16[768,128]{1,0:T(8,128)(2,1)S(1)} %get-tuple-element.47), channel_id=1, source_target_pairs={{0,15},{1,2},{2,1},{3,4},{4,3},{5,6},{6,5},{7,8},{8,7},{9,10},{10,... | collective-permute-start | bytes 589832 | tf_op jit(solution)/shard_map/ppermute | solution.py:606
  17.1 2.8 %shard_map.113.weights = bf16[2304,384]{1,0:T(8,128)(2,1)} custom-call(bf16[27,64,128]{2,1,0:T(8,128)(2,1)} %bitcast.24, bf16[27,128,128]{2,1,0:T(8,128)(2,1)} %bitcast.22), custom_call_target="tpu_custom_call" | custom-call | bytes 4000000 | tf_op jit(solution)/shard_map/pallas_call | solution.py:636
  19.8 1.9 %collective-permute-done.3.r4 = bf16[768,128]{1,0:T(8,128)(2,1)S(1)} collective-permute-done((bf16[768,128]{1,0:T(8,128)(2,1)S(1)}, bf16[768,128]{1,0:T(8,128)(2,1)S(1)}, u32[]{:S(2)}, u32[]{:S(2)}) %collective-permute-start.3) | collective-permute-done | bytes 196640 | tf_op jit(solution)/shard_map/ppermute | solution.py:606
  21.8 8.4 %shard_map.114 = (bf16[8,128,64]{2,1,0:T(8,128)(2,1)}, f32[5,128,128]{2,1,0:T(8,128)S(1)}, f32[4,128,128]{2,1,0:T(8,128)S(1)}, f32[7,80,128]{2,1,0:T(8,128)S(1)}...) custom-call(bf16[16,128,128]{2,1,0:T(8,128)(2,1)S(1)} %get-tuple-ele, ...), custom_call_target="tpu_custom_call" | custom-call | flops 4000000000 | bytes 4000000 | tf_op jit(solution)/shard_map/pallas_call | solution.py:664
  30.2 1.6 %collective-permute-start.4 = (bf16[2,64,128]{2,1,0:T(8,128)(2,1)S(1)}, bf16[2,64,128]{2,1,0:T(8,128)(2,1)S(1)}, u32[]{:S(2)}, u32[]{:S(2)}) collective-permute-start(bf16[2,64,128]{2,1,0:T(8,128)(2,1)S(1)} %get-tuple-element.82), channel_id=1, source_target_pairs={{0,16},{1,17},{2,18},{3,19},{4,20},{5,21},{6,22},{7,23},{8,24},{9,... | collective-permute-start | bytes 98312 | tf_op jit(solution)/shard_map/ppermute | solution.py:606
  31.8 2.3 %collective-permute-start.5 = (bf16[2,64,128]{2,1,0:T(8,128)(2,1)S(1)}, bf16[2,64,128]{2,1,0:T(8,128)(2,1)S(1)}, u32[]{:S(2)}, u32[]{:S(2)}) collective-permute-start(bf16[2,64,128]{2,1,0:T(8,128)(2,1)S(1)} %get-tuple-element.83), channel_id=1, source_target_pairs={{0,112},{1,113},{2,114},{3,115},{4,116},{5,117},{6,118},{7,119},{8... | collective-permute-start | bytes 98312 | tf_op jit(solution)/shard_map/ppermute | solution.py:606
  34.1 1.5 %shard_map.115 = (bf16[1728,128]{1,0:T(8,128)(2,1)S(1)}, bf16[1728,128]{1,0:T(8,128)(2,1)S(1)}, s32[1,1]{1,0:T(1,128)}) custom-call(bf16[51200,384]{1,0:T(8,128)(2,1)} %get-tuple-element.50.kept_hbm, bf16[4,64,128]{2,1,0:T(8,128)(2,1)S(1)} %get-tuple-element.51.g_dc), custom_call_target="tpu_custom_call" | custom-call | flops 300000000 | bytes 4000000 | tf_op jit(solution)/shard_map/pallas_call | solution.py:712
  36.3 0.4 collective-permute-done.5
  36.7 1.8 %collective-permute-start.6 = (bf16[8,16,128]{2,1,0:T(8,128)(2,1)S(1)}, bf16[8,16,128]{2,1,0:T(8,128)(2,1)S(1)}, u32[]{:S(2)}, u32[]{:S(2)}) collective-permute-start(bf16[8,16,128]{2,1,0:T(8,128)(2,1)S(1)} %get-tuple-element.75), channel_id=1, source_target_pairs={{0,1},{1,0},{2,3},{3,2},{4,5},{5,4},{6,7},{7,6},{8,9},{9,8},{10,11... | collective-permute-start | bytes 98312 | tf_op jit(solution)/shard_map/ppermute | solution.py:606
  38.5 3.3 %collective-permute-start.7 = (bf16[8,16,128]{2,1,0:T(8,128)(2,1)S(1)}, bf16[8,16,128]{2,1,0:T(8,128)(2,1)S(1)}, u32[]{:S(2)}, u32[]{:S(2)}) collective-permute-start(bf16[8,16,128]{2,1,0:T(8,128)(2,1)S(1)} %broadcast_select_fusion.2), channel_id=1, source_target_pairs={{0,15},{1,2},{2,1},{3,4},{4,3},{5,6},{6,5},{7,8},{8,7},{9,10},{10,... | collective-permute-start | bytes 98312 | tf_op jit(solution)/shard_map/ppermute | solution.py:606
  41.8 3.1 %shard_map.116 = (bf16[1296,128]{1,0:T(8,128)(2,1)S(1)}, bf16[1296,128]{1,0:T(8,128)(2,1)S(1)}) custom-call(bf16[51200,384]{1,0:T(8,128)(2,1)} %get-tuple-element.50.kept_hbm), custom_call_target="tpu_custom_call" | custom-call | flops 1000000000 | bytes 4000000 | tf_op jit(solution)/shard_map/pallas_call | solution.py:700
  44.9 1.5 %collective-permute-start.9 = (bf16[1728,128]{1,0:T(8,128)(2,1)S(1)}, bf16[1728,128]{1,0:T(8,128)(2,1)S(1)}, u32[]{:S(2)}, u32[]{:S(2)}) collective-permute-start(bf16[1728,128]{1,0:T(8,128)(2,1)S(1)} %get-tuple-element.57), channel_id=1, source_target_pairs={{0,1},{1,0},{2,3},{3,2},{4,5},{5,4},{6,7},{7,6},{8,9},{9,8},{10,11... | collective-permute-start | bytes 1327112 | tf_op jit(solution)/shard_map/ppermute | solution.py:606
  46.4 0.1 collective-permute-start.8
  46.6 2.2 %shard_map.117 = (bf16[1296,128]{1,0:T(8,128)(2,1)S(1)}, bf16[1296,128]{1,0:T(8,128)(2,1)S(1)}) custom-call(bf16[8,96,128]{2,1,0:T(8,128)(2,1)S(1)} %pad_maximum_fusion.gx, f32[7,80,128]{2,1,0:T(8,128)S(1)} %get-tuple-element.59.slope_ec, bf16[7,64,256]{2,1,0:T(8,128)(2,1)S(1)} %get-tuple-element.60.s_pool, bf16[6,128,384]{2,1,0:T(8,128)(2,1)S(1)} %get-tuple-element.61.s_in, ...), custom_call_target="tpu_custom_call" | custom-call | flops 500000000 | bytes 4000000 | tf_op jit(solution)/shard_map/pallas_call | solution.py:742
  48.8 0.5 collective-permute-start.10
  49.3 0.1 add_convert_fusion.2
  49.3 1.2 %collective-permute-done.10 = bf16[1296,128]{1,0:T(8,128)(2,1)S(1)} collective-permute-done((bf16[1296,128]{1,0:T(8,128)(2,1)S(1)}, bf16[1296,128]{1,0:T(8,128)(2,1)S(1)}, u32[]{:S(2)}, u32[]{:S(2)}) %collective-permute-start.10) | collective-permute-done | bytes 331808 | tf_op jit(solution)/shard_map/ppermute | solution.py:606
  50.6 0.1 add_convert_fusion
  50.8 26.4 %all_to_all.10 = bf16[64,72,128]{2,1,0:T(8,128)(2,1)S(1)} all-to-all(bf16[64,72,128]{2,1,0:T(8,128)(2,1)S(1)} %bitcast.20), channel_id=1, replica_groups=mesh['row'=8,'colh'=8,'core'=2] {'row','colh'}, dimensions={0} | all-to-all | bytes 2359296 | tf_op jit(solution)/shard_map/all_to_all | solution.py:759
  77.2 0.2 reduce_sum.12
  77.4 0.2 broadcast_in_dim.14
  77.6 22.9 %all_to_all.11.total = bf16[64,72,128]{2,1,0:T(8,128)(2,1)S(1)} all-to-all(bf16[64,72,128]{2,1,0:T(8,128)(2,1)S(1)} %broadcast_in_dim.14), channel_id=1, replica_groups=mesh['row'=8,'colh'=8,'core'=2] {'row','colh'}, dimensions={0} | all-to-all | bytes 2359296 | tf_op jit(solution)/shard_map/all_to_all | solution.py:761
  100.4 2.9 %collective-permute-start.11 = (bf16[64,72,128]{2,1,0:T(8,128)(2,1)S(1)}, bf16[64,72,128]{2,1,0:T(8,128)(2,1)S(1)}, u32[]{:S(2)}, u32[]{:S(2)}) collective-permute-start(bf16[64,72,128]{2,1,0:T(8,128)(2,1)S(1)} %all_to_all.11.total), channel_id=1, source_target_pairs={{0,1},{1,0},{2,3},{3,2},{4,5},{5,4},{6,7},{7,6},{8,9},{9,8},{10,11... | collective-permute-start | bytes 3538952 | tf_op jit(solution)/shard_map/ppermute | solution.py:606
  103.4 1.6 %shard_map.118 = (f32[27,64,192]{2,1,0:T(8,128)}, f32[27,128,128]{2,1,0:T(8,128)}, f32[27,64,64]{2,1,0:T(8,128)}, f32[27,64,128]{2,1,0:T(8,128)}) custom-call(bf16[64,72,128]{2,1,0:T(8,128)(2,1)S(1)} %all_to_all.11.total), custom_call_target="tpu_custom_call" | custom-call | bytes 4000000 | tf_op jit(solution)/shard_map/pallas_call | solution.py:767
  105.0 0.8 collective-permute-done.11.total
  105.8 1.6 %shard_map.119 = (f32[27,64,192]{2,1,0:T(8,128)}, f32[27,128,128]{2,1,0:T(8,128)}, f32[27,64,64]{2,1,0:T(8,128)}, f32[27,64,128]{2,1,0:T(8,128)}) custom-call(bf16[64,72,128]{2,1,0:T(8,128)(2,1)S(1)} %collective-permute-done.11.total, ...), custom_call_target="tpu_custom_call", output_to_operand_aliasing={{0}: (1, {}), {1}: (2, {}), {2}: (3, {}), {3}: (4, {})} | custom-call | bytes 4000000 | tf_op jit(solution)/shard_map/pallas_call | solution.py:767
  (24 shorter events, 0.3 us)
Async XLA Ops:
  2.6 9.3 %collective-permute-start = (bf16[528,128]{1,0:T(8,128)(2,1)}, bf16[528,128]{1,0:T(8,128)(2,1)S(1)}, u32[]{:S(2)}, u32[]{:S(2)}) collective-permute-start(bf16[528,128]{1,0:T(8,128)(2,1)} %get-tuple-element.40.p1), channel_id=1, source_target_pairs={{0,16},{1,17},{2,18},{3,19},{4,20},{5,21},{6,22},{7,23},{8,24},{9,... | collective-permute-start | bytes 405512 | tf_op jit(solution)/shard_map/ppermute | solution.py:606
  5.1 6.8 %collective-permute-start.1 = (bf16[528,128]{1,0:T(8,128)(2,1)}, bf16[528,128]{1,0:T(8,128)(2,1)S(1)}, u32[]{:S(2)}, u32[]{:S(2)}) collective-permute-start(bf16[528,128]{1,0:T(8,128)(2,1)} %get-tuple-element.41.p2), channel_id=1, source_target_pairs={{0,112},{1,113},{2,114},{3,115},{4,116},{5,117},{6,118},{7,119},{8... | collective-permute-start | bytes 405512 | tf_op jit(solution)/shard_map/ppermute | solution.py:606
  7.4 4.5 %copy-start.1 = (bf16[8,16,8,64]{3,2,1,0:T(8,128)(2,1)S(1)}, bf16[8,16,8,64]{3,2,1,0:T(8,128)(2,1)}, u32[]{:S(2)}) copy-start(bf16[8,16,8,64]{3,2,1,0:T(8,128)(2,1)} %param.13) | copy-start | bytes 393220
  7.4 4.5 %copy-start.2 = (bf16[528,128]{1,0:T(8,128)(2,1)S(1)}, bf16[528,128]{1,0:T(8,128)(2,1)}, u32[]{:S(2)}) copy-start(bf16[528,128]{1,0:T(8,128)(2,1)} %get-tuple-element.40.p1) | copy-start | bytes 405508
  7.4 4.5 %copy-start.3 = (bf16[528,128]{1,0:T(8,128)(2,1)S(1)}, bf16[528,128]{1,0:T(8,128)(2,1)}, u32[]{:S(2)}) copy-start(bf16[528,128]{1,0:T(8,128)(2,1)} %get-tuple-element.41.p2) | copy-start | bytes 405508
  12.2 7.6 %collective-permute-start.2 = (bf16[768,128]{1,0:T(8,128)(2,1)S(1)}, bf16[768,128]{1,0:T(8,128)(2,1)S(1)}, u32[]{:S(2)}, u32[]{:S(2)}) collective-permute-start(bf16[768,128]{1,0:T(8,128)(2,1)S(1)} %get-tuple-element.45), channel_id=1, source_target_pairs={{0,1},{1,0},{2,3},{3,2},{4,5},{5,4},{6,7},{7,6},{8,9},{9,8},{10,11... | collective-permute-start | bytes 589832 | tf_op jit(solution)/shard_map/ppermute | solution.py:606
  13.8 8.0 %collective-permute-start.3 = (bf16[768,128]{1,0:T(8,128)(2,1)S(1)}, bf16[768,128]{1,0:T(8,128)(2,1)S(1)}, u32[]{:S(2)}, u32[]{:S(2)}) collective-permute-start(bf16[768,128]{1,0:T(8,128)(2,1)S(1)} %get-tuple-element.47), channel_id=1, source_target_pairs={{0,15},{1,2},{2,1},{3,4},{4,3},{5,6},{6,5},{7,8},{8,7},{9,10},{10,... | collective-permute-start | bytes 589832 | tf_op jit(solution)/shard_map/ppermute | solution.py:606
  30.2 6.1 %collective-permute-start.4 = (bf16[2,64,128]{2,1,0:T(8,128)(2,1)S(1)}, bf16[2,64,128]{2,1,0:T(8,128)(2,1)S(1)}, u32[]{:S(2)}, u32[]{:S(2)}) collective-permute-start(bf16[2,64,128]{2,1,0:T(8,128)(2,1)S(1)} %get-tuple-element.82), channel_id=1, source_target_pairs={{0,16},{1,17},{2,18},{3,19},{4,20},{5,21},{6,22},{7,23},{8,24},{9,... | collective-permute-start | bytes 98312 | tf_op jit(solution)/shard_map/ppermute | solution.py:606
  31.8 4.9 %collective-permute-start.5 = (bf16[2,64,128]{2,1,0:T(8,128)(2,1)S(1)}, bf16[2,64,128]{2,1,0:T(8,128)(2,1)S(1)}, u32[]{:S(2)}, u32[]{:S(2)}) collective-permute-start(bf16[2,64,128]{2,1,0:T(8,128)(2,1)S(1)} %get-tuple-element.83), channel_id=1, source_target_pairs={{0,112},{1,113},{2,114},{3,115},{4,116},{5,117},{6,118},{7,119},{8... | collective-permute-start | bytes 98312 | tf_op jit(solution)/shard_map/ppermute | solution.py:606
  36.7 9.8 %collective-permute-start.6 = (bf16[8,16,128]{2,1,0:T(8,128)(2,1)S(1)}, bf16[8,16,128]{2,1,0:T(8,128)(2,1)S(1)}, u32[]{:S(2)}, u32[]{:S(2)}) collective-permute-start(bf16[8,16,128]{2,1,0:T(8,128)(2,1)S(1)} %get-tuple-element.75), channel_id=1, source_target_pairs={{0,1},{1,0},{2,3},{3,2},{4,5},{5,4},{6,7},{7,6},{8,9},{9,8},{10,11... | collective-permute-start | bytes 98312 | tf_op jit(solution)/shard_map/ppermute | solution.py:606
  38.5 8.1 %copy-start = (bf16[2304,384]{1,0:T(8,128)(2,1)S(1)}, bf16[2304,384]{1,0:T(8,128)(2,1)}, u32[]{:S(2)}) copy-start(bf16[2304,384]{1,0:T(8,128)(2,1)} %shard_map.113.weights) | copy-start | bytes 5308420
  38.5 8.0 %collective-permute-start.7 = (bf16[8,16,128]{2,1,0:T(8,128)(2,1)S(1)}, bf16[8,16,128]{2,1,0:T(8,128)(2,1)S(1)}, u32[]{:S(2)}, u32[]{:S(2)}) collective-permute-start(bf16[8,16,128]{2,1,0:T(8,128)(2,1)S(1)} %broadcast_select_fusion.2), channel_id=1, source_target_pairs={{0,15},{1,2},{2,1},{3,4},{4,3},{5,6},{6,5},{7,8},{8,7},{9,10},{10,... | collective-permute-start | bytes 98312 | tf_op jit(solution)/shard_map/ppermute | solution.py:606
  44.9 5.7 %collective-permute-start.9 = (bf16[1728,128]{1,0:T(8,128)(2,1)S(1)}, bf16[1728,128]{1,0:T(8,128)(2,1)S(1)}, u32[]{:S(2)}, u32[]{:S(2)}) collective-permute-start(bf16[1728,128]{1,0:T(8,128)(2,1)S(1)} %get-tuple-element.57), channel_id=1, source_target_pairs={{0,1},{1,0},{2,3},{3,2},{4,5},{5,4},{6,7},{7,6},{8,9},{9,8},{10,11... | collective-permute-start | bytes 1327112 | tf_op jit(solution)/shard_map/ppermute | solution.py:606
  46.4 2.8 %collective-permute-start.8 = (bf16[1296,128]{1,0:T(8,128)(2,1)S(1)}, bf16[1296,128]{1,0:T(8,128)(2,1)S(1)}, u32[]{:S(2)}, u32[]{:S(2)}) collective-permute-start(bf16[1296,128]{1,0:T(8,128)(2,1)S(1)} %get-tuple-element.55), channel_id=1, source_target_pairs={{0,1},{1,0},{2,3},{3,2},{4,5},{5,4},{6,7},{7,6},{8,9},{9,8},{10,11... | collective-permute-start | bytes 995336 | tf_op jit(solution)/shard_map/ppermute | solution.py:606
  48.8 1.8 %collective-permute-start.10 = (bf16[1296,128]{1,0:T(8,128)(2,1)S(1)}, bf16[1296,128]{1,0:T(8,128)(2,1)S(1)}, u32[]{:S(2)}, u32[]{:S(2)}) collective-permute-start(bf16[1296,128]{1,0:T(8,128)(2,1)S(1)} %get-tuple-element.66), channel_id=1, source_target_pairs={{0,1},{1,0},{2,3},{3,2},{4,5},{5,4},{6,7},{7,6},{8,9},{9,8},{10,11... | collective-permute-start | bytes 995336 | tf_op jit(solution)/shard_map/ppermute | solution.py:606
  100.4 5.4 %collective-permute-start.11 = (bf16[64,72,128]{2,1,0:T(8,128)(2,1)S(1)}, bf16[64,72,128]{2,1,0:T(8,128)(2,1)S(1)}, u32[]{:S(2)}, u32[]{:S(2)}) collective-permute-start(bf16[64,72,128]{2,1,0:T(8,128)(2,1)S(1)} %all_to_all.11.total), channel_id=1, source_target_pairs={{0,1},{1,0},{2,3},{3,2},{4,5},{5,4},{6,7},{7,6},{8,9},{9,8},{10,11... | collective-permute-start | bytes 3538952 | tf_op jit(solution)/shard_map/ppermute | solution.py:606
